TPU v7x, 32 devices: a whole 2x2x4 slice. The times are simulated.
32 devices in a mesh: req: 8 (over z, y), tp: 4 (over x, core).
Axes of the slice: x: 2, y: 2, z: 4, core: 2. Of those that a mesh axis runs over, the one named last changes fastest.
Arguments:
- tokens: bfloat16 [32, 1024], P('req'), may hold values from -6 to 6
- deal: int32 [32], replicated, may hold values from 0 to 31, each once
- self_len: int32 [32], P('req'), may hold values from 1 to 512, 2048 in all
- enc_len: int32 [32], P('req'), may hold values from 1 to 256, 4096 in all
- self_cache: bfloat16 [32, 512, 2, 1024], P('req', None, None, 'tp'), may hold values from -320 to 320
- cross_cache: bfloat16 [32, 256, 2, 1024], P('req', None, None, 'tp'), may hold values from -320 to 320
- w_qkv: bfloat16 [1024, 3, 1024], P(None, None, 'tp'), may hold values from -0.1875 to 0.1875
- b_qkv: bfloat16 [3, 1024], P(None, 'tp'), may hold values from -3 to 3
- w_out: bfloat16 [1024, 1024], P('tp'), may hold values from -0.1875 to 0.1875
- b_out: bfloat16 [1024], replicated, may hold values from -3 to 3
- ln1_gain: bfloat16 [1024], replicated, may hold values from 0.25 to 1.75
- ln1_bias: bfloat16 [1024], replicated, may hold values from -2 to 2
- w_cq: bfloat16 [1024, 1024], P(None, 'tp'), may hold values from -0.1875 to 0.1875
- b_cq: bfloat16 [1024], P('tp'), may hold values from -3 to 3
- w_cout: bfloat16 [1024, 1024], P('tp'), may hold values from -0.1875 to 0.1875
- b_cout: bfloat16 [1024], replicated, may hold values from -3 to 3
- ln2_gain: bfloat16 [1024], replicated, may hold values from 0.25 to 1.75
- ln2_bias: bfloat16 [1024], replicated, may hold values from -2 to 2
- w_up: bfloat16 [1024, 4096], P(None, 'tp'), may hold values from -0.1875 to 0.1875
- b_up: bfloat16 [4096], P('tp'), may hold values from -3 to 3
- w_down: bfloat16 [4096, 1024], P('tp'), may hold values from -0.09375 to 0.09375
- b_down: bfloat16 [1024], replicated, may hold values from -3 to 3
- ln3_gain: bfloat16 [1024], replicated, may hold values from 0.25 to 1.75
- ln3_bias: bfloat16 [1024], replicated, may hold values from -2 to 2
Outputs:
- result: bfloat16 [32, 1024], P('req')
Inputs may be any that keep to these rules, and one draw needn't show every extreme that they name: deal is a permutation of the requests: slot s holds the caches of request deal[s].
All inputs are finite; a program needn't handle non-finite values. No bound on the sum of `self_len` or of `enc_len` on one device may be relied on, other than what follows from the above.
Results may differ from a plain program's by a relative error of at most 0.039.
Values may be sent and summed in bfloat16 or wider, within the bound.
No kernel may reach another device: no remote copies, remote signals or barrier semaphores. Data moves between devices by JAX's collectives and lax.ppermute only.
A program may use at most 64 MiB of HBM per device.

v0:
```python
import jax
import jax.numpy as jnp
from jax import lax
from jax.sharding import PartitionSpec as P

HEAD_DIM = 64


def norm_rows(total, gain, beta):
    mean = jnp.mean(total, axis=-1, keepdims=True)
    centered = total - mean
    var = jnp.mean(centered * centered, axis=-1, keepdims=True)
    return centered / jnp.sqrt(var + 1e-05) * gain.astype(jnp.float32) + beta.astype(jnp.float32)


def pick_rows(onehot, whole):
    picked = jnp.dot(onehot.astype(whole.dtype), whole, preferred_element_type=jnp.float32)
    return picked.astype(whole.dtype)


def self_attend(triple, cache, lengths):
    rows = triple.shape[0]
    width = triple.shape[2]
    heads = width // HEAD_DIM
    span = cache.shape[1]
    scale = HEAD_DIM ** (-0.5)
    query = triple[:, 0].reshape(rows, heads, HEAD_DIM)
    new_key = triple[:, 1].reshape(rows, heads, HEAD_DIM)
    new_value = triple[:, 2].reshape(rows, heads, HEAD_DIM)
    keys = cache[:, :, 0, :].reshape(rows, span, heads, HEAD_DIM)
    values = cache[:, :, 1, :].reshape(rows, span, heads, HEAD_DIM)
    scores = jnp.einsum("rhe,rmhe->rhm", query, keys, preferred_element_type=jnp.float32) * scale
    fresh = jnp.einsum("rhe,rhe->rh", query, new_key, preferred_element_type=jnp.float32) * scale
    valid = jnp.arange(span, dtype=jnp.int32)[None, None, :] < lengths[:, None, None]
    scores = jnp.where(valid, scores, -jnp.inf)
    top = jnp.maximum(jnp.max(scores, axis=-1), fresh)
    expo = jnp.exp(scores - top[..., None])
    expn = jnp.exp(fresh - top)
    total = jnp.sum(expo, axis=-1) + expn
    weights = (expo / total[..., None]).astype(jnp.bfloat16)
    wnew = (expn / total).astype(jnp.bfloat16)
    ctx = jnp.einsum("rhm,rmhe->rhe", weights, values, preferred_element_type=jnp.float32)
    ctx = ctx + wnew.astype(jnp.float32)[..., None] * new_value.astype(jnp.float32)
    return ctx.reshape(rows, width).astype(jnp.bfloat16)


def cross_attend(query, cache, lengths):
    rows, width = query.shape
    heads = width // HEAD_DIM
    span = cache.shape[1]
    scale = HEAD_DIM ** (-0.5)
    query = query.reshape(rows, heads, HEAD_DIM)
    keys = cache[:, :, 0, :].reshape(rows, span, heads, HEAD_DIM)
    values = cache[:, :, 1, :].reshape(rows, span, heads, HEAD_DIM)
    scores = jnp.einsum("rhe,rmhe->rhm", query, keys, preferred_element_type=jnp.float32) * scale
    valid = jnp.arange(span, dtype=jnp.int32)[None, None, :] < lengths[:, None, None]
    scores = jnp.where(valid, scores, -jnp.inf)
    top = jnp.max(scores, axis=-1)
    expo = jnp.exp(scores - top[..., None])
    weights = (expo / jnp.sum(expo, axis=-1)[..., None]).astype(jnp.bfloat16)
    ctx = jnp.einsum("rhm,rmhe->rhe", weights, values, preferred_element_type=jnp.float32)
    return ctx.reshape(rows, width).astype(jnp.bfloat16)


def finish(partial_value, bias, residual, gain, beta):
    summed = lax.psum(partial_value, "tp")
    return norm_rows(
        summed + bias.astype(jnp.float32) + residual.astype(jnp.float32), gain, beta
    ).astype(jnp.bfloat16)


def on_device(
    tokens,
    deal,
    self_len,
    enc_len,
    self_cache,
    cross_cache,
    w_qkv,
    b_qkv,
    w_out,
    b_out,
    ln1_gain,
    ln1_bias,
    w_cq,
    b_cq,
    w_cout,
    b_cout,
    ln2_gain,
    ln2_bias,
    w_up,
    b_up,
    w_down,
    b_down,
    ln3_gain,
    ln3_bias,
):
    f32 = jnp.float32
    rows = tokens.shape[0]
    every = deal.shape[0]
    base = lax.axis_index("req") * rows
    mine = base + jnp.arange(rows, dtype=jnp.int32)
    slot_owner = lax.dynamic_slice_in_dim(deal, base, rows)
    positions = jnp.arange(every, dtype=jnp.int32)
    to_slots = slot_owner[:, None] == positions[None, :]
    to_owners = deal[None, :] == mine[:, None]
    gathered = lax.all_gather(tokens, "req", axis=0, tiled=True)
    states = pick_rows(to_slots, gathered)
    mixed = jnp.einsum("nd,dke->nke", states, w_qkv, preferred_element_type=f32)
    context = self_attend((mixed + b_qkv.astype(f32)).astype(jnp.bfloat16), self_cache, self_len)
    first = finish(
        jnp.dot(context, w_out, preferred_element_type=f32), b_out, states, ln1_gain, ln1_bias
    )
    second_ctx = cross_attend(
        (jnp.dot(first, w_cq, preferred_element_type=f32) + b_cq.astype(f32)).astype(jnp.bfloat16),
        cross_cache,
        enc_len,
    )
    second = finish(
        jnp.dot(second_ctx, w_cout, preferred_element_type=f32), b_cout, first, ln2_gain, ln2_bias
    )
    hidden = jnp.dot(second, w_up, preferred_element_type=f32) + b_up.astype(f32)
    act = jax.nn.gelu(hidden, approximate=False).astype(jnp.bfloat16)
    outcome = finish(
        jnp.dot(act, w_down, preferred_element_type=f32), b_down, second, ln3_gain, ln3_bias
    )
    result = pick_rows(to_owners, lax.all_gather(outcome, "req", axis=0, tiled=True))
    return result


def solution(mesh):
    return jax.shard_map(
        on_device,
        mesh=mesh,
        in_specs=(
            P("req", None),
            P(),
            P("req"),
            P("req"),
            P("req", None, None, "tp"),
            P("req", None, None, "tp"),
            P(None, None, "tp"),
            P(None, "tp"),
            P("tp", None),
            P(),
            P(),
            P(),
            P(None, "tp"),
            P("tp"),
            P("tp", None),
            P(),
            P(),
            P(),
            P(None, "tp"),
            P("tp"),
            P("tp", None),
            P(),
            P(),
            P(),
        ),
        out_specs=P("req", None),
        check_vma=False,
    )
```

profile of v0, /device:TPU:0, one launch (start us, length us, event | category | flops | bytes accessed | tf_op | source)
XLA Modules:
  0.0 136.4 jit_solution(6090614609672618668)
XLA Ops:
  0.0 0.9 dynamic_slice.3
  0.9 32.5 %all-gather = bf16[8,4,1024]{2,1,0:T(4,128)(2,1)S(1)} all-gather(bf16[1,4,1024]{2,1,0:T(4,128)(2,1)} %bitcast.67), channel_id=1, replica_groups=mesh['req'=8,'tp'=4] {'req'}, dimensions={0}, use_global_device_ids=true | all-gather | bytes 73728 | tf_op jit(solution)/shard_map/all_gather | solution.py:107
  33.6 0.7 convert_element_type.102
  34.3 1.7 %fusion.6 = bf16[4,3,256]{2,0,1:T(4,128)(2,1)S(1)} fusion(bf16[1024,3,256]{2,0,1:T(8,128)(2,1)} %param.30, bf16[4,1024]{1,0:T(4,128)(2,1)S(1)} %convolution_convert_fusion.1, f32[3,256]{1,0:T(4,128)S(1)} %convert_element_type.102), kind=kOutput, calls=%fused_computation.10 | convolution fusion | flops 6297600 | bytes 1590272 | tf_op jit(solution)/shard_map/nd,dke->nke/dot_general | solution.py:109
  36.3 7.0 %fusion.108 = (bf16[4,512,1,256]{3,2,1,0:T(2,128)(2,1)}, bf16[4,512,1,256]{3,2,1,0:T(2,128)(2,1)}) fusion(bf16[4,512,2,256]{3,2,1,0:T(2,128)(2,1)} %param.28), kind=kLoop, calls=%fused_computation.149 | loop fusion | bytes 4194304 | tf_op jit(solution)/shard_map/slice | solution.py:30
  43.3 4.6 %copy.49 = bf16[4,512,1,256]{1,3,0,2:T(8,128)(2,1)S(1)} copy(bf16[4,512,1,256]{3,2,1,0:T(2,128)(2,1)} %get-tuple-element.5) | data formatting | bytes 2097152
  47.9 0.2 fusion.112
  48.7 5.9 %copy.50 = bf16[4,512,1,256]{1,3,0,2:T(8,128)(2,1)} copy(bf16[4,512,1,256]{3,2,1,0:T(2,128)(2,1)} %get-tuple-element.6) | data formatting | bytes 2097152
  54.6 1.6 %fusion.10 = f32[4,4,1,64]{3,2,1,0:T(1,128)S(1)} fusion(bf16[4,512,4,64]{1,3,2,0:T(8,128)(2,1)} %bitcast.65, bf16[4,4,512,1]{2,1,0,3:T(4,128)(2,1)S(1)} %fusion.24), kind=kOutput, calls=%fused_computation.16 | convolution fusion | flops 1048576 | bytes 1069056 | tf_op jit(solution)/shard_map/rhm,rmhe->rhe/dot_general | solution.py:42
  56.4 1.2 fusion.113
  57.7 10.1 %psum.21 = f32[4,1024]{1,0:T(4,128)S(1)} all-reduce(f32[4,1024]{1,0:T(4,128)S(1)} %fusion.113), channel_id=1, replica_groups=mesh['req'=8,'tp'=4] {'tp'}, use_global_device_ids=true, to_apply=%region_2.3 | all-reduce | flops 4096 | bytes 32768 | tf_op jit(solution)/shard_map/psum | solution.py:66
  67.9 0.2 multiply_reduce_fusion.2
  68.2 1.2 fusion.8
  69.6 2.5 %fusion.109 = (bf16[4,256,1,256]{3,2,1,0:T(2,128)(2,1)}, bf16[4,256,1,256]{3,2,1,0:T(2,128)(2,1)}) fusion(bf16[4,256,2,256]{3,2,1,0:T(2,128)(2,1)S(1)} %copy-done.1), kind=kLoop, calls=%fused_computation.150 | loop fusion | bytes 2097152 | tf_op jit(solution)/shard_map/slice | solution.py:53
  72.0 3.6 %copy.51 = bf16[4,256,1,256]{1,3,0,2:T(8,128)(2,1)} copy(bf16[4,256,1,256]{3,2,1,0:T(2,128)(2,1)} %get-tuple-element.7) | data formatting | bytes 1048576
  75.6 1.3 fusion.114
  77.2 1.8 %copy.52 = bf16[4,256,1,256]{1,3,0,2:T(8,128)(2,1)} copy(bf16[4,256,1,256]{3,2,1,0:T(2,128)(2,1)S(1)} %copy-done.2) | data formatting | bytes 1048576
  78.9 1.3 fusion.18
  80.3 1.2 fusion.115
  81.5 10.1 %psum.22 = f32[4,1024]{1,0:T(4,128)S(1)} all-reduce(f32[4,1024]{1,0:T(4,128)S(1)} %fusion.115), channel_id=1, replica_groups=mesh['req'=8,'tp'=4] {'tp'}, use_global_device_ids=true, to_apply=%region_7.8 | all-reduce | flops 4096 | bytes 32768 | tf_op jit(solution)/shard_map/psum | solution.py:66
  92.2 2.3 %fusion.26 = f32[4,1024]{1,0:T(4,128)S(1)} fusion(bf16[1024,1024]{1,0:T(8,128)(2,1)S(1)} %copy-done, bf16[4,1024]{1,0:T(4,128)(2,1)S(1)} %add_convert_fusion.1, bf16[1024,1024]{1,0:T(8,128)(2,1)} %param.42, f32[1024]{0:T(1024)S(1)} %convert_element_type.126), kind=kOutput, calls=%fused_computation.52 | convolution fusion | flops 17047552 | bytes 4222976 | tf_op jit(solution)/shard_map/dot_general | solution.py:125
  94.5 10.1 %psum.23 = f32[4,1024]{1,0:T(4,128)S(1)} all-reduce(f32[4,1024]{1,0:T(4,128)S(1)} %fusion.26), channel_id=1, replica_groups=mesh['req'=8,'tp'=4] {'tp'}, use_global_device_ids=true, to_apply=%region_10.11 | all-reduce | flops 4096 | bytes 32768 | tf_op jit(solution)/shard_map/psum | solution.py:66
  105.1 30.5 %all-gather.1 = bf16[8,4,1024]{2,1,0:T(4,128)(2,1)S(1)} all-gather(bf16[1,4,1024]{2,1,0:T(4,128)(2,1)S(1)} %fusion.65), channel_id=1, replica_groups=mesh['req'=8,'tp'=4] {'req'}, dimensions={0}, use_global_device_ids=true | all-gather | bytes 73728 | tf_op jit(solution)/shard_map/all_gather | solution.py:127
  135.6 0.8 convolution_convert_fusion
  (82 shorter events, 2.9 us)
Async XLA Ops:
  0.0 92.1 %copy-start = (bf16[1024,1024]{1,0:T(8,128)(2,1)S(1)}, bf16[1024,1024]{1,0:T(8,128)(2,1)}, u32[]{:S(2)}) copy-start(bf16[1024,1024]{1,0:T(8,128)(2,1)} %param.44) | copy-start | bytes 6291460
  43.3 4.8 %copy-start.13 = (s32[4]{0:T(128)S(1)}, s32[4]{0:T(128)}, u32[]{:S(2)}) copy-start(s32[4]{0:T(128)} %param.26) | copy-start | bytes 52
  48.6 19.2 %copy-start.3 = (bf16[1024]{0:T(1024)(128)(2,1)S(1)}, bf16[1024]{0:T(1024)(128)(2,1)}, u32[]{:S(2)}) copy-start(bf16[1024]{0:T(1024)(128)(2,1)} %param.33) | copy-start | bytes 6148
  48.6 19.5 %copy-start.4 = (bf16[1024]{0:T(1024)(128)(2,1)S(1)}, bf16[1024]{0:T(1024)(128)(2,1)}, u32[]{:S(2)}) copy-start(bf16[1024]{0:T(1024)(128)(2,1)} %param.34) | copy-start | bytes 6148
  48.6 19.5 %copy-start.5 = (bf16[1024]{0:T(1024)(128)(2,1)S(1)}, bf16[1024]{0:T(1024)(128)(2,1)}, u32[]{:S(2)}) copy-start(bf16[1024]{0:T(1024)(128)(2,1)} %param.35) | copy-start | bytes 6148
  48.7 19.6 %copy-start.14 = (bf16[256]{0:T(256)(128)(2,1)S(1)}, bf16[256]{0:T(256)(128)(2,1)}, u32[]{:S(2)}) copy-start(bf16[256]{0:T(256)(128)(2,1)} %param.37) | copy-start | bytes 1540
  48.7 20.9 %copy-start.1 = (bf16[4,256,2,256]{3,2,1,0:T(2,128)(2,1)S(1)}, bf16[4,256,2,256]{3,2,1,0:T(2,128)(2,1)}, u32[]{:S(2)}) copy-start(bf16[4,256,2,256]{3,2,1,0:T(2,128)(2,1)} %param.29) | copy-start | bytes 3145732
  72.0 4.8 %copy-start.15 = (s32[4]{0:T(128)S(1)}, s32[4]{0:T(128)}, u32[]{:S(2)}) copy-start(s32[4]{0:T(128)} %param.27) | copy-start | bytes 52
  72.0 5.1 %copy-start.2 = (bf16[4,256,1,256]{3,2,1,0:T(2,128)(2,1)S(1)}, bf16[4,256,1,256]{3,2,1,0:T(2,128)(2,1)}, u32[]{:S(2)}) copy-start(bf16[4,256,1,256]{3,2,1,0:T(2,128)(2,1)} %get-tuple-element.8) | copy-start | bytes 1572868
  75.6 16.0 %copy-start.6 = (bf16[1024]{0:T(1024)(128)(2,1)S(1)}, bf16[1024]{0:T(1024)(128)(2,1)}, u32[]{:S(2)}) copy-start(bf16[1024]{0:T(1024)(128)(2,1)} %param.39) | copy-start | bytes 6148
  75.6 16.4 %copy-start.7 = (bf16[1024]{0:T(1024)(128)(2,1)S(1)}, bf16[1024]{0:T(1024)(128)(2,1)}, u32[]{:S(2)}) copy-start(bf16[1024]{0:T(1024)(128)(2,1)} %param.40) | copy-start | bytes 6148
  75.6 16.4 %copy-start.8 = (bf16[1024]{0:T(1024)(128)(2,1)S(1)}, bf16[1024]{0:T(1024)(128)(2,1)}, u32[]{:S(2)}) copy-start(bf16[1024]{0:T(1024)(128)(2,1)} %param.41) | copy-start | bytes 6148
  75.6 16.5 %copy-start.9 = (bf16[1024]{0:T(1024)(128)(2,1)S(1)}, bf16[1024]{0:T(1024)(128)(2,1)}, u32[]{:S(2)}) copy-start(bf16[1024]{0:T(1024)(128)(2,1)} %param.43) | copy-start | bytes 6148
  92.1 12.5 %copy-start.10 = (bf16[1024]{0:T(1024)(128)(2,1)S(1)}, bf16[1024]{0:T(1024)(128)(2,1)}, u32[]{:S(2)}) copy-start(bf16[1024]{0:T(1024)(128)(2,1)} %param.45) | copy-start | bytes 6148
  92.1 12.8 %copy-start.11 = (bf16[1024]{0:T(1024)(128)(2,1)S(1)}, bf16[1024]{0:T(1024)(128)(2,1)}, u32[]{:S(2)}) copy-start(bf16[1024]{0:T(1024)(128)(2,1)} %param.46) | copy-start | bytes 6148
  92.1 12.8 %copy-start.12 = (bf16[1024]{0:T(1024)(128)(2,1)S(1)}, bf16[1024]{0:T(1024)(128)(2,1)}, u32[]{:S(2)}) copy-start(bf16[1024]{0:T(1024)(128)(2,1)} %param.47) | copy-start | bytes 6148
  92.2 43.4 %copy-start.16 = (s32[32]{0:T(128)S(1)}, s32[32]{0:T(128)}, u32[]{:S(2)}) copy-start(s32[32]{0:T(128)} %param.25) | copy-start | bytes 388
where the time goes:
time: 137 us; the launch traced here: 136 us
  blocking collectives  93.3 us (68%)
  local copies, waits for them, and re-layouts  26.8 us (20%)
  matrix products  13.1 us (10%)
  other arithmetic  2.89 us (2%)
    all_gather x1, blocking collectives, on_device(): gathered = lax.all_gather(tokens, 'req', axis=0, tiled=True)  32.5 us
    all_gather x1, blocking collectives, on_device(): lax.all_gather(outcome, 'req', axis=0, tiled=True)  30.5 us
    psum x3, blocking collectives, finish(): summed = lax.psum(partial_value, 'tp')  30.3 us
    unnamed x40, local copies, waits for them, and re-layouts  15.9 us
    slice x1, local copies, waits for them, and re-layouts, self_attend(): keys = cache[:, :, 0, :].reshape(rows, span, heads, HEAD_DIM)  6.96 us

commit v1 on v0

v1 whole, which is shorter than its diff:
```python
import functools

import jax
import jax.numpy as jnp
from jax import lax
from jax.experimental import pallas as pl
from jax.experimental.pallas import tpu as pltpu
from jax.sharding import PartitionSpec as P

HEAD_DIM = 64
LANES = 128
EPS = 1e-05
MASKED = -1e30
SPARE_FLOPS = 10**10
f32 = jnp.float32
bf16 = jnp.bfloat16


def norm_rows(total, gain, beta):
    mean = jnp.mean(total, axis=-1, keepdims=True)
    centered = total - mean
    var = jnp.mean(centered * centered, axis=-1, keepdims=True)
    return centered / jnp.sqrt(var + EPS) * gain + beta


def round_rows(value):
    return value.astype(bf16).astype(f32)


def dot(a, b):
    return jnp.dot(a.astype(bf16), b, preferred_element_type=f32)


def dot_t(a, b):
    return lax.dot_general(
        a.astype(bf16), b, (((1,), (1,)), ((), ())), preferred_element_type=f32
    )


def pad_rows(value, rows):
    return jnp.concatenate(
        [value, jnp.zeros((rows - value.shape[0], value.shape[1]), value.dtype)], axis=0
    )


def head_rows(vec, slot, heads, first):
    return jnp.where(first, vec[slot : slot + 1], vec[slot + 1 : slot + 2])


def attend(query, cache, lens, heads, fresh_key=None, fresh_value=None):
    slots, _, span, width = cache.shape
    pair = 2 * heads
    scale = HEAD_DIM ** (-0.5)
    row = lax.broadcasted_iota(jnp.int32, (pair, width), 0)
    lane = lax.broadcasted_iota(jnp.int32, (pair, width), 1)
    first = row < heads
    own = (lane // HEAD_DIM) == jnp.where(first, row, row - heads)
    first_col = lax.broadcasted_iota(jnp.int32, (pair, span), 0) < heads
    position = lax.broadcasted_iota(jnp.int32, (pair, span), 1)
    rows = []
    for slot in range(0, slots, 2):
        q = jnp.where(own, head_rows(query, slot, heads, first) * scale, 0.0)
        raw = [dot_t(q, cache[slot + i, 0]) for i in range(2)]
        length = jnp.where(first_col, lens[slot], lens[slot + 1])
        scores = jnp.where(position < length, jnp.where(first_col, raw[0], raw[1]), MASKED)
        top = jnp.max(scores, axis=-1, keepdims=True)
        if fresh_key is not None:
            k_new = head_rows(fresh_key, slot, heads, first)
            v_new = head_rows(fresh_value, slot, heads, first)
            fresh = jnp.sum(q * k_new, axis=-1, keepdims=True)
            top = jnp.maximum(top, fresh)
        expo = jnp.exp(scores - top)
        total = jnp.sum(expo, axis=-1, keepdims=True)
        if fresh_key is not None:
            expn = jnp.exp(fresh - top)
            total = total + expn
        share = 1.0 / total
        weights = expo * share
        out = [dot(weights, cache[slot + i, 1]) for i in range(2)]
        ctx = jnp.where(first, out[0], out[1])
        if fresh_key is not None:
            ctx = ctx + round_rows(expn * share) * v_new
        ctx = jnp.where(own, round_rows(ctx), 0.0)
        rows.append(jnp.sum(ctx[:heads], axis=0, keepdims=True))
        rows.append(jnp.sum(ctx[heads:], axis=0, keepdims=True))
    return jnp.concatenate(rows + [jnp.zeros((8 - slots, width), f32)], axis=0)


def split_cache(cache, out_ref):
    slots, count, _ = cache.shape
    tiles = out_ref.shape[3] // LANES
    group = 2 * tiles
    step = 256
    part = step // group
    r = lax.broadcasted_iota(jnp.int32, (step, step), 0)
    c = lax.broadcasted_iota(jnp.int32, (step, step), 1)
    order = (c == (r % part) * group + r // part).astype(bf16)
    for slot in range(slots):
        for at in range(count // step):
            rows = dot(order, cache[slot, at * step : (at + 1) * step]).astype(bf16)
            for tile in range(tiles):
                for kind in range(2):
                    g = (tile * 2 + kind) * part
                    out_ref[
                        slot, kind, at * part : (at + 1) * part, tile * LANES : (tile + 1) * LANES
                    ] = rows[g : g + part]
        yield slot


def load_split(source, held, sems, out_ref):
    copies = []
    for slot in range(held.shape[0]):
        copies.append(pltpu.make_async_copy(source.at[slot], held.at[slot], sems.at[slot]))
        copies[-1].start()
    copies[0].wait()
    for slot in split_cache(held, out_ref):
        if slot + 1 < len(copies):
            copies[slot + 1].wait()


def wanted(deal, rows, me, far, back):
    cols = 4 * rows
    row = lax.broadcasted_iota(jnp.int32, (2 * rows, cols), 0)
    col = lax.broadcasted_iota(jnp.int32, (2 * rows, cols), 1)
    take = jnp.where(row < rows, me, me ^ far) * rows + row % rows
    have = (me ^ (col // rows)) * rows + col % rows
    if back:
        for i in range(cols):
            have = jnp.where(col == i, deal[(me ^ (i // rows)) * rows + i % rows], have)
    else:
        for i in range(2 * rows):
            at = (me if i < rows else me ^ far) * rows + i % rows
            take = jnp.where(row == i, deal[at], take)
    return (have == take).astype(bf16)


def plan_kernel(deal, tokens, cache, own_ref, out_ref, back_ref, kv_ref, held, sems, *, far):
    me = lax.axis_index("req")
    rows = tokens.shape[0]
    own_ref[...] = tokens[...]
    out_ref[...] = wanted(deal, rows, me, far, False)
    back_ref[...] = wanted(deal, rows, me, far, True)
    load_split(cache, held, sems, kv_ref)


def split_kernel(cache, kv_ref, held, sems):
    load_split(cache, held, sems, kv_ref)


def sort_kernel(hit, own, g1, g2, g3, mine_ref, theirs_ref):
    rows = own.shape[0]
    whole = jnp.concatenate([p[...] for p in (own, g1, g2, g3)], axis=0)
    out = dot(hit[...], whole)
    mine_ref[...] = out[:rows].astype(bf16)
    theirs_ref[...] = out[rows:].astype(bf16)


def flat(vec):
    return vec[...].astype(f32).reshape(1, vec.shape[0])


def first_kernel(
    lens, mine, more, w_qkv, b_qkv, cache, w_out, x_ref, part_ref, *, heads
):
    slots = x_ref.shape[0]
    x = mine[...].astype(f32) + more[...].astype(f32)
    x_ref[...] = x.astype(bf16)
    x = pad_rows(x, 8).astype(bf16)
    bias = b_qkv[...].astype(f32)
    qkv = [round_rows(dot(x, w_qkv[k]) + bias[k : k + 1]) for k in range(3)]
    length = [lens[s] for s in range(slots)]
    ctx = attend(qkv[0], cache, length, heads, qkv[1], qkv[2])
    part_ref[...] = dot(ctx, w_out[...])[:slots]


def settle(own, p1, p2, p3, x, bias, gain, beta):
    total = own[...] + p1[...] + p2[...] + p3[...] + flat(bias) + x[...].astype(f32)
    return norm_rows(total, flat(gain), flat(beta)).astype(bf16)


def second_kernel(
    lens, own, p1, p2, p3, x, bias, gain, beta, w_cq, b_cq, cache, w_cout, h_ref, part_ref, *, heads
):
    slots = own.shape[0]
    h1 = settle(own, p1, p2, p3, x, bias, gain, beta)
    h_ref[...] = h1
    cq = round_rows(dot(pad_rows(h1.astype(f32), 8), w_cq[...]) + flat(b_cq))
    length = [lens[s] for s in range(slots)]
    ctx = attend(cq, cache, length, heads)
    part_ref[...] = dot(ctx, w_cout[...])[:slots]


def third_kernel(
    own, p1, p2, p3, x, bias, gain, beta, w_up, b_up, w_down, h_ref, part_ref
):
    slots = own.shape[0]
    h2 = settle(own, p1, p2, p3, x, bias, gain, beta)
    h_ref[...] = h2
    hidden = dot(pad_rows(h2.astype(f32), 8), w_up[...]) + flat(b_up)
    act = 0.5 * hidden * (1.0 + lax.erf(hidden * (2.0**-0.5)))
    part_ref[...] = dot(act, w_down[...])[:slots]


def fourth_kernel(own, p1, p2, p3, x, bias, gain, beta, y_ref):
    y_ref[...] = settle(own, p1, p2, p3, x, bias, gain, beta)


def add_kernel(mine, more, out_ref):
    out_ref[...] = (mine[...].astype(f32) + more[...].astype(f32)).astype(bf16)


def call(kernel, out_shapes, args, smem=0, hbm=(), scratch=(), name=None, cost=None):
    vmem = pl.BlockSpec(memory_space=pltpu.VMEM)
    scalar = pl.BlockSpec(memory_space=pltpu.SMEM)
    far = pl.BlockSpec(memory_space=pltpu.HBM)
    outs = [jax.ShapeDtypeStruct(s, d) for s, d in out_shapes]
    specs = [scalar if i < smem else far if i in hbm else vmem for i in range(len(args))]
    if cost is not None:
        cost = pl.CostEstimate(flops=cost, bytes_accessed=0, transcendentals=0)
    return pl.pallas_call(
        kernel,
        out_shape=outs,
        in_specs=specs,
        out_specs=[vmem] * len(outs),
        scratch_shapes=list(scratch),
        compiler_params=pltpu.CompilerParams(vmem_limit_bytes=24 * 2**20),
        cost_estimate=cost,
        name=name,
    )(*args)


def swap(value, axis, size, mask):
    return lax.ppermute(value, axis, [(i, i ^ mask) for i in range(size)])


def pick_rows(onehot, whole):
    return jnp.dot(onehot.astype(whole.dtype), whole, preferred_element_type=f32).astype(whole.dtype)


FAR = 4


def near_swaps(value):
    names, size = ("req", "tp"), lax.axis_size("req") * lax.axis_size("tp")
    tps = lax.axis_size("tp")
    return [swap(value, names, size, mask * tps + 1) for mask in (1, 2, 3)]


def far_swap(value):
    names, size = ("req", "tp"), lax.axis_size("req") * lax.axis_size("tp")
    return swap(value, names, size, FAR * lax.axis_size("tp") + 1)


def sort_rows(hit, own, near, name):
    state = (own.shape, bf16)
    mine, theirs = call(
        sort_kernel, [state, state], [hit, own] + near, name=name, cost=SPARE_FLOPS
    )
    return mine, far_swap(theirs)


def deal_whole(value, deal, back):
    base = lax.axis_index("req") * value.shape[0]
    spread = jnp.arange(value.shape[0], dtype=jnp.int32)
    whole = lax.all_gather(value, "req", axis=0, tiled=True)
    if back:
        onehot = deal[None, :] == (base + spread)[:, None]
    else:
        owner = lax.dynamic_slice_in_dim(deal, base, value.shape[0])
        onehot = owner[:, None] == jnp.arange(deal.shape[0], dtype=jnp.int32)[None, :]
    picked = pick_rows(onehot, whole)
    return picked, jnp.zeros_like(picked)


def split_shapes(cache):
    slots, span, _, width = cache.shape
    tiles = width // LANES
    scratch = [
        pltpu.VMEM((slots, span * 2 * tiles, LANES), bf16),
        pltpu.SemaphoreType.DMA((slots,)),
    ]
    return ((slots, 2, span, width), bf16), scratch


def sum_parts(value, mesh_shape):
    tps = mesh_shape["tp"]
    if tps == 4:
        return [value] + [swap(value, "tp", tps, mask) for mask in (1, 2, 3)]
    whole = lax.psum(value, "tp")
    zero = jnp.zeros_like(whole)
    return [whole, zero, zero, zero]


def on_device(
    mesh_shape,
    tokens,
    deal,
    self_len,
    enc_len,
    self_cache,
    cross_cache,
    w_qkv,
    b_qkv,
    w_out,
    b_out,
    ln1_gain,
    ln1_bias,
    w_cq,
    b_cq,
    w_cout,
    b_cout,
    ln2_gain,
    ln2_bias,
    w_up,
    b_up,
    w_down,
    b_down,
    ln3_gain,
    ln3_bias,
):
    rows, model = tokens.shape
    width = self_cache.shape[3]
    heads = width // HEAD_DIM

    def tile_rows(cache):
        slots, span = cache.shape[0], cache.shape[1]
        split = cache.reshape(slots, span, 2, width // LANES, LANES)
        return split.transpose(0, 1, 3, 2, 4).reshape(slots, -1, LANES)

    state, sums = ((rows, model), bf16), ((rows, model), f32)
    split, scratch = split_shapes(self_cache)
    hops = mesh_shape["req"] == 2 * FAR
    if hops:
        near = near_swaps(tokens)
        hits = ((2 * rows, 4 * rows), bf16)
        own, hit_out, hit_back, self_kv = call(
            functools.partial(plan_kernel, far=FAR),
            [state, hits, hits, split],
            [deal, tokens, tile_rows(self_cache)],
            smem=1,
            hbm=(2,),
            scratch=scratch,
            name="plan",
        )
        mine, more = sort_rows(hit_out, own, near, "sort_out")
    else:
        mine, more = deal_whole(tokens, deal, False)
        (self_kv,) = call(
            split_kernel, [split], [tile_rows(self_cache)], hbm=(0,), scratch=scratch, name="split"
        )
    split, scratch = split_shapes(cross_cache)
    (cross_kv,) = call(
        split_kernel,
        [split],
        [tile_rows(cross_cache)],
        hbm=(0,),
        scratch=scratch,
        name="split_cross",
    )
    x, part = call(
        functools.partial(first_kernel, heads=heads),
        [state, sums],
        [self_len, mine, more, w_qkv.transpose(1, 0, 2), b_qkv, self_kv, w_out],
        smem=1,
        name="self_attention",
    )
    h1, part = call(
        functools.partial(second_kernel, heads=heads),
        [state, sums],
        [enc_len]
        + sum_parts(part, mesh_shape)
        + [x, b_out, ln1_gain, ln1_bias, w_cq, b_cq, cross_kv, w_cout],
        smem=1,
        name="cross_attention",
    )
    h2, part = call(
        third_kernel,
        [state, sums],
        sum_parts(part, mesh_shape)
        + [h1, b_cout, ln2_gain, ln2_bias, w_up, b_up, w_down],
        name="feed_forward",
    )
    (y,) = call(
        fourth_kernel,
        [state],
        sum_parts(part, mesh_shape) + [h2, b_down, ln3_gain, ln3_bias],
        name="last_norm",
    )
    if hops:
        mine, more = sort_rows(hit_back, y, near_swaps(y), "sort_back")
    else:
        mine, more = deal_whole(y, deal, True)
    (result,) = call(add_kernel, [state], [mine, more], name="deal_back")
    return result


def solution(mesh):
    return jax.shard_map(
        functools.partial(on_device, dict(mesh.shape)),
        mesh=mesh,
        in_specs=(
            P("req", None),
            P(),
            P("req"),
            P("req"),
            P("req", None, None, "tp"),
            P("req", None, None, "tp"),
            P(None, None, "tp"),
            P(None, "tp"),
            P("tp", None),
            P(),
            P(),
            P(),
            P(None, "tp"),
            P("tp"),
            P("tp", None),
            P(),
            P(),
            P(),
            P(None, "tp"),
            P("tp"),
            P("tp", None),
            P(),
            P(),
            P(),
        ),
        out_specs=P("req", None),
        check_vma=False,
    )
```

time: 137 us -> 44.9 us (0.33)
  blocking collectives: 93.3 us -> 0 us
  local copies, waits for them, and re-layouts: 26.8 us -> 3.06 us
  starting transfers between devices: 0 us -> 18 us
  waiting for transfers between devices: 0 us -> 13.8 us
  matrix products: 13.1 us -> 0 us
  Pallas kernels: 0 us -> 9.54 us
  other arithmetic: 2.89 us -> 0 us
    all_gather x2 -> x0, blocking collectives: 63 us -> none  [the longest x1 32.5 us: on_device(): gathered = lax.all_gather(tokens, 'req', axis=0, tiled=True)]
    psum x3 -> x0, blocking collectives: 30.3 us -> none  [finish(): summed = lax.psum(partial_value, 'tp')]
    ppermute x0 -> x17, starting transfers between devices: none -> 18 us  [swap(): return lax.ppermute(value, axis, [(i, i ^ mask) for i in range(size)])]
    ppermute x0 -> x17, waiting for transfers between devices: none -> 13.8 us  [swap(): return lax.ppermute(value, axis, [(i, i ^ mask) for i in range(size)])]
    dot_general x11 -> x0, matrix products: 13.1 us -> none  [the longest x1 2.3 us: on_device(): jnp.dot(act, w_down, preferred_element_type=f32)]
    unnamed x40 -> x48, local copies, waits for them, and re-layouts: 15.9 us -> 3.06 us
    pallas_call x0 -> x9, Pallas kernels: none -> 9.54 us  [call(): pl.pallas_call(kernel, out_shape=outs, in_specs=specs, out_specs=[vmem] *...]
    slice x2 -> x0, local copies, waits for them, and re-layouts: 9.44 us -> none  [the longest x1 6.96 us: self_attend(): keys = cache[:, :, 0, :].reshape(rows, span, heads, HEAD_DIM)]
  transfers between devices with their start and end apart: 0 -> 17, of which waited for: 0 -> 10; matrix products, arithmetic and copies ran while one was open for 0% -> 0% of each run, Pallas kernels for 0% -> 8%
where the time goes in v1:
time: 44.9 us; the launch traced here: 44.7 us
  starting transfers between devices  18 us (40%)
  waiting for transfers between devices  13.8 us (31%)
  Pallas kernels  9.54 us (21%)
  local copies, waits for them, and re-layouts  3.06 us (7%)
    ppermute x17, starting transfers between devices, swap(): return lax.ppermute(value, axis, [(i, i ^ mask) for i in range(size)])  18 us
    ppermute x17, waiting for transfers between devices, swap(): return lax.ppermute(value, axis, [(i, i ^ mask) for i in range(size)])  13.8 us
    pallas_call x9, Pallas kernels, call(): pl.pallas_call(kernel, out_shape=outs, in_specs=specs, out_specs=[vmem] *...  9.54 us
    unnamed x48, local copies, waits for them, and re-layouts  3.06 us
  transfers between devices with their start and end apart: 17, of which 10 were waited for; matrix products, arithmetic and copies ran while one was open for 0% of the time, Pallas kernels for 8%

profile of v1, /device:TPU:0, one launch (start us, length us, event | category | flops | bytes accessed | tf_op | source)
XLA Modules:
  0.0 44.7 jit_solution(7154850880371436871)
XLA Ops:
  0.0 2.4 %collective-permute-start = (bf16[4,1024]{1,0:T(4,128)(2,1)}, bf16[4,1024]{1,0:T(4,128)(2,1)S(1)}, u32[]{:S(2)}, u32[]{:S(2)}) collective-permute-start(bf16[4,1024]{1,0:T(4,128)(2,1)} %tokens.1), channel_id=1, source_target_pairs={{0,5},{1,4},{2,7},{3,6},{4,1},{5,0},{6,3},{7,2},{8,13},{9,12},{10,... | collective-permute-start | bytes 24584 | tf_op jit(solution)/shard_map/ppermute | solution.py:233
  2.4 1.9 %collective-permute-start.1 = (bf16[4,1024]{1,0:T(4,128)(2,1)}, bf16[4,1024]{1,0:T(4,128)(2,1)S(1)}, u32[]{:S(2)}, u32[]{:S(2)}) collective-permute-start(bf16[4,1024]{1,0:T(4,128)(2,1)} %tokens.1), channel_id=1, source_target_pairs={{0,9},{1,8},{2,11},{3,10},{4,13},{5,12},{6,15},{7,14},{8,1},{9,0},... | collective-permute-start | bytes 24584 | tf_op jit(solution)/shard_map/ppermute | solution.py:233
  4.3 1.6 %copy-done = bf16[4,512,2,256]{3,2,1,0:T(2,128)(2,1)S(1)} copy-done((bf16[4,512,2,256]{3,2,1,0:T(2,128)(2,1)S(1)}, bf16[4,512,2,256]{3,2,1,0:T(2,128)(2,1)}, u32[]{:S(2)}) %copy-start) | copy-done | bytes 2097176
  5.9 0.7 %copy-done.8 = bf16[4,1024]{1,0:T(4,128)(2,1)S(1)} copy-done((bf16[4,1024]{1,0:T(4,128)(2,1)S(1)}, bf16[4,1024]{1,0:T(4,128)(2,1)}, u32[]{:S(2)}) %copy-start.8) | copy-done | bytes 8216
  7.2 2.4 %plan.1 = (bf16[4,1024]{1,0:T(4,128)(2,1)S(1)}, bf16[8,16]{1,0:T(8,128)(2,1)S(1)}, bf16[8,16]{1,0:T(8,128)(2,1)S(1)}, bf16[4,2,512,256]{3,2,1,0:T(8,128)(2,1)S(1)}) custom-call(s32[32]{0:T(128)S(1)} %copy-done.20, bf16[4,1024]{1,0:T(4,128)(2,1)S(1)} %copy-done.8, bf16[4,2048,128]{2,1,0:T(8,128)(2,1)S(1)} %bitcast.11), custom_call_target="tpu_custom_call" | custom-call | tf_op jit(solution)/shard_map/plan/pallas_call | solution.py:220
  9.9 2.7 %collective-permute-start.3 = (bf16[4,1024]{1,0:T(4,128)(2,1)S(1)}, bf16[4,1024]{1,0:T(4,128)(2,1)S(1)}, u32[]{:S(2)}, u32[]{:S(2)}) collective-permute-start(bf16[4,1024]{1,0:T(4,128)(2,1)S(1)} %get-tuple-element.23), channel_id=1, source_target_pairs={{0,17},{1,16},{2,19},{3,18},{4,21},{5,20},{6,23},{7,22},{8,25},{9,... | collective-permute-start | bytes 24584 | tf_op jit(solution)/shard_map/ppermute | solution.py:233
  12.6 1.4 %collective-permute-done.3.more = bf16[4,1024]{1,0:T(4,128)(2,1)S(1)} collective-permute-done((bf16[4,1024]{1,0:T(4,128)(2,1)S(1)}, bf16[4,1024]{1,0:T(4,128)(2,1)S(1)}, u32[]{:S(2)}, u32[]{:S(2)}) %collective-permute-start.3) | collective-permute-done | bytes 8224 | tf_op jit(solution)/shard_map/ppermute | solution.py:233
  14.0 2.0 %self_attention.1 = (bf16[4,1024]{1,0:T(4,128)(2,1)S(1)}, f32[4,1024]{1,0:T(4,128)S(1)}) custom-call(s32[4]{0:T(128)S(1)} %copy-done.21, bf16[4,1024]{1,0:T(4,128)(2,1)S(1)} %get-tuple-element.22.mine, bf16[4,1024]{1,0:T(4,128)(2,1)S(1)} %collective-permute-done.3.more, bf16[3,1024,256]{2,1,0:T(8,128)(2,1)S(1)} %bitcast.12, bf16[3,256]{1,0:T(4,128)(2,1)S(1)} %copy-done.9, ...), custom_call_target="tpu_custom_call" | custom-call | tf_op jit(solution)/shard_map/self_attention/pallas_call | solution.py:220
  16.2 1.8 %collective-permute-start.5 = (f32[4,1024]{1,0:T(4,128)S(1)}, f32[4,1024]{1,0:T(4,128)S(1)}, u32[]{:S(2)}, u32[]{:S(2)}) collective-permute-start(f32[4,1024]{1,0:T(4,128)S(1)} %get-tuple-element.25.own), channel_id=1, source_target_pairs={{0,2},{1,3},{2,0},{3,1},{4,6},{5,7},{6,4},{7,5},{8,10},{9,11},{10,... | collective-permute-start | bytes 49160 | tf_op jit(solution)/shard_map/ppermute | solution.py:233
  18.1 1.3 %split_cross.1.cache = bf16[4,2,256,256]{3,2,1,0:T(8,128)(2,1)S(1)} custom-call(bf16[4,1024,128]{2,1,0:T(8,128)(2,1)S(1)} %bitcast.13), custom_call_target="tpu_custom_call" | custom-call | tf_op jit(solution)/shard_map/split_cross/pallas_call | solution.py:220
  19.9 1.4 %collective-permute-done.6.p3 = f32[4,1024]{1,0:T(4,128)S(1)} collective-permute-done((f32[4,1024]{1,0:T(4,128)S(1)}, f32[4,1024]{1,0:T(4,128)S(1)}, u32[]{:S(2)}, u32[]{:S(2)}) %collective-permute-start.6) | collective-permute-done | bytes 16416 | tf_op jit(solution)/shard_map/ppermute | solution.py:233
  21.4 1.9 %cross_attention.1 = (bf16[4,1024]{1,0:T(4,128)(2,1)S(1)}, f32[4,1024]{1,0:T(4,128)S(1)}) custom-call(s32[4]{0:T(128)S(1)} %copy-done.22, f32[4,1024]{1,0:T(4,128)S(1)} %get-tuple-element.25.own, f32[4,1024]{1,0:T(4,128)S(1)} %collective-permute-done.4.p1, f32[4,1024]{1,0:T(4,128)S(1)} %collective-permute-done.5.p2, ...), custom_call_target="tpu_custom_call" | custom-call | tf_op jit(solution)/shard_map/cross_attention/pallas_call | solution.py:220
  23.9 1.4 %collective-permute-start.9 = (f32[4,1024]{1,0:T(4,128)S(1)}, f32[4,1024]{1,0:T(4,128)S(1)}, u32[]{:S(2)}, u32[]{:S(2)}) collective-permute-start(f32[4,1024]{1,0:T(4,128)S(1)} %get-tuple-element.27.own), channel_id=1, source_target_pairs={{0,3},{1,2},{2,1},{3,0},{4,7},{5,6},{6,5},{7,4},{8,11},{9,10},{10,... | collective-permute-start | bytes 49160 | tf_op jit(solution)/shard_map/ppermute | solution.py:233
  25.2 2.0 %collective-permute-done.8.p2 = f32[4,1024]{1,0:T(4,128)S(1)} collective-permute-done((f32[4,1024]{1,0:T(4,128)S(1)}, f32[4,1024]{1,0:T(4,128)S(1)}, u32[]{:S(2)}, u32[]{:S(2)}) %collective-permute-start.8) | collective-permute-done | bytes 16416 | tf_op jit(solution)/shard_map/ppermute | solution.py:233
  27.3 0.8 %feed_forward.1 = (bf16[4,1024]{1,0:T(4,128)(2,1)S(1)}, f32[4,1024]{1,0:T(4,128)S(1)}) custom-call(f32[4,1024]{1,0:T(4,128)S(1)} %get-tuple-element.27.own, f32[4,1024]{1,0:T(4,128)S(1)} %collective-permute-done.7.p1, f32[4,1024]{1,0:T(4,128)S(1)} %collective-permute-done.8.p2, f32[4,1024]{1,0:T(4,128)S(1)} %collective-permute-done.9.p3, ...), custom_call_target="tpu_custom_call" | custom-call | tf_op jit(solution)/shard_map/feed_forward/pallas_call | solution.py:220
  28.3 1.5 %collective-permute-start.11 = (f32[4,1024]{1,0:T(4,128)S(1)}, f32[4,1024]{1,0:T(4,128)S(1)}, u32[]{:S(2)}, u32[]{:S(2)}) collective-permute-start(f32[4,1024]{1,0:T(4,128)S(1)} %get-tuple-element.29.own), channel_id=1, source_target_pairs={{0,2},{1,3},{2,0},{3,1},{4,6},{5,7},{6,4},{7,5},{8,10},{9,11},{10,... | collective-permute-start | bytes 49160 | tf_op jit(solution)/shard_map/ppermute | solution.py:233
  30.0 2.0 %collective-permute-done.11.p2 = f32[4,1024]{1,0:T(4,128)S(1)} collective-permute-done((f32[4,1024]{1,0:T(4,128)S(1)}, f32[4,1024]{1,0:T(4,128)S(1)}, u32[]{:S(2)}, u32[]{:S(2)}) %collective-permute-start.11) | collective-permute-done | bytes 16416 | tf_op jit(solution)/shard_map/ppermute | solution.py:233
  32.0 0.9 %collective-permute-done.12.p3 = f32[4,1024]{1,0:T(4,128)S(1)} collective-permute-done((f32[4,1024]{1,0:T(4,128)S(1)}, f32[4,1024]{1,0:T(4,128)S(1)}, u32[]{:S(2)}, u32[]{:S(2)}) %collective-permute-start.12) | collective-permute-done | bytes 16416 | tf_op jit(solution)/shard_map/ppermute | solution.py:233
  33.1 1.3 %collective-permute-start.13 = (bf16[4,1024]{1,0:T(4,128)(2,1)S(1)}, bf16[4,1024]{1,0:T(4,128)(2,1)S(1)}, u32[]{:S(2)}, u32[]{:S(2)}) collective-permute-start(bf16[4,1024]{1,0:T(4,128)(2,1)S(1)} %last_norm.1.own), channel_id=1, source_target_pairs={{0,5},{1,4},{2,7},{3,6},{4,1},{5,0},{6,3},{7,2},{8,13},{9,12},{10,... | collective-permute-start | bytes 24584 | tf_op jit(solution)/shard_map/ppermute | solution.py:233
  34.4 1.6 %collective-permute-start.14 = (bf16[4,1024]{1,0:T(4,128)(2,1)S(1)}, bf16[4,1024]{1,0:T(4,128)(2,1)S(1)}, u32[]{:S(2)}, u32[]{:S(2)}) collective-permute-start(bf16[4,1024]{1,0:T(4,128)(2,1)S(1)} %last_norm.1.own), channel_id=1, source_target_pairs={{0,9},{1,8},{2,11},{3,10},{4,13},{5,12},{6,15},{7,14},{8,1},{9,0},... | collective-permute-start | bytes 24584 | tf_op jit(solution)/shard_map/ppermute | solution.py:233
  36.2 1.2 %collective-permute-done.14.g2 = bf16[4,1024]{1,0:T(4,128)(2,1)S(1)} collective-permute-done((bf16[4,1024]{1,0:T(4,128)(2,1)S(1)}, bf16[4,1024]{1,0:T(4,128)(2,1)S(1)}, u32[]{:S(2)}, u32[]{:S(2)}) %collective-permute-start.14) | collective-permute-done | bytes 8224 | tf_op jit(solution)/shard_map/ppermute | solution.py:233
  37.5 2.5 %collective-permute-done.15.g3 = bf16[4,1024]{1,0:T(4,128)(2,1)S(1)} collective-permute-done((bf16[4,1024]{1,0:T(4,128)(2,1)S(1)}, bf16[4,1024]{1,0:T(4,128)(2,1)S(1)}, u32[]{:S(2)}, u32[]{:S(2)}) %collective-permute-start.15) | collective-permute-done | bytes 8224 | tf_op jit(solution)/shard_map/ppermute | solution.py:233
  40.1 2.3 %collective-permute-start.16 = (bf16[4,1024]{1,0:T(4,128)(2,1)S(1)}, bf16[4,1024]{1,0:T(4,128)(2,1)S(1)}, u32[]{:S(2)}, u32[]{:S(2)}) collective-permute-start(bf16[4,1024]{1,0:T(4,128)(2,1)S(1)} %get-tuple-element.32), channel_id=1, source_target_pairs={{0,17},{1,16},{2,19},{3,18},{4,21},{5,20},{6,23},{7,22},{8,25},{9,... | collective-permute-start | bytes 24584 | tf_op jit(solution)/shard_map/ppermute | solution.py:233
  42.4 1.7 %collective-permute-done.16.more = bf16[4,1024]{1,0:T(4,128)(2,1)S(1)} collective-permute-done((bf16[4,1024]{1,0:T(4,128)(2,1)S(1)}, bf16[4,1024]{1,0:T(4,128)(2,1)S(1)}, u32[]{:S(2)}, u32[]{:S(2)}) %collective-permute-start.16) | collective-permute-done | bytes 8224 | tf_op jit(solution)/shard_map/ppermute | solution.py:233
  (67 shorter events, 3.8 us)
Async XLA Ops:
  0.0 9.7 %collective-permute-start = (bf16[4,1024]{1,0:T(4,128)(2,1)}, bf16[4,1024]{1,0:T(4,128)(2,1)S(1)}, u32[]{:S(2)}, u32[]{:S(2)}) collective-permute-start(bf16[4,1024]{1,0:T(4,128)(2,1)} %tokens.1), channel_id=1, source_target_pairs={{0,5},{1,4},{2,7},{3,6},{4,1},{5,0},{6,3},{7,2},{8,13},{9,12},{10,... | collective-permute-start | bytes 24584 | tf_op jit(solution)/shard_map/ppermute | solution.py:233
  2.4 7.3 %collective-permute-start.1 = (bf16[4,1024]{1,0:T(4,128)(2,1)}, bf16[4,1024]{1,0:T(4,128)(2,1)S(1)}, u32[]{:S(2)}, u32[]{:S(2)}) collective-permute-start(bf16[4,1024]{1,0:T(4,128)(2,1)} %tokens.1), channel_id=1, source_target_pairs={{0,9},{1,8},{2,11},{3,10},{4,13},{5,12},{6,15},{7,14},{8,1},{9,0},... | collective-permute-start | bytes 24584 | tf_op jit(solution)/shard_map/ppermute | solution.py:233
  4.3 5.4 %collective-permute-start.2 = (bf16[4,1024]{1,0:T(4,128)(2,1)}, bf16[4,1024]{1,0:T(4,128)(2,1)S(1)}, u32[]{:S(2)}, u32[]{:S(2)}) collective-permute-start(bf16[4,1024]{1,0:T(4,128)(2,1)} %tokens.1), channel_id=1, source_target_pairs={{0,13},{1,12},{2,15},{3,14},{4,9},{5,8},{6,11},{7,10},{8,5},{9,4},... | collective-permute-start | bytes 24584 | tf_op jit(solution)/shard_map/ppermute | solution.py:233
  9.9 4.1 %collective-permute-start.3 = (bf16[4,1024]{1,0:T(4,128)(2,1)S(1)}, bf16[4,1024]{1,0:T(4,128)(2,1)S(1)}, u32[]{:S(2)}, u32[]{:S(2)}) collective-permute-start(bf16[4,1024]{1,0:T(4,128)(2,1)S(1)} %get-tuple-element.23), channel_id=1, source_target_pairs={{0,17},{1,16},{2,19},{3,18},{4,21},{5,20},{6,23},{7,22},{8,25},{9,... | collective-permute-start | bytes 24584 | tf_op jit(solution)/shard_map/ppermute | solution.py:233
  14.0 7.4 %copy-start.5 = (bf16[1024,256]{1,0:T(8,128)(2,1)S(1)}, bf16[1024,256]{1,0:T(8,128)(2,1)}, u32[]{:S(2)}) copy-start(bf16[1024,256]{1,0:T(8,128)(2,1)} %w_cq.1) | copy-start | bytes 1572868
  16.0 3.3 %collective-permute-start.4 = (f32[4,1024]{1,0:T(4,128)S(1)}, f32[4,1024]{1,0:T(4,128)S(1)}, u32[]{:S(2)}, u32[]{:S(2)}) collective-permute-start(f32[4,1024]{1,0:T(4,128)S(1)} %get-tuple-element.25.own), channel_id=1, source_target_pairs={{0,1},{1,0},{2,3},{3,2},{4,5},{5,4},{6,7},{7,6},{8,9},{9,8},{10,11... | collective-permute-start | bytes 49160 | tf_op jit(solution)/shard_map/ppermute | solution.py:233
  16.2 3.7 %collective-permute-start.5 = (f32[4,1024]{1,0:T(4,128)S(1)}, f32[4,1024]{1,0:T(4,128)S(1)}, u32[]{:S(2)}, u32[]{:S(2)}) collective-permute-start(f32[4,1024]{1,0:T(4,128)S(1)} %get-tuple-element.25.own), channel_id=1, source_target_pairs={{0,2},{1,3},{2,0},{3,1},{4,6},{5,7},{6,4},{7,5},{8,10},{9,11},{10,... | collective-permute-start | bytes 49160 | tf_op jit(solution)/shard_map/ppermute | solution.py:233
  18.0 3.3 %collective-permute-start.6 = (f32[4,1024]{1,0:T(4,128)S(1)}, f32[4,1024]{1,0:T(4,128)S(1)}, u32[]{:S(2)}, u32[]{:S(2)}) collective-permute-start(f32[4,1024]{1,0:T(4,128)S(1)} %get-tuple-element.25.own), channel_id=1, source_target_pairs={{0,3},{1,2},{2,1},{3,0},{4,7},{5,6},{6,5},{7,4},{8,11},{9,10},{10,... | collective-permute-start | bytes 49160 | tf_op jit(solution)/shard_map/ppermute | solution.py:233
  18.0 9.2 %copy-start.1 = (bf16[1024,1024]{1,0:T(8,128)(2,1)S(1)}, bf16[1024,1024]{1,0:T(8,128)(2,1)}, u32[]{:S(2)}) copy-start(bf16[1024,1024]{1,0:T(8,128)(2,1)} %w_up.1) | copy-start | bytes 6291460
  18.0 9.2 %copy-start.2 = (bf16[1024,1024]{1,0:T(8,128)(2,1)S(1)}, bf16[1024,1024]{1,0:T(8,128)(2,1)}, u32[]{:S(2)}) copy-start(bf16[1024,1024]{1,0:T(8,128)(2,1)} %w_down.1) | copy-start | bytes 6291460
  18.0 9.2 %copy-start.13 = (bf16[1024]{0:T(1024)(128)(2,1)S(1)}, bf16[1024]{0:T(1024)(128)(2,1)}, u32[]{:S(2)}) copy-start(bf16[1024]{0:T(1024)(128)(2,1)} %bias.4) | copy-start | bytes 6148
  18.0 9.2 %copy-start.14 = (bf16[1024]{0:T(1024)(128)(2,1)S(1)}, bf16[1024]{0:T(1024)(128)(2,1)}, u32[]{:S(2)}) copy-start(bf16[1024]{0:T(1024)(128)(2,1)} %gain.4) | copy-start | bytes 6148
  18.0 9.2 %copy-start.15 = (bf16[1024]{0:T(1024)(128)(2,1)S(1)}, bf16[1024]{0:T(1024)(128)(2,1)}, u32[]{:S(2)}) copy-start(bf16[1024]{0:T(1024)(128)(2,1)} %beta.4) | copy-start | bytes 6148
  18.1 9.2 %copy-start.16 = (bf16[1024]{0:T(1024)(128)(2,1)S(1)}, bf16[1024]{0:T(1024)(128)(2,1)}, u32[]{:S(2)}) copy-start(bf16[1024]{0:T(1024)(128)(2,1)} %b_up.1) | copy-start | bytes 6148
  23.3 1.9 %collective-permute-start.7 = (f32[4,1024]{1,0:T(4,128)S(1)}, f32[4,1024]{1,0:T(4,128)S(1)}, u32[]{:S(2)}, u32[]{:S(2)}) collective-permute-start(f32[4,1024]{1,0:T(4,128)S(1)} %get-tuple-element.27.own), channel_id=1, source_target_pairs={{0,1},{1,0},{2,3},{3,2},{4,5},{5,4},{6,7},{7,6},{8,9},{9,8},{10,11... | collective-permute-start | bytes 49160 | tf_op jit(solution)/shard_map/ppermute | solution.py:233
  23.4 3.8 %collective-permute-start.8 = (f32[4,1024]{1,0:T(4,128)S(1)}, f32[4,1024]{1,0:T(4,128)S(1)}, u32[]{:S(2)}, u32[]{:S(2)}) collective-permute-start(f32[4,1024]{1,0:T(4,128)S(1)} %get-tuple-element.27.own), channel_id=1, source_target_pairs={{0,2},{1,3},{2,0},{3,1},{4,6},{5,7},{6,4},{7,5},{8,10},{9,11},{10,... | collective-permute-start | bytes 49160 | tf_op jit(solution)/shard_map/ppermute | solution.py:233
  23.9 3.3 %collective-permute-start.9 = (f32[4,1024]{1,0:T(4,128)S(1)}, f32[4,1024]{1,0:T(4,128)S(1)}, u32[]{:S(2)}, u32[]{:S(2)}) collective-permute-start(f32[4,1024]{1,0:T(4,128)S(1)} %get-tuple-element.27.own), channel_id=1, source_target_pairs={{0,3},{1,2},{2,1},{3,0},{4,7},{5,6},{6,5},{7,4},{8,11},{9,10},{10,... | collective-permute-start | bytes 49160 | tf_op jit(solution)/shard_map/ppermute | solution.py:233
  28.1 1.9 %collective-permute-start.10 = (f32[4,1024]{1,0:T(4,128)S(1)}, f32[4,1024]{1,0:T(4,128)S(1)}, u32[]{:S(2)}, u32[]{:S(2)}) collective-permute-start(f32[4,1024]{1,0:T(4,128)S(1)} %get-tuple-element.29.own), channel_id=1, source_target_pairs={{0,1},{1,0},{2,3},{3,2},{4,5},{5,4},{6,7},{7,6},{8,9},{9,8},{10,11... | collective-permute-start | bytes 49160 | tf_op jit(solution)/shard_map/ppermute | solution.py:233
  28.3 3.7 %collective-permute-start.11 = (f32[4,1024]{1,0:T(4,128)S(1)}, f32[4,1024]{1,0:T(4,128)S(1)}, u32[]{:S(2)}, u32[]{:S(2)}) collective-permute-start(f32[4,1024]{1,0:T(4,128)S(1)} %get-tuple-element.29.own), channel_id=1, source_target_pairs={{0,2},{1,3},{2,0},{3,1},{4,6},{5,7},{6,4},{7,5},{8,10},{9,11},{10,... | collective-permute-start | bytes 49160 | tf_op jit(solution)/shard_map/ppermute | solution.py:233
  29.7 3.2 %collective-permute-start.12 = (f32[4,1024]{1,0:T(4,128)S(1)}, f32[4,1024]{1,0:T(4,128)S(1)}, u32[]{:S(2)}, u32[]{:S(2)}) collective-permute-start(f32[4,1024]{1,0:T(4,128)S(1)} %get-tuple-element.29.own), channel_id=1, source_target_pairs={{0,3},{1,2},{2,1},{3,0},{4,7},{5,6},{6,5},{7,4},{8,11},{9,10},{10,... | collective-permute-start | bytes 49160 | tf_op jit(solution)/shard_map/ppermute | solution.py:233
  33.1 3.1 %collective-permute-start.13 = (bf16[4,1024]{1,0:T(4,128)(2,1)S(1)}, bf16[4,1024]{1,0:T(4,128)(2,1)S(1)}, u32[]{:S(2)}, u32[]{:S(2)}) collective-permute-start(bf16[4,1024]{1,0:T(4,128)(2,1)S(1)} %last_norm.1.own), channel_id=1, source_target_pairs={{0,5},{1,4},{2,7},{3,6},{4,1},{5,0},{6,3},{7,2},{8,13},{9,12},{10,... | collective-permute-start | bytes 24584 | tf_op jit(solution)/shard_map/ppermute | solution.py:233
  34.4 3.1 %collective-permute-start.14 = (bf16[4,1024]{1,0:T(4,128)(2,1)S(1)}, bf16[4,1024]{1,0:T(4,128)(2,1)S(1)}, u32[]{:S(2)}, u32[]{:S(2)}) collective-permute-start(bf16[4,1024]{1,0:T(4,128)(2,1)S(1)} %last_norm.1.own), channel_id=1, source_target_pairs={{0,9},{1,8},{2,11},{3,10},{4,13},{5,12},{6,15},{7,14},{8,1},{9,0},... | collective-permute-start | bytes 24584 | tf_op jit(solution)/shard_map/ppermute | solution.py:233
  36.0 4.0 %collective-permute-start.15 = (bf16[4,1024]{1,0:T(4,128)(2,1)S(1)}, bf16[4,1024]{1,0:T(4,128)(2,1)S(1)}, u32[]{:S(2)}, u32[]{:S(2)}) collective-permute-start(bf16[4,1024]{1,0:T(4,128)(2,1)S(1)} %last_norm.1.own), channel_id=1, source_target_pairs={{0,13},{1,12},{2,15},{3,14},{4,9},{5,8},{6,11},{7,10},{8,5},{9,4},... | collective-permute-start | bytes 24584 | tf_op jit(solution)/shard_map/ppermute | solution.py:233
  40.1 4.0 %collective-permute-start.16 = (bf16[4,1024]{1,0:T(4,128)(2,1)S(1)}, bf16[4,1024]{1,0:T(4,128)(2,1)S(1)}, u32[]{:S(2)}, u32[]{:S(2)}) collective-permute-start(bf16[4,1024]{1,0:T(4,128)(2,1)S(1)} %get-tuple-element.32), channel_id=1, source_target_pairs={{0,17},{1,16},{2,19},{3,18},{4,21},{5,20},{6,23},{7,22},{8,25},{9,... | collective-permute-start | bytes 24584 | tf_op jit(solution)/shard_map/ppermute | solution.py:233
  (17 other events, 75.0 us)

commit v2 on v1

--- a/solution.py
+++ b/solution.py
@@ -48,7 +48,9 @@
 
 
 def attend(query, cache, lens, heads, fresh_key=None, fresh_value=None):
-    slots, _, span, width = cache.shape
+    where = [(ref, s) for ref in cache for s in range(ref.shape[0])]
+    slots = len(where)
+    _, _, span, width = cache[0].shape
     pair = 2 * heads
     scale = HEAD_DIM ** (-0.5)
     row = lax.broadcasted_iota(jnp.int32, (pair, width), 0)
@@ -60,7 +62,7 @@
     rows = []
     for slot in range(0, slots, 2):
         q = jnp.where(own, head_rows(query, slot, heads, first) * scale, 0.0)
-        raw = [dot_t(q, cache[slot + i, 0]) for i in range(2)]
+        raw = [dot_t(q, ref[at, 0]) for ref, at in where[slot : slot + 2]]
         length = jnp.where(first_col, lens[slot], lens[slot + 1])
         scores = jnp.where(position < length, jnp.where(first_col, raw[0], raw[1]), MASKED)
         top = jnp.max(scores, axis=-1, keepdims=True)
@@ -74,20 +76,19 @@
         if fresh_key is not None:
             expn = jnp.exp(fresh - top)
             total = total + expn
-        share = 1.0 / total
-        weights = expo * share
-        out = [dot(weights, cache[slot + i, 1]) for i in range(2)]
+        out = [dot(expo, ref[at, 1]) for ref, at in where[slot : slot + 2]]
         ctx = jnp.where(first, out[0], out[1])
         if fresh_key is not None:
-            ctx = ctx + round_rows(expn * share) * v_new
-        ctx = jnp.where(own, round_rows(ctx), 0.0)
+            ctx = ctx + round_rows(expn) * v_new
+        ctx = jnp.where(own, round_rows(ctx * (1.0 / total)), 0.0)
         rows.append(jnp.sum(ctx[:heads], axis=0, keepdims=True))
         rows.append(jnp.sum(ctx[heads:], axis=0, keepdims=True))
     return jnp.concatenate(rows + [jnp.zeros((8 - slots, width), f32)], axis=0)
 
 
-def split_cache(cache, out_ref):
-    slots, count, _ = cache.shape
+def split_cache(cache, out_ref, start):
+    slots = out_ref.shape[0]
+    count = cache.shape[1]
     tiles = out_ref.shape[3] // LANES
     group = 2 * tiles
     step = 256
@@ -97,25 +98,13 @@
     order = (c == (r % part) * group + r // part).astype(bf16)
     for slot in range(slots):
         for at in range(count // step):
-            rows = dot(order, cache[slot, at * step : (at + 1) * step]).astype(bf16)
+            rows = dot(order, cache[start + slot, at * step : (at + 1) * step]).astype(bf16)
             for tile in range(tiles):
                 for kind in range(2):
                     g = (tile * 2 + kind) * part
                     out_ref[
                         slot, kind, at * part : (at + 1) * part, tile * LANES : (tile + 1) * LANES
                     ] = rows[g : g + part]
-        yield slot
-
-
-def load_split(source, held, sems, out_ref):
-    copies = []
-    for slot in range(held.shape[0]):
-        copies.append(pltpu.make_async_copy(source.at[slot], held.at[slot], sems.at[slot]))
-        copies[-1].start()
-    copies[0].wait()
-    for slot in split_cache(held, out_ref):
-        if slot + 1 < len(copies):
-            copies[slot + 1].wait()
 
 
 def wanted(deal, rows, me, far, back):
@@ -134,17 +123,21 @@
     return (have == take).astype(bf16)
 
 
-def plan_kernel(deal, tokens, cache, own_ref, out_ref, back_ref, kv_ref, held, sems, *, far):
+def stub_kernel(out_ref):
+    out_ref[...] = jnp.zeros_like(out_ref)
+
+
+def plan_kernel(deal, stub, tokens, cache, own_ref, out_ref, back_ref, kv_ref, *, far):
     me = lax.axis_index("req")
     rows = tokens.shape[0]
     own_ref[...] = tokens[...]
     out_ref[...] = wanted(deal, rows, me, far, False)
     back_ref[...] = wanted(deal, rows, me, far, True)
-    load_split(cache, held, sems, kv_ref)
-
-
-def split_kernel(cache, kv_ref, held, sems):
-    load_split(cache, held, sems, kv_ref)
+    split_cache(cache, kv_ref, 0)
+
+
+def split_kernel(after, cache, kv_ref, *, start):
+    split_cache(cache, kv_ref, start)
 
 
 def sort_kernel(hit, own, g1, g2, g3, mine_ref, theirs_ref):
@@ -160,8 +153,9 @@
 
 
 def first_kernel(
-    lens, mine, more, w_qkv, b_qkv, cache, w_out, x_ref, part_ref, *, heads
+    lens, mine, more, w_qkv, b_qkv, w_out, *refs, heads
 ):
+    *cache, x_ref, part_ref = refs
     slots = x_ref.shape[0]
     x = mine[...].astype(f32) + more[...].astype(f32)
     x_ref[...] = x.astype(bf16)
@@ -186,7 +180,7 @@
     h_ref[...] = h1
     cq = round_rows(dot(pad_rows(h1.astype(f32), 8), w_cq[...]) + flat(b_cq))
     length = [lens[s] for s in range(slots)]
-    ctx = attend(cq, cache, length, heads)
+    ctx = attend(cq, [cache], length, heads)
     part_ref[...] = dot(ctx, w_cout[...])[:slots]
 
 
@@ -209,24 +203,23 @@
     out_ref[...] = (mine[...].astype(f32) + more[...].astype(f32)).astype(bf16)
 
 
-def call(kernel, out_shapes, args, smem=0, hbm=(), scratch=(), name=None, cost=None):
+def call(kernel, out_shapes, args, smem=0, name=None, cost=None):
     vmem = pl.BlockSpec(memory_space=pltpu.VMEM)
     scalar = pl.BlockSpec(memory_space=pltpu.SMEM)
-    far = pl.BlockSpec(memory_space=pltpu.HBM)
     outs = [jax.ShapeDtypeStruct(s, d) for s, d in out_shapes]
-    specs = [scalar if i < smem else far if i in hbm else vmem for i in range(len(args))]
+    specs = [scalar if i < smem else vmem for i in range(len(args))]
     if cost is not None:
         cost = pl.CostEstimate(flops=cost, bytes_accessed=0, transcendentals=0)
-    return pl.pallas_call(
+    made = pl.pallas_call(
         kernel,
         out_shape=outs,
         in_specs=specs,
         out_specs=[vmem] * len(outs),
-        scratch_shapes=list(scratch),
         compiler_params=pltpu.CompilerParams(vmem_limit_bytes=24 * 2**20),
         cost_estimate=cost,
         name=name,
     )(*args)
+    return list(made)
 
 
 def swap(value, axis, size, mask):
@@ -272,14 +265,20 @@
     return picked, jnp.zeros_like(picked)
 
 
-def split_shapes(cache):
+def split_part(after, cache, start, slots, name):
+    _, span, _, width = cache.shape
+    return call(
+        functools.partial(split_kernel, start=start),
+        [((slots, 2, span, width), bf16)],
+        [after, tile_rows(cache)],
+        name=name,
+    )
+
+
+def tile_rows(cache):
     slots, span, _, width = cache.shape
-    tiles = width // LANES
-    scratch = [
-        pltpu.VMEM((slots, span * 2 * tiles, LANES), bf16),
-        pltpu.SemaphoreType.DMA((slots,)),
-    ]
-    return ((slots, 2, span, width), bf16), scratch
+    split = cache.reshape(slots, span, 2, width // LANES, LANES)
+    return split.transpose(0, 1, 3, 2, 4).reshape(slots, -1, LANES)
 
 
 def sum_parts(value, mesh_shape):
@@ -322,48 +321,33 @@
     width = self_cache.shape[3]
     heads = width // HEAD_DIM
 
-    def tile_rows(cache):
-        slots, span = cache.shape[0], cache.shape[1]
-        split = cache.reshape(slots, span, 2, width // LANES, LANES)
-        return split.transpose(0, 1, 3, 2, 4).reshape(slots, -1, LANES)
-
     state, sums = ((rows, model), bf16), ((rows, model), f32)
-    split, scratch = split_shapes(self_cache)
     hops = mesh_shape["req"] == 2 * FAR
     if hops:
         near = near_swaps(tokens)
         hits = ((2 * rows, 4 * rows), bf16)
-        own, hit_out, hit_back, self_kv = call(
+        half = rows // 2
+        (stub,) = call(stub_kernel, [((8, LANES), f32)], [], name="stub", cost=SPARE_FLOPS)
+        own, hit_out, hit_back, kv = call(
             functools.partial(plan_kernel, far=FAR),
-            [state, hits, hits, split],
-            [deal, tokens, tile_rows(self_cache)],
+            [state, hits, hits, ((half, 2, self_cache.shape[1], width), bf16)],
+            [deal, stub, tokens, tile_rows(self_cache)],
             smem=1,
-            hbm=(2,),
-            scratch=scratch,
             name="plan",
         )
         mine, more = sort_rows(hit_out, own, near, "sort_out")
+        self_kv = [kv] + split_part(mine, self_cache, half, rows - half, "split_self")
     else:
         mine, more = deal_whole(tokens, deal, False)
-        (self_kv,) = call(
-            split_kernel, [split], [tile_rows(self_cache)], hbm=(0,), scratch=scratch, name="split"
-        )
-    split, scratch = split_shapes(cross_cache)
-    (cross_kv,) = call(
-        split_kernel,
-        [split],
-        [tile_rows(cross_cache)],
-        hbm=(0,),
-        scratch=scratch,
-        name="split_cross",
-    )
+        self_kv = split_part(mine, self_cache, 0, rows, "split_self")
     x, part = call(
         functools.partial(first_kernel, heads=heads),
         [state, sums],
-        [self_len, mine, more, w_qkv.transpose(1, 0, 2), b_qkv, self_kv, w_out],
+        [self_len, mine, more, w_qkv.transpose(1, 0, 2), b_qkv, w_out] + list(self_kv),
         smem=1,
         name="self_attention",
     )
+    (cross_kv,) = split_part(x, cross_cache, 0, rows, "split_cross")
     h1, part = call(
         functools.partial(second_kernel, heads=heads),
         [state, sums],

time: 44.9 us -> 40.6 us (0.904)
  local copies, waits for them, and re-layouts: 3.06 us -> 0.13 us
  waiting for transfers between devices: 13.8 us -> 15.2 us
  Pallas kernels: 9.54 us -> 8.15 us
  starting transfers between devices: 18 us -> 16.7 us
    unnamed x48, local copies, waits for them, and re-layouts: 3.06 us -> 0.13 us
    ppermute x17, waiting for transfers between devices: 13.8 us -> 15.2 us  [swap(): return lax.ppermute(value, axis, [(i, i ^ mask) for i in range(size)])]
    pallas_call x9 -> x11, Pallas kernels: 9.54 us -> 8.15 us  [call(): pl.pallas_call(kernel, out_shape=outs, in_specs=specs, out_specs=[vmem] *...]
    ppermute x17, starting transfers between devices: 18 us -> 16.7 us  [swap(): return lax.ppermute(value, axis, [(i, i ^ mask) for i in range(size)])]
  transfers between devices with their start and end apart: 17 -> 17, of which waited for: 10 -> 13; matrix products, arithmetic and copies ran while one was open for 0% -> 0% of each run, Pallas kernels for 8% -> 7%
where the time goes in v2:
time: 40.6 us; the launch traced here: 40.5 us
  starting transfers between devices  16.7 us (41%)
  waiting for transfers between devices  15.2 us (37%)
  Pallas kernels  8.15 us (20%)
    ppermute x17, starting transfers between devices, swap(): return lax.ppermute(value, axis, [(i, i ^ mask) for i in range(size)])  16.7 us
    ppermute x17, waiting for transfers between devices, swap(): return lax.ppermute(value, axis, [(i, i ^ mask) for i in range(size)])  15.2 us
    pallas_call x11, Pallas kernels, call(): pl.pallas_call(kernel, out_shape=outs, in_specs=specs, out_specs=[vmem] *...  8.15 us
  transfers between devices with their start and end apart: 17, of which 13 were waited for; matrix products, arithmetic and copies ran while one was open for 0% of the time, Pallas kernels for 7%

profile of v2, /device:TPU:0, one launch (start us, length us, event | category | flops | bytes accessed | tf_op | source)
XLA Modules:
  0.0 40.5 jit_solution(12489080657668476222)
XLA Ops:
  0.0 2.5 %collective-permute-start = (bf16[4,1024]{1,0:T(4,128)(2,1)}, bf16[4,1024]{1,0:T(4,128)(2,1)S(1)}, u32[]{:S(2)}, u32[]{:S(2)}) collective-permute-start(bf16[4,1024]{1,0:T(4,128)(2,1)} %tokens.1), channel_id=1, source_target_pairs={{0,5},{1,4},{2,7},{3,6},{4,1},{5,0},{6,3},{7,2},{8,13},{9,12},{10,... | collective-permute-start | bytes 24584 | tf_op jit(solution)/shard_map/ppermute | solution.py:226
  2.5 1.8 %collective-permute-start.2 = (bf16[4,1024]{1,0:T(4,128)(2,1)}, bf16[4,1024]{1,0:T(4,128)(2,1)S(1)}, u32[]{:S(2)}, u32[]{:S(2)}) collective-permute-start(bf16[4,1024]{1,0:T(4,128)(2,1)} %tokens.1), channel_id=1, source_target_pairs={{0,13},{1,12},{2,15},{3,14},{4,9},{5,8},{6,11},{7,10},{8,5},{9,4},... | collective-permute-start | bytes 24584 | tf_op jit(solution)/shard_map/ppermute | solution.py:226
  4.4 1.2 %plan.1 = (bf16[4,1024]{1,0:T(4,128)(2,1)S(1)}, bf16[8,16]{1,0:T(8,128)(2,1)S(1)}, bf16[8,16]{1,0:T(8,128)(2,1)S(1)}, bf16[2,2,512,256]{3,2,1,0:T(8,128)(2,1)S(1)}) custom-call(s32[32]{0:T(128)S(1)} %copy-done.20, f32[8,128]{1,0:T(8,128)S(1)} %stub.1, bf16[4,1024]{1,0:T(4,128)(2,1)S(1)} %copy-done.8, bf16[4,2048,128]{2,1,0:T(8,128)(2,1)S(1)} %bitcast.11), custom_call_target="tpu_custom_call" | custom-call | tf_op jit(solution)/shard_map/plan/pallas_call | solution.py:213
  5.6 1.0 %collective-permute-done.2.g3 = bf16[4,1024]{1,0:T(4,128)(2,1)S(1)} collective-permute-done((bf16[4,1024]{1,0:T(4,128)(2,1)}, bf16[4,1024]{1,0:T(4,128)(2,1)S(1)}, u32[]{:S(2)}, u32[]{:S(2)}) %collective-permute-start.2) | collective-permute-done | bytes 8224 | tf_op jit(solution)/shard_map/ppermute | solution.py:226
  6.7 0.9 %collective-permute-done.1.g2 = bf16[4,1024]{1,0:T(4,128)(2,1)S(1)} collective-permute-done((bf16[4,1024]{1,0:T(4,128)(2,1)}, bf16[4,1024]{1,0:T(4,128)(2,1)S(1)}, u32[]{:S(2)}, u32[]{:S(2)}) %collective-permute-start.1) | collective-permute-done | bytes 8224 | tf_op jit(solution)/shard_map/ppermute | solution.py:226
  7.7 2.4 %collective-permute-start.3 = (bf16[4,1024]{1,0:T(4,128)(2,1)S(1)}, bf16[4,1024]{1,0:T(4,128)(2,1)S(1)}, u32[]{:S(2)}, u32[]{:S(2)}) collective-permute-start(bf16[4,1024]{1,0:T(4,128)(2,1)S(1)} %get-tuple-element.23), channel_id=1, source_target_pairs={{0,17},{1,16},{2,19},{3,18},{4,21},{5,20},{6,23},{7,22},{8,25},{9,... | collective-permute-start | bytes 24584 | tf_op jit(solution)/shard_map/ppermute | solution.py:226
  10.8 1.0 %collective-permute-done.3.more = bf16[4,1024]{1,0:T(4,128)(2,1)S(1)} collective-permute-done((bf16[4,1024]{1,0:T(4,128)(2,1)S(1)}, bf16[4,1024]{1,0:T(4,128)(2,1)S(1)}, u32[]{:S(2)}, u32[]{:S(2)}) %collective-permute-start.3) | collective-permute-done | bytes 8224 | tf_op jit(solution)/shard_map/ppermute | solution.py:226
  11.8 1.8 %self_attention.1 = (bf16[4,1024]{1,0:T(4,128)(2,1)S(1)}, f32[4,1024]{1,0:T(4,128)S(1)}) custom-call(s32[4]{0:T(128)S(1)} %copy-done.21, bf16[4,1024]{1,0:T(4,128)(2,1)S(1)} %get-tuple-element.22.after.mine, bf16[4,1024]{1,0:T(4,128)(2,1)S(1)} %collective-permute-done.3.more, bf16[3,1024,256]{2,1,0:T(8,128)(2,1)S(1)} %bitcast.13, ...), custom_call_target="tpu_custom_call" | custom-call | tf_op jit(solution)/shard_map/self_attention/pallas_call | solution.py:213
  13.7 1.3 %collective-permute-start.6 = (f32[4,1024]{1,0:T(4,128)S(1)}, f32[4,1024]{1,0:T(4,128)S(1)}, u32[]{:S(2)}, u32[]{:S(2)}) collective-permute-start(f32[4,1024]{1,0:T(4,128)S(1)} %get-tuple-element.25.own), channel_id=1, source_target_pairs={{0,3},{1,2},{2,1},{3,0},{4,7},{5,6},{6,5},{7,4},{8,11},{9,10},{10,... | collective-permute-start | bytes 49160 | tf_op jit(solution)/shard_map/ppermute | solution.py:226
  15.7 0.7 %split_cross.1.cache = bf16[4,2,256,256]{3,2,1,0:T(8,128)(2,1)S(1)} custom-call(bf16[4,1024]{1,0:T(4,128)(2,1)S(1)} %get-tuple-element.26.after.x, bf16[4,1024,128]{2,1,0:T(8,128)(2,1)S(1)} %bitcast.14), custom_call_target="tpu_custom_call" | custom-call | tf_op jit(solution)/shard_map/split_cross/pallas_call | solution.py:213
  16.9 1.8 %collective-permute-done.5.p2 = f32[4,1024]{1,0:T(4,128)S(1)} collective-permute-done((f32[4,1024]{1,0:T(4,128)S(1)}, f32[4,1024]{1,0:T(4,128)S(1)}, u32[]{:S(2)}, u32[]{:S(2)}) %collective-permute-start.5) | collective-permute-done | bytes 16416 | tf_op jit(solution)/shard_map/ppermute | solution.py:226
  18.8 1.8 %cross_attention.1 = (bf16[4,1024]{1,0:T(4,128)(2,1)S(1)}, f32[4,1024]{1,0:T(4,128)S(1)}) custom-call(s32[4]{0:T(128)S(1)} %copy-done.22, f32[4,1024]{1,0:T(4,128)S(1)} %get-tuple-element.25.own, f32[4,1024]{1,0:T(4,128)S(1)} %collective-permute-done.4.p1, f32[4,1024]{1,0:T(4,128)S(1)} %collective-permute-done.5.p2, ...), custom_call_target="tpu_custom_call" | custom-call | tf_op jit(solution)/shard_map/cross_attention/pallas_call | solution.py:213
  20.6 0.9 %collective-permute-start.8 = (f32[4,1024]{1,0:T(4,128)S(1)}, f32[4,1024]{1,0:T(4,128)S(1)}, u32[]{:S(2)}, u32[]{:S(2)}) collective-permute-start(f32[4,1024]{1,0:T(4,128)S(1)} %get-tuple-element.27.own), channel_id=1, source_target_pairs={{0,2},{1,3},{2,0},{3,1},{4,6},{5,7},{6,4},{7,5},{8,10},{9,11},{10,... | collective-permute-start | bytes 49160 | tf_op jit(solution)/shard_map/ppermute | solution.py:226
  21.4 1.0 %collective-permute-start.7 = (f32[4,1024]{1,0:T(4,128)S(1)}, f32[4,1024]{1,0:T(4,128)S(1)}, u32[]{:S(2)}, u32[]{:S(2)}) collective-permute-start(f32[4,1024]{1,0:T(4,128)S(1)} %get-tuple-element.27.own), channel_id=1, source_target_pairs={{0,1},{1,0},{2,3},{3,2},{4,5},{5,4},{6,7},{7,6},{8,9},{9,8},{10,11... | collective-permute-start | bytes 49160 | tf_op jit(solution)/shard_map/ppermute | solution.py:226
  22.5 1.3 %collective-permute-done.9.p3 = f32[4,1024]{1,0:T(4,128)S(1)} collective-permute-done((f32[4,1024]{1,0:T(4,128)S(1)}, f32[4,1024]{1,0:T(4,128)S(1)}, u32[]{:S(2)}, u32[]{:S(2)}) %collective-permute-start.9) | collective-permute-done | bytes 16416 | tf_op jit(solution)/shard_map/ppermute | solution.py:226
  24.5 0.8 %feed_forward.1 = (bf16[4,1024]{1,0:T(4,128)(2,1)S(1)}, f32[4,1024]{1,0:T(4,128)S(1)}) custom-call(f32[4,1024]{1,0:T(4,128)S(1)} %get-tuple-element.27.own, f32[4,1024]{1,0:T(4,128)S(1)} %collective-permute-done.7.p1, f32[4,1024]{1,0:T(4,128)S(1)} %collective-permute-done.8.p2, f32[4,1024]{1,0:T(4,128)S(1)} %collective-permute-done.9.p3, ...), custom_call_target="tpu_custom_call" | custom-call | tf_op jit(solution)/shard_map/feed_forward/pallas_call | solution.py:213
  26.5 0.7 %collective-permute-start.10 = (f32[4,1024]{1,0:T(4,128)S(1)}, f32[4,1024]{1,0:T(4,128)S(1)}, u32[]{:S(2)}, u32[]{:S(2)}) collective-permute-start(f32[4,1024]{1,0:T(4,128)S(1)} %get-tuple-element.29.own), channel_id=1, source_target_pairs={{0,1},{1,0},{2,3},{3,2},{4,5},{5,4},{6,7},{7,6},{8,9},{9,8},{10,11... | collective-permute-start | bytes 49160 | tf_op jit(solution)/shard_map/ppermute | solution.py:226
  27.2 1.3 %collective-permute-done.12.p3 = f32[4,1024]{1,0:T(4,128)S(1)} collective-permute-done((f32[4,1024]{1,0:T(4,128)S(1)}, f32[4,1024]{1,0:T(4,128)S(1)}, u32[]{:S(2)}, u32[]{:S(2)}) %collective-permute-start.12) | collective-permute-done | bytes 16416 | tf_op jit(solution)/shard_map/ppermute | solution.py:226
  28.5 1.1 %collective-permute-done.11.p2 = f32[4,1024]{1,0:T(4,128)S(1)} collective-permute-done((f32[4,1024]{1,0:T(4,128)S(1)}, f32[4,1024]{1,0:T(4,128)S(1)}, u32[]{:S(2)}, u32[]{:S(2)}) %collective-permute-start.11) | collective-permute-done | bytes 16416 | tf_op jit(solution)/shard_map/ppermute | solution.py:226
  30.2 2.5 %collective-permute-start.14 = (bf16[4,1024]{1,0:T(4,128)(2,1)S(1)}, bf16[4,1024]{1,0:T(4,128)(2,1)S(1)}, u32[]{:S(2)}, u32[]{:S(2)}) collective-permute-start(bf16[4,1024]{1,0:T(4,128)(2,1)S(1)} %last_norm.1.own), channel_id=1, source_target_pairs={{0,9},{1,8},{2,11},{3,10},{4,13},{5,12},{6,15},{7,14},{8,1},{9,0},... | collective-permute-start | bytes 24584 | tf_op jit(solution)/shard_map/ppermute | solution.py:226
  32.7 1.2 %collective-permute-done.15.g3 = bf16[4,1024]{1,0:T(4,128)(2,1)S(1)} collective-permute-done((bf16[4,1024]{1,0:T(4,128)(2,1)S(1)}, bf16[4,1024]{1,0:T(4,128)(2,1)S(1)}, u32[]{:S(2)}, u32[]{:S(2)}) %collective-permute-start.15) | collective-permute-done | bytes 8224 | tf_op jit(solution)/shard_map/ppermute | solution.py:226
  34.1 1.7 %collective-permute-done.13.g1 = bf16[4,1024]{1,0:T(4,128)(2,1)S(1)} collective-permute-done((bf16[4,1024]{1,0:T(4,128)(2,1)S(1)}, bf16[4,1024]{1,0:T(4,128)(2,1)S(1)}, u32[]{:S(2)}, u32[]{:S(2)}) %collective-permute-start.13) | collective-permute-done | bytes 8224 | tf_op jit(solution)/shard_map/ppermute | solution.py:226
  35.9 1.5 %collective-permute-start.16 = (bf16[4,1024]{1,0:T(4,128)(2,1)S(1)}, bf16[4,1024]{1,0:T(4,128)(2,1)S(1)}, u32[]{:S(2)}, u32[]{:S(2)}) collective-permute-start(bf16[4,1024]{1,0:T(4,128)(2,1)S(1)} %get-tuple-element.32), channel_id=1, source_target_pairs={{0,17},{1,16},{2,19},{3,18},{4,21},{5,20},{6,23},{7,22},{8,25},{9,... | collective-permute-start | bytes 24584 | tf_op jit(solution)/shard_map/ppermute | solution.py:226
  37.4 2.5 %collective-permute-done.16.more = bf16[4,1024]{1,0:T(4,128)(2,1)S(1)} collective-permute-done((bf16[4,1024]{1,0:T(4,128)(2,1)S(1)}, bf16[4,1024]{1,0:T(4,128)(2,1)S(1)}, u32[]{:S(2)}, u32[]{:S(2)}) %collective-permute-start.16) | collective-permute-done | bytes 8224 | tf_op jit(solution)/shard_map/ppermute | solution.py:226
  (69 shorter events, 5.5 us)
Async XLA Ops:
  0.0 5.6 %collective-permute-start = (bf16[4,1024]{1,0:T(4,128)(2,1)}, bf16[4,1024]{1,0:T(4,128)(2,1)S(1)}, u32[]{:S(2)}, u32[]{:S(2)}) collective-permute-start(bf16[4,1024]{1,0:T(4,128)(2,1)} %tokens.1), channel_id=1, source_target_pairs={{0,5},{1,4},{2,7},{3,6},{4,1},{5,0},{6,3},{7,2},{8,13},{9,12},{10,... | collective-permute-start | bytes 24584 | tf_op jit(solution)/shard_map/ppermute | solution.py:226
  2.5 4.2 %collective-permute-start.2 = (bf16[4,1024]{1,0:T(4,128)(2,1)}, bf16[4,1024]{1,0:T(4,128)(2,1)S(1)}, u32[]{:S(2)}, u32[]{:S(2)}) collective-permute-start(bf16[4,1024]{1,0:T(4,128)(2,1)} %tokens.1), channel_id=1, source_target_pairs={{0,13},{1,12},{2,15},{3,14},{4,9},{5,8},{6,11},{7,10},{8,5},{9,4},... | collective-permute-start | bytes 24584 | tf_op jit(solution)/shard_map/ppermute | solution.py:226
  4.3 3.3 %collective-permute-start.1 = (bf16[4,1024]{1,0:T(4,128)(2,1)}, bf16[4,1024]{1,0:T(4,128)(2,1)S(1)}, u32[]{:S(2)}, u32[]{:S(2)}) collective-permute-start(bf16[4,1024]{1,0:T(4,128)(2,1)} %tokens.1), channel_id=1, source_target_pairs={{0,9},{1,8},{2,11},{3,10},{4,13},{5,12},{6,15},{7,14},{8,1},{9,0},... | collective-permute-start | bytes 24584 | tf_op jit(solution)/shard_map/ppermute | solution.py:226
  7.7 4.0 %collective-permute-start.3 = (bf16[4,1024]{1,0:T(4,128)(2,1)S(1)}, bf16[4,1024]{1,0:T(4,128)(2,1)S(1)}, u32[]{:S(2)}, u32[]{:S(2)}) collective-permute-start(bf16[4,1024]{1,0:T(4,128)(2,1)S(1)} %get-tuple-element.23), channel_id=1, source_target_pairs={{0,17},{1,16},{2,19},{3,18},{4,21},{5,20},{6,23},{7,22},{8,25},{9,... | collective-permute-start | bytes 24584 | tf_op jit(solution)/shard_map/ppermute | solution.py:226
  11.8 6.9 %copy-start.5 = (bf16[1024,256]{1,0:T(8,128)(2,1)S(1)}, bf16[1024,256]{1,0:T(8,128)(2,1)}, u32[]{:S(2)}) copy-start(bf16[1024,256]{1,0:T(8,128)(2,1)} %w_cq.1) | copy-start | bytes 1572868
  13.7 3.2 %collective-permute-start.6 = (f32[4,1024]{1,0:T(4,128)S(1)}, f32[4,1024]{1,0:T(4,128)S(1)}, u32[]{:S(2)}, u32[]{:S(2)}) collective-permute-start(f32[4,1024]{1,0:T(4,128)S(1)} %get-tuple-element.25.own), channel_id=1, source_target_pairs={{0,3},{1,2},{2,1},{3,0},{4,7},{5,6},{6,5},{7,4},{8,11},{9,10},{10,... | collective-permute-start | bytes 49160 | tf_op jit(solution)/shard_map/ppermute | solution.py:226
  15.0 3.8 %collective-permute-start.5 = (f32[4,1024]{1,0:T(4,128)S(1)}, f32[4,1024]{1,0:T(4,128)S(1)}, u32[]{:S(2)}, u32[]{:S(2)}) collective-permute-start(f32[4,1024]{1,0:T(4,128)S(1)} %get-tuple-element.25.own), channel_id=1, source_target_pairs={{0,2},{1,3},{2,0},{3,1},{4,6},{5,7},{6,4},{7,5},{8,10},{9,11},{10,... | collective-permute-start | bytes 49160 | tf_op jit(solution)/shard_map/ppermute | solution.py:226
  15.5 3.2 %collective-permute-start.4 = (f32[4,1024]{1,0:T(4,128)S(1)}, f32[4,1024]{1,0:T(4,128)S(1)}, u32[]{:S(2)}, u32[]{:S(2)}) collective-permute-start(f32[4,1024]{1,0:T(4,128)S(1)} %get-tuple-element.25.own), channel_id=1, source_target_pairs={{0,1},{1,0},{2,3},{3,2},{4,5},{5,4},{6,7},{7,6},{8,9},{9,8},{10,11... | collective-permute-start | bytes 49160 | tf_op jit(solution)/shard_map/ppermute | solution.py:226
  15.6 8.8 %copy-start.1 = (bf16[1024,1024]{1,0:T(8,128)(2,1)S(1)}, bf16[1024,1024]{1,0:T(8,128)(2,1)}, u32[]{:S(2)}) copy-start(bf16[1024,1024]{1,0:T(8,128)(2,1)} %w_up.1) | copy-start | bytes 6291460
  15.6 8.8 %copy-start.2 = (bf16[1024,1024]{1,0:T(8,128)(2,1)S(1)}, bf16[1024,1024]{1,0:T(8,128)(2,1)}, u32[]{:S(2)}) copy-start(bf16[1024,1024]{1,0:T(8,128)(2,1)} %w_down.1) | copy-start | bytes 6291460
  15.6 8.8 %copy-start.13 = (bf16[1024]{0:T(1024)(128)(2,1)S(1)}, bf16[1024]{0:T(1024)(128)(2,1)}, u32[]{:S(2)}) copy-start(bf16[1024]{0:T(1024)(128)(2,1)} %bias.4) | copy-start | bytes 6148
  15.6 8.8 %copy-start.14 = (bf16[1024]{0:T(1024)(128)(2,1)S(1)}, bf16[1024]{0:T(1024)(128)(2,1)}, u32[]{:S(2)}) copy-start(bf16[1024]{0:T(1024)(128)(2,1)} %gain.4) | copy-start | bytes 6148
  15.6 8.8 %copy-start.15 = (bf16[1024]{0:T(1024)(128)(2,1)S(1)}, bf16[1024]{0:T(1024)(128)(2,1)}, u32[]{:S(2)}) copy-start(bf16[1024]{0:T(1024)(128)(2,1)} %beta.4) | copy-start | bytes 6148
  15.7 8.8 %copy-start.16 = (bf16[1024]{0:T(1024)(128)(2,1)S(1)}, bf16[1024]{0:T(1024)(128)(2,1)}, u32[]{:S(2)}) copy-start(bf16[1024]{0:T(1024)(128)(2,1)} %b_up.1) | copy-start | bytes 6148
  20.6 3.2 %collective-permute-start.9 = (f32[4,1024]{1,0:T(4,128)S(1)}, f32[4,1024]{1,0:T(4,128)S(1)}, u32[]{:S(2)}, u32[]{:S(2)}) collective-permute-start(f32[4,1024]{1,0:T(4,128)S(1)} %get-tuple-element.27.own), channel_id=1, source_target_pairs={{0,3},{1,2},{2,1},{3,0},{4,7},{5,6},{6,5},{7,4},{8,11},{9,10},{10,... | collective-permute-start | bytes 49160 | tf_op jit(solution)/shard_map/ppermute | solution.py:226
  20.6 3.8 %collective-permute-start.8 = (f32[4,1024]{1,0:T(4,128)S(1)}, f32[4,1024]{1,0:T(4,128)S(1)}, u32[]{:S(2)}, u32[]{:S(2)}) collective-permute-start(f32[4,1024]{1,0:T(4,128)S(1)} %get-tuple-element.27.own), channel_id=1, source_target_pairs={{0,2},{1,3},{2,0},{3,1},{4,6},{5,7},{6,4},{7,5},{8,10},{9,11},{10,... | collective-permute-start | bytes 49160 | tf_op jit(solution)/shard_map/ppermute | solution.py:226
  21.4 2.9 %collective-permute-start.7 = (f32[4,1024]{1,0:T(4,128)S(1)}, f32[4,1024]{1,0:T(4,128)S(1)}, u32[]{:S(2)}, u32[]{:S(2)}) collective-permute-start(f32[4,1024]{1,0:T(4,128)S(1)} %get-tuple-element.27.own), channel_id=1, source_target_pairs={{0,1},{1,0},{2,3},{3,2},{4,5},{5,4},{6,7},{7,6},{8,9},{9,8},{10,11... | collective-permute-start | bytes 49160 | tf_op jit(solution)/shard_map/ppermute | solution.py:226
  25.3 3.2 %collective-permute-start.12 = (f32[4,1024]{1,0:T(4,128)S(1)}, f32[4,1024]{1,0:T(4,128)S(1)}, u32[]{:S(2)}, u32[]{:S(2)}) collective-permute-start(f32[4,1024]{1,0:T(4,128)S(1)} %get-tuple-element.29.own), channel_id=1, source_target_pairs={{0,3},{1,2},{2,1},{3,0},{4,7},{5,6},{6,5},{7,4},{8,11},{9,10},{10,... | collective-permute-start | bytes 49160 | tf_op jit(solution)/shard_map/ppermute | solution.py:226
  25.9 3.8 %collective-permute-start.11 = (f32[4,1024]{1,0:T(4,128)S(1)}, f32[4,1024]{1,0:T(4,128)S(1)}, u32[]{:S(2)}, u32[]{:S(2)}) collective-permute-start(f32[4,1024]{1,0:T(4,128)S(1)} %get-tuple-element.29.own), channel_id=1, source_target_pairs={{0,2},{1,3},{2,0},{3,1},{4,6},{5,7},{6,4},{7,5},{8,10},{9,11},{10,... | collective-permute-start | bytes 49160 | tf_op jit(solution)/shard_map/ppermute | solution.py:226
  26.5 3.2 %collective-permute-start.10 = (f32[4,1024]{1,0:T(4,128)S(1)}, f32[4,1024]{1,0:T(4,128)S(1)}, u32[]{:S(2)}, u32[]{:S(2)}) collective-permute-start(f32[4,1024]{1,0:T(4,128)S(1)} %get-tuple-element.29.own), channel_id=1, source_target_pairs={{0,1},{1,0},{2,3},{3,2},{4,5},{5,4},{6,7},{7,6},{8,9},{9,8},{10,11... | collective-permute-start | bytes 49160 | tf_op jit(solution)/shard_map/ppermute | solution.py:226
  29.9 4.0 %collective-permute-start.15 = (bf16[4,1024]{1,0:T(4,128)(2,1)S(1)}, bf16[4,1024]{1,0:T(4,128)(2,1)S(1)}, u32[]{:S(2)}, u32[]{:S(2)}) collective-permute-start(bf16[4,1024]{1,0:T(4,128)(2,1)S(1)} %last_norm.1.own), channel_id=1, source_target_pairs={{0,13},{1,12},{2,15},{3,14},{4,9},{5,8},{6,11},{7,10},{8,5},{9,4},... | collective-permute-start | bytes 24584 | tf_op jit(solution)/shard_map/ppermute | solution.py:226
  30.2 3.9 %collective-permute-start.14 = (bf16[4,1024]{1,0:T(4,128)(2,1)S(1)}, bf16[4,1024]{1,0:T(4,128)(2,1)S(1)}, u32[]{:S(2)}, u32[]{:S(2)}) collective-permute-start(bf16[4,1024]{1,0:T(4,128)(2,1)S(1)} %last_norm.1.own), channel_id=1, source_target_pairs={{0,9},{1,8},{2,11},{3,10},{4,13},{5,12},{6,15},{7,14},{8,1},{9,0},... | collective-permute-start | bytes 24584 | tf_op jit(solution)/shard_map/ppermute | solution.py:226
  32.7 3.1 %collective-permute-start.13 = (bf16[4,1024]{1,0:T(4,128)(2,1)S(1)}, bf16[4,1024]{1,0:T(4,128)(2,1)S(1)}, u32[]{:S(2)}, u32[]{:S(2)}) collective-permute-start(bf16[4,1024]{1,0:T(4,128)(2,1)S(1)} %last_norm.1.own), channel_id=1, source_target_pairs={{0,5},{1,4},{2,7},{3,6},{4,1},{5,0},{6,3},{7,2},{8,13},{9,12},{10,... | collective-permute-start | bytes 24584 | tf_op jit(solution)/shard_map/ppermute | solution.py:226
  35.9 4.0 %collective-permute-start.16 = (bf16[4,1024]{1,0:T(4,128)(2,1)S(1)}, bf16[4,1024]{1,0:T(4,128)(2,1)S(1)}, u32[]{:S(2)}, u32[]{:S(2)}) collective-permute-start(bf16[4,1024]{1,0:T(4,128)(2,1)S(1)} %get-tuple-element.32), channel_id=1, source_target_pairs={{0,17},{1,16},{2,19},{3,18},{4,21},{5,20},{6,23},{7,22},{8,25},{9,... | collective-permute-start | bytes 24584 | tf_op jit(solution)/shard_map/ppermute | solution.py:226
  (17 other events, 81.3 us)

commit v3 on v2

--- a/solution.py
+++ b/solution.py
@@ -12,6 +12,7 @@
 EPS = 1e-05
 MASKED = -1e30
 SPARE_FLOPS = 10**10
+NORM_1, NORM_2, NORM_3, B_UP, B_CQ, B_QKV, TABLE_ROWS = 0, 3, 6, 9, 10, 11, 16
 f32 = jnp.float32
 bf16 = jnp.bfloat16
 
@@ -47,7 +48,7 @@
     return jnp.where(first, vec[slot : slot + 1], vec[slot + 1 : slot + 2])
 
 
-def attend(query, cache, lens, heads, fresh_key=None, fresh_value=None):
+def attend(query, cache, limits, heads, fresh_key=None, fresh_value=None):
     where = [(ref, s) for ref in cache for s in range(ref.shape[0])]
     slots = len(where)
     _, _, span, width = cache[0].shape
@@ -63,7 +64,8 @@
     for slot in range(0, slots, 2):
         q = jnp.where(own, head_rows(query, slot, heads, first) * scale, 0.0)
         raw = [dot_t(q, ref[at, 0]) for ref, at in where[slot : slot + 2]]
-        length = jnp.where(first_col, lens[slot], lens[slot + 1])
+        length = limits[slot * heads : (slot + 2) * heads]
+        length = jnp.concatenate([length] * (span // LANES), axis=1)
         scores = jnp.where(position < length, jnp.where(first_col, raw[0], raw[1]), MASKED)
         top = jnp.max(scores, axis=-1, keepdims=True)
         if fresh_key is not None:
@@ -107,32 +109,56 @@
                     ] = rows[g : g + part]
 
 
-def wanted(deal, rows, me, far, back):
-    cols = 4 * rows
-    row = lax.broadcasted_iota(jnp.int32, (2 * rows, cols), 0)
-    col = lax.broadcasted_iota(jnp.int32, (2 * rows, cols), 1)
-    take = jnp.where(row < rows, me, me ^ far) * rows + row % rows
-    have = (me ^ (col // rows)) * rows + col % rows
-    if back:
-        for i in range(cols):
-            have = jnp.where(col == i, deal[(me ^ (i // rows)) * rows + i % rows], have)
-    else:
-        for i in range(2 * rows):
-            at = (me if i < rows else me ^ far) * rows + i % rows
-            take = jnp.where(row == i, deal[at], take)
-    return (have == take).astype(bf16)
+def wanted(deal, rows, me, core, back):
+    blocks = len(GATHER[0])
+    shape = (8, blocks * rows)
+    row = lax.broadcasted_iota(jnp.int32, shape, 0)
+    col = lax.broadcasted_iota(jnp.int32, shape, 1)
+    origin = [me ^ jnp.where(core == 0, a, max(b, 0)) for a, b in zip(*GATHER)]
+    used = [(core == 0) | (b >= 0) for b in GATHER[1]]
+    take, have = me * rows + row, jnp.full(shape, -1, jnp.int32)
+    for i in range(blocks * rows):
+        ident = origin[i // rows] * rows + i % rows
+        ident = jnp.where(used[i // rows], deal[ident] if back else ident, -1)
+        have = jnp.where(col == i, ident, have)
+    if not back:
+        for i in range(rows):
+            take = jnp.where(row == i, deal[me * rows + i], take)
+    return ((have == take) & (row < rows)).astype(bf16)
 
 
 def stub_kernel(out_ref):
     out_ref[...] = jnp.zeros_like(out_ref)
 
 
-def plan_kernel(deal, stub, tokens, cache, own_ref, out_ref, back_ref, kv_ref, *, far):
-    me = lax.axis_index("req")
+def spread_lengths(lens, ref, heads):
+    slot = lax.broadcasted_iota(jnp.int32, ref.shape, 0) // heads
+    out = jnp.zeros(ref.shape, jnp.int32)
+    for s in range(ref.shape[0] // heads):
+        out = jnp.where(slot == s, lens[s], out)
+    ref[...] = out
+
+
+def table_kernel(*refs):
+    *vecs, table_ref = refs
+    table_ref[...] = jnp.zeros_like(table_ref)
+    for i, vec in enumerate(vecs):
+        if len(vec.shape) == 1:
+            table_ref[i : i + 1, : vec.shape[0]] = vec[...].astype(f32).reshape(1, vec.shape[0])
+        else:
+            table_ref[i : i + vec.shape[0], : vec.shape[1]] = vec[...].astype(f32)
+
+
+def plan_kernel(deal, self_len, enc_len, stub, tokens, cache, *refs, heads):
+    *vecs, own_ref, out_ref, back_ref, self_ref, enc_ref, kv_ref, table_ref = refs
+    table_kernel(*vecs, table_ref)
+    spread_lengths(self_len, self_ref, heads)
+    spread_lengths(enc_len, enc_ref, heads)
+    me, core = lax.axis_index("req"), lax.axis_index("tp") % 2
     rows = tokens.shape[0]
     own_ref[...] = tokens[...]
-    out_ref[...] = wanted(deal, rows, me, far, False)
-    back_ref[...] = wanted(deal, rows, me, far, True)
+    out_ref[...] = wanted(deal, rows, me, core, False)
+    back_ref[...] = wanted(deal, rows, me, core, True)
     split_cache(cache, kv_ref, 0)
 
 
@@ -140,63 +166,56 @@
     split_cache(cache, kv_ref, start)
 
 
-def sort_kernel(hit, own, g1, g2, g3, mine_ref, theirs_ref):
-    rows = own.shape[0]
-    whole = jnp.concatenate([p[...] for p in (own, g1, g2, g3)], axis=0)
-    out = dot(hit[...], whole)
-    mine_ref[...] = out[:rows].astype(bf16)
-    theirs_ref[...] = out[rows:].astype(bf16)
-
-
-def flat(vec):
-    return vec[...].astype(f32).reshape(1, vec.shape[0])
+def sort_kernel(hit, *refs):
+    *blocks, out_ref = refs
+    whole = jnp.concatenate([p[...] for p in blocks], axis=0)
+    out_ref[...] = dot(hit[...], whole)[: out_ref.shape[0]].astype(bf16)
 
 
 def first_kernel(
-    lens, mine, more, w_qkv, b_qkv, w_out, *refs, heads
+    limits, mine, more, w_qkv, vecs, w_out, *refs, heads
 ):
     *cache, x_ref, part_ref = refs
     slots = x_ref.shape[0]
     x = mine[...].astype(f32) + more[...].astype(f32)
     x_ref[...] = x.astype(bf16)
     x = pad_rows(x, 8).astype(bf16)
-    bias = b_qkv[...].astype(f32)
-    qkv = [round_rows(dot(x, w_qkv[k]) + bias[k : k + 1]) for k in range(3)]
-    length = [lens[s] for s in range(slots)]
-    ctx = attend(qkv[0], cache, length, heads, qkv[1], qkv[2])
-    part_ref[...] = dot(ctx, w_out[...])[:slots]
-
-
-def settle(own, p1, p2, p3, x, bias, gain, beta):
-    total = own[...] + p1[...] + p2[...] + p3[...] + flat(bias) + x[...].astype(f32)
-    return norm_rows(total, flat(gain), flat(beta)).astype(bf16)
-
-
-def second_kernel(
-    lens, own, p1, p2, p3, x, bias, gain, beta, w_cq, b_cq, cache, w_cout, h_ref, part_ref, *, heads
-):
-    slots = own.shape[0]
-    h1 = settle(own, p1, p2, p3, x, bias, gain, beta)
+    width = w_out.shape[0]
+    bias = [vecs[B_QKV + k : B_QKV + k + 1, :width] for k in range(3)]
+    qkv = [round_rows(dot(x, w_qkv[k]) + bias[k]) for k in range(3)]
+    ctx = attend(qkv[0], cache, limits, heads, qkv[1], qkv[2])
+    part_ref[...] = dot(ctx, w_out[...])[:slots].astype(bf16)
+
+
+def settle(parts, x, vecs, at):
+    total = vecs[at : at + 1] + x[...].astype(f32)
+    for part in parts:
+        total = total + part[...].astype(f32)
+    return norm_rows(total, vecs[at + 1 : at + 2], vecs[at + 2 : at + 3]).astype(bf16)
+
+
+def second_kernel(limits, p0, p1, p2, p3, x, vecs, w_cq, cache, w_cout, h_ref, part_ref, *, heads):
+    slots = p0.shape[0]
+    h1 = settle((p0, p1, p2, p3), x, vecs, NORM_1)
     h_ref[...] = h1
-    cq = round_rows(dot(pad_rows(h1.astype(f32), 8), w_cq[...]) + flat(b_cq))
-    length = [lens[s] for s in range(slots)]
-    ctx = attend(cq, [cache], length, heads)
-    part_ref[...] = dot(ctx, w_cout[...])[:slots]
-
-
-def third_kernel(
-    own, p1, p2, p3, x, bias, gain, beta, w_up, b_up, w_down, h_ref, part_ref
-):
-    slots = own.shape[0]
-    h2 = settle(own, p1, p2, p3, x, bias, gain, beta)
+    bias = vecs[B_CQ : B_CQ + 1, : w_cq.shape[1]]
+    cq = round_rows(dot(pad_rows(h1.astype(f32), 8), w_cq[...]) + bias)
+    ctx = attend(cq, [cache], limits, heads)
+    part_ref[...] = dot(ctx, w_cout[...])[:slots].astype(bf16)
+
+
+def third_kernel(p0, p1, p2, p3, x, vecs, w_up, w_down, h_ref, part_ref):
+    slots = p0.shape[0]
+    h2 = settle((p0, p1, p2, p3), x, vecs, NORM_2)
     h_ref[...] = h2
-    hidden = dot(pad_rows(h2.astype(f32), 8), w_up[...]) + flat(b_up)
+    bias = vecs[B_UP : B_UP + 1, : w_up.shape[1]]
+    hidden = dot(pad_rows(h2.astype(f32), 8), w_up[...]) + bias
     act = 0.5 * hidden * (1.0 + lax.erf(hidden * (2.0**-0.5)))
-    part_ref[...] = dot(act, w_down[...])[:slots]
-
-
-def fourth_kernel(own, p1, p2, p3, x, bias, gain, beta, y_ref):
-    y_ref[...] = settle(own, p1, p2, p3, x, bias, gain, beta)
+    part_ref[...] = dot(act, w_down[...])[:slots].astype(bf16)
+
+
+def fourth_kernel(p0, p1, p2, p3, x, vecs, y_ref):
+    y_ref[...] = settle((p0, p1, p2, p3), x, vecs, NORM_3)
 
 
 def add_kernel(mine, more, out_ref):
@@ -230,26 +249,33 @@
     return jnp.dot(onehot.astype(whole.dtype), whole, preferred_element_type=f32).astype(whole.dtype)
 
 
-FAR = 4
-
-
-def near_swaps(value):
-    names, size = ("req", "tp"), lax.axis_size("req") * lax.axis_size("tp")
-    tps = lax.axis_size("tp")
-    return [swap(value, names, size, mask * tps + 1) for mask in (1, 2, 3)]
-
-
-def far_swap(value):
-    names, size = ("req", "tp"), lax.axis_size("req") * lax.axis_size("tp")
-    return swap(value, names, size, FAR * lax.axis_size("tp") + 1)
-
-
-def sort_rows(hit, own, near, name):
-    state = (own.shape, bf16)
-    mine, theirs = call(
-        sort_kernel, [state, state], [hit, own] + near, name=name, cost=SPARE_FLOPS
-    )
-    return mine, far_swap(theirs)
+GATHER = ((0, 1, 3, 6, 7), (-1, -1, 2, 4, 5))
+
+
+def in_order(swaps):
+    return list(lax.optimization_barrier(swaps))
+
+
+def gather_blocks(value, mesh_shape, far_first):
+    reqs, tps = mesh_shape["req"], mesh_shape["tp"]
+    masks = list(zip(*GATHER))[1:]
+    got = []
+    for a, b in masks if far_first else masks[::-1]:
+        b = a if b < 0 else b
+        pairs = []
+        for r in range(reqs):
+            for t in range(tps):
+                pairs.append(((r ^ (b if t % 2 else a)) * tps + (t ^ 1), r * tps + t))
+        got.append(lax.ppermute(value, ("req", "tp"), pairs))
+    got = in_order(got)
+    return got if far_first else got[::-1]
+
+
+def sort_rows(hit, own, got, mesh_shape, name):
+    (mine,) = call(
+        sort_kernel, [(own.shape, bf16)], [hit, own] + got, name=name
+    )
+    return mine, swap(mine, "tp", mesh_shape["tp"], 1)
 
 
 def deal_whole(value, deal, back):
@@ -284,8 +310,8 @@
 def sum_parts(value, mesh_shape):
     tps = mesh_shape["tp"]
     if tps == 4:
-        return [value] + [swap(value, "tp", tps, mask) for mask in (1, 2, 3)]
-    whole = lax.psum(value, "tp")
+        return [value] + in_order([swap(value, "tp", tps, mask) for mask in (1, 2, 3)])
+    whole = lax.psum(value.astype(f32), "tp")
     zero = jnp.zeros_like(whole)
     return [whole, zero, zero, zero]
 
@@ -321,57 +347,64 @@
     width = self_cache.shape[3]
     heads = width // HEAD_DIM
 
-    state, sums = ((rows, model), bf16), ((rows, model), f32)
-    hops = mesh_shape["req"] == 2 * FAR
+    state, sums = ((rows, model), bf16), ((rows, model), bf16)
+    vecs = [b_out, ln1_gain, ln1_bias, b_cout, ln2_gain, ln2_bias, b_down, ln3_gain, ln3_bias]
+    vecs += [b_up, b_cq, b_qkv]
+    table = ((TABLE_ROWS, max(model, b_up.shape[0])), f32)
+    hops = mesh_shape["req"] == 8 and mesh_shape["tp"] == 4
     if hops:
-        near = near_swaps(tokens)
-        hits = ((2 * rows, 4 * rows), bf16)
+        got = gather_blocks(tokens, mesh_shape, False)
+        hits = ((8, len(GATHER[0]) * rows), bf16)
         half = rows // 2
         (stub,) = call(stub_kernel, [((8, LANES), f32)], [], name="stub", cost=SPARE_FLOPS)
-        own, hit_out, hit_back, kv = call(
-            functools.partial(plan_kernel, far=FAR),
-            [state, hits, hits, ((half, 2, self_cache.shape[1], width), bf16)],
-            [deal, stub, tokens, tile_rows(self_cache)],
-            smem=1,
+        limits = ((rows * heads, LANES), jnp.int32)
+        own, hit_out, hit_back, self_limits, enc_limits, kv, vecs = call(
+            functools.partial(plan_kernel, heads=heads),
+            [state, hits, hits, limits, limits, ((half, 2, self_cache.shape[1], width), bf16), table],
+            [deal, self_len, enc_len, stub, tokens, tile_rows(self_cache)] + vecs,
+            smem=3,
             name="plan",
         )
-        mine, more = sort_rows(hit_out, own, near, "sort_out")
+        mine, more = sort_rows(hit_out, own, got, mesh_shape, "sort_out")
         self_kv = [kv] + split_part(mine, self_cache, half, rows - half, "split_self")
     else:
         mine, more = deal_whole(tokens, deal, False)
+        (vecs,) = call(table_kernel, [table], vecs, name="table")
+        self_limits, enc_limits = (
+            jnp.broadcast_to(jnp.repeat(lens, heads)[:, None], (rows * heads, LANES))
+            for lens in (self_len, enc_len)
+        )
         self_kv = split_part(mine, self_cache, 0, rows, "split_self")
     x, part = call(
         functools.partial(first_kernel, heads=heads),
         [state, sums],
-        [self_len, mine, more, w_qkv.transpose(1, 0, 2), b_qkv, w_out] + list(self_kv),
-        smem=1,
+        [self_limits, mine, more, w_qkv.transpose(1, 0, 2), vecs, w_out] + self_kv,
         name="self_attention",
     )
     (cross_kv,) = split_part(x, cross_cache, 0, rows, "split_cross")
     h1, part = call(
         functools.partial(second_kernel, heads=heads),
         [state, sums],
-        [enc_len]
+        [enc_limits]
         + sum_parts(part, mesh_shape)
-        + [x, b_out, ln1_gain, ln1_bias, w_cq, b_cq, cross_kv, w_cout],
-        smem=1,
+        + [x, vecs, w_cq, cross_kv, w_cout],
         name="cross_attention",
     )
     h2, part = call(
         third_kernel,
         [state, sums],
-        sum_parts(part, mesh_shape)
-        + [h1, b_cout, ln2_gain, ln2_bias, w_up, b_up, w_down],
+        sum_parts(part, mesh_shape) + [h1, vecs, w_up, w_down],
         name="feed_forward",
     )
     (y,) = call(
         fourth_kernel,
         [state],
-        sum_parts(part, mesh_shape) + [h2, b_down, ln3_gain, ln3_bias],
+        sum_parts(part, mesh_shape) + [h2, vecs],
         name="last_norm",
     )
     if hops:
-        mine, more = sort_rows(hit_back, y, near_swaps(y), "sort_back")
+        got = gather_blocks(y, mesh_shape, True)
+        mine, more = sort_rows(hit_back, y, got, mesh_shape, "sort_back")
     else:
         mine, more = deal_whole(y, deal, True)
     (result,) = call(add_kernel, [state], [mine, more], name="deal_back")

time: 40.6 us -> 38.5 us (0.948)
  waiting for transfers between devices: 15.2 us -> 11.9 us
  starting transfers between devices: 16.7 us -> 18.9 us
  Pallas kernels: 8.15 us -> 7.13 us
    ppermute x0 -> x8, starting transfers between devices: none -> 12.7 us  [gather_blocks(): got.append(lax.ppermute(value, ('req', 'tp'), pairs))]
    ppermute x17 -> x11, starting transfers between devices: 16.7 us -> 6.24 us  [swap(): return lax.ppermute(value, axis, [(i, i ^ mask) for i in range(size)])]
    ppermute x17 -> x11, waiting for transfers between devices: 15.2 us -> 7.8 us  [swap(): return lax.ppermute(value, axis, [(i, i ^ mask) for i in range(size)])]
    ppermute x0 -> x8, waiting for transfers between devices: none -> 4.07 us  [gather_blocks(): got.append(lax.ppermute(value, ('req', 'tp'), pairs))]
    pallas_call x11, Pallas kernels: 8.15 us -> 7.13 us  [call(): pl.pallas_call(kernel, out_shape=outs, in_specs=specs, out_specs=[vmem] *...]
  transfers between devices with their start and end apart: 17 -> 19, of which waited for: 13 -> 12; matrix products, arithmetic and copies ran while one was open for 0% -> 0% of each run, Pallas kernels for 7% -> 7%
where the time goes in v3:
time: 38.5 us; the launch traced here: 38.3 us
  starting transfers between devices  18.9 us (49%)
  waiting for transfers between devices  11.9 us (31%)
  Pallas kernels  7.13 us (19%)
    ppermute x8, starting transfers between devices, gather_blocks(): got.append(lax.ppermute(value, ('req', 'tp'), pairs))  12.7 us
    ppermute x11, waiting for transfers between devices, swap(): return lax.ppermute(value, axis, [(i, i ^ mask) for i in range(size)])  7.8 us
    pallas_call x11, Pallas kernels, call(): pl.pallas_call(kernel, out_shape=outs, in_specs=specs, out_specs=[vmem] *...  7.13 us
    ppermute x11, starting transfers between devices, swap(): return lax.ppermute(value, axis, [(i, i ^ mask) for i in range(size)])  6.24 us
    ppermute x8, waiting for transfers between devices, gather_blocks(): got.append(lax.ppermute(value, ('req', 'tp'), pairs))  4.07 us
  transfers between devices with their start and end apart: 19, of which 12 were waited for; matrix products, arithmetic and copies ran while one was open for 0% of the time, Pallas kernels for 7%

profile of v3, /device:TPU:0, one launch (start us, length us, event | category | flops | bytes accessed | tf_op | source)
XLA Modules:
  0.0 38.3 jit_solution(2168190003375098679)
XLA Ops:
  0.1 3.5 %collective-permute-start.1 = (bf16[4,1024]{1,0:T(4,128)(2,1)}, bf16[4,1024]{1,0:T(4,128)(2,1)S(1)}, u32[]{:S(2)}, u32[]{:S(2)}) collective-permute-start(bf16[4,1024]{1,0:T(4,128)(2,1)} %tokens.1), channel_id=1, source_target_pairs={{25,0},{16,1},{27,2},{18,3},{29,4},{20,5},{31,6},{22,7},{17,8},{24... | collective-permute-start | bytes 24584 | tf_op jit(solution)/shard_map/ppermute | solution.py:269
  3.7 1.7 %collective-permute-start = (bf16[4,1024]{1,0:T(4,128)(2,1)}, bf16[4,1024]{1,0:T(4,128)(2,1)S(1)}, u32[]{:S(2)}, u32[]{:S(2)}) collective-permute-start(bf16[4,1024]{1,0:T(4,128)(2,1)} %tokens.1), channel_id=1, source_target_pairs={{29,0},{20,1},{31,2},{22,3},{25,4},{16,5},{27,6},{18,7},{21,8},{28... | collective-permute-start | bytes 24584 | tf_op jit(solution)/shard_map/ppermute | solution.py:269
  5.4 1.1 %collective-permute-start.3 = (bf16[4,1024]{1,0:T(4,128)(2,1)}, bf16[4,1024]{1,0:T(4,128)(2,1)S(1)}, u32[]{:S(2)}, u32[]{:S(2)}) collective-permute-start(bf16[4,1024]{1,0:T(4,128)(2,1)} %tokens.1), channel_id=1, source_target_pairs={{5,0},{4,1},{7,2},{6,3},{1,4},{0,5},{3,6},{2,7},{13,8},{12,9},{15,... | collective-permute-start | bytes 24584 | tf_op jit(solution)/shard_map/ppermute | solution.py:269
  6.7 1.3 %plan.1 = (bf16[4,1024]{1,0:T(4,128)(2,1)S(1)}, bf16[8,20]{1,0:T(8,128)(2,1)S(1)}, bf16[8,20]{1,0:T(8,128)(2,1)S(1)}, s32[16,128]{1,0:T(8,128)S(1)}, s32[16,128]...) custom-call(s32[32]{0:T(128)S(1)} %copy-done.20, s32[4]{0:T(128)S(1)} %copy-done.21, ...), custom_call_target="tpu_custom_call" | custom-call | tf_op jit(solution)/shard_map/plan/pallas_call | solution.py:232
  8.0 1.7 %collective-permute-done.refs_4_ = bf16[4,1024]{1,0:T(4,128)(2,1)S(1)} collective-permute-done((bf16[4,1024]{1,0:T(4,128)(2,1)}, bf16[4,1024]{1,0:T(4,128)(2,1)S(1)}, u32[]{:S(2)}, u32[]{:S(2)}) %collective-permute-start) | collective-permute-done | bytes 8224 | tf_op jit(solution)/shard_map/ppermute | solution.py:269
  9.7 1.0 %collective-permute-done.2.refs_2_ = bf16[4,1024]{1,0:T(4,128)(2,1)S(1)} collective-permute-done((bf16[4,1024]{1,0:T(4,128)(2,1)}, bf16[4,1024]{1,0:T(4,128)(2,1)S(1)}, u32[]{:S(2)}, u32[]{:S(2)}) %collective-permute-start.2) | collective-permute-done | bytes 8224 | tf_op jit(solution)/shard_map/ppermute | solution.py:269
  10.9 0.7 %split_self.1.refs_1_ = bf16[2,2,512,256]{3,2,1,0:T(8,128)(2,1)S(1)} custom-call(bf16[4,1024]{1,0:T(4,128)(2,1)S(1)} %sort_out.1.after.mine, bf16[4,2048,128]{2,1,0:T(8,128)(2,1)S(1)} %bitcast.12), custom_call_target="tpu_custom_call" | custom-call | tf_op jit(solution)/shard_map/split_self/pallas_call | solution.py:232
  12.1 1.3 %self_attention.1 = (bf16[4,1024]{1,0:T(4,128)(2,1)S(1)}, bf16[4,1024]{1,0:T(4,128)(2,1)S(1)}) custom-call(s32[16,128]{1,0:T(8,128)S(1)} %get-tuple-element.37.limits, bf16[4,1024]{1,0:T(4,128)(2,1)S(1)} %sort_out.1.after.mine, bf16[4,1024]{1,0:T(4,128)(2,1)S(1)} %collective-permute-done.4.more, bf16[3,1024,256]{2,1,0:T(8,128)(2,1)S(1)} %bitcast.13, ...), custom_call_target="tpu_custom_call" | custom-call | tf_op jit(solution)/shard_map/self_attention/pallas_call | solution.py:232
  13.3 1.3 %collective-permute-start.7 = (bf16[4,1024]{1,0:T(4,128)(2,1)S(1)}, bf16[4,1024]{1,0:T(4,128)(2,1)S(1)}, u32[]{:S(2)}, u32[]{:S(2)}) collective-permute-start(bf16[4,1024]{1,0:T(4,128)(2,1)S(1)} %get-tuple-element.46.p0), channel_id=1, source_target_pairs={{0,3},{1,2},{2,1},{3,0},{4,7},{5,6},{6,5},{7,4},{8,11},{9,10},{10,... | collective-permute-start | bytes 24584 | tf_op jit(solution)/shard_map/ppermute | solution.py:245
  15.2 0.7 %split_cross.1.cache = bf16[4,2,256,256]{3,2,1,0:T(8,128)(2,1)S(1)} custom-call(bf16[4,1024]{1,0:T(4,128)(2,1)S(1)} %get-tuple-element.50.after.x, bf16[4,1024,128]{2,1,0:T(8,128)(2,1)S(1)} %bitcast.14), custom_call_target="tpu_custom_call" | custom-call | tf_op jit(solution)/shard_map/split_cross/pallas_call | solution.py:232
  16.4 1.8 %collective-permute-done.6.p2 = bf16[4,1024]{1,0:T(4,128)(2,1)S(1)} collective-permute-done((bf16[4,1024]{1,0:T(4,128)(2,1)S(1)}, bf16[4,1024]{1,0:T(4,128)(2,1)S(1)}, u32[]{:S(2)}, u32[]{:S(2)}) %collective-permute-start.6) | collective-permute-done | bytes 8224 | tf_op jit(solution)/shard_map/ppermute | solution.py:245
  18.3 1.2 %cross_attention.1 = (bf16[4,1024]{1,0:T(4,128)(2,1)S(1)}, bf16[4,1024]{1,0:T(4,128)(2,1)S(1)}) custom-call(s32[16,128]{1,0:T(8,128)S(1)} %get-tuple-element.36.limits, bf16[4,1024]{1,0:T(4,128)(2,1)S(1)} %get-tuple-element.46.p0, bf16[4,1024]{1,0:T(4,128)(2,1)S(1)} %collective-permute-done.5.p1, bf16[4,1024]{1,0:T(4,128)(2,1)S(1)} %collective-permute-done.6.p2, ...), custom_call_target="tpu_custom_call" | custom-call | tf_op jit(solution)/shard_map/cross_attention/pallas_call | solution.py:232
  19.5 0.8 %collective-permute-start.9 = (bf16[4,1024]{1,0:T(4,128)(2,1)S(1)}, bf16[4,1024]{1,0:T(4,128)(2,1)S(1)}, u32[]{:S(2)}, u32[]{:S(2)}) collective-permute-start(bf16[4,1024]{1,0:T(4,128)(2,1)S(1)} %get-tuple-element.51.p0), channel_id=1, source_target_pairs={{0,2},{1,3},{2,0},{3,1},{4,6},{5,7},{6,4},{7,5},{8,10},{9,11},{10,... | collective-permute-start | bytes 24584 | tf_op jit(solution)/shard_map/ppermute | solution.py:245
  20.4 1.0 %collective-permute-start.8 = (bf16[4,1024]{1,0:T(4,128)(2,1)S(1)}, bf16[4,1024]{1,0:T(4,128)(2,1)S(1)}, u32[]{:S(2)}, u32[]{:S(2)}) collective-permute-start(bf16[4,1024]{1,0:T(4,128)(2,1)S(1)} %get-tuple-element.51.p0), channel_id=1, source_target_pairs={{0,1},{1,0},{2,3},{3,2},{4,5},{5,4},{6,7},{7,6},{8,9},{9,8},{10,11... | collective-permute-start | bytes 24584 | tf_op jit(solution)/shard_map/ppermute | solution.py:245
  21.4 1.2 %collective-permute-done.10.p3 = bf16[4,1024]{1,0:T(4,128)(2,1)S(1)} collective-permute-done((bf16[4,1024]{1,0:T(4,128)(2,1)S(1)}, bf16[4,1024]{1,0:T(4,128)(2,1)S(1)}, u32[]{:S(2)}, u32[]{:S(2)}) %collective-permute-start.10) | collective-permute-done | bytes 8224 | tf_op jit(solution)/shard_map/ppermute | solution.py:245
  23.2 0.8 %feed_forward.1 = (bf16[4,1024]{1,0:T(4,128)(2,1)S(1)}, bf16[4,1024]{1,0:T(4,128)(2,1)S(1)}) custom-call(bf16[4,1024]{1,0:T(4,128)(2,1)S(1)} %get-tuple-element.51.p0, bf16[4,1024]{1,0:T(4,128)(2,1)S(1)} %collective-permute-done.8.p1, bf16[4,1024]{1,0:T(4,128)(2,1)S(1)} %collective-permute-done.9.p2, bf16[4,1024]{1,0:T(4,128)(2,1)S(1)} %collective-permute-done.10.p3, ...), custom_call_target="tpu_custom_call" | custom-call | tf_op jit(solution)/shard_map/feed_forward/pallas_call | solution.py:232
  25.2 0.7 %collective-permute-start.11 = (bf16[4,1024]{1,0:T(4,128)(2,1)S(1)}, bf16[4,1024]{1,0:T(4,128)(2,1)S(1)}, u32[]{:S(2)}, u32[]{:S(2)}) collective-permute-start(bf16[4,1024]{1,0:T(4,128)(2,1)S(1)} %get-tuple-element.56.p0), channel_id=1, source_target_pairs={{0,1},{1,0},{2,3},{3,2},{4,5},{5,4},{6,7},{7,6},{8,9},{9,8},{10,11... | collective-permute-start | bytes 24584 | tf_op jit(solution)/shard_map/ppermute | solution.py:245
  25.9 1.2 %collective-permute-done.13.p3 = bf16[4,1024]{1,0:T(4,128)(2,1)S(1)} collective-permute-done((bf16[4,1024]{1,0:T(4,128)(2,1)S(1)}, bf16[4,1024]{1,0:T(4,128)(2,1)S(1)}, u32[]{:S(2)}, u32[]{:S(2)}) %collective-permute-start.13) | collective-permute-done | bytes 8224 | tf_op jit(solution)/shard_map/ppermute | solution.py:245
  27.2 1.1 %collective-permute-done.12.p2 = bf16[4,1024]{1,0:T(4,128)(2,1)S(1)} collective-permute-done((bf16[4,1024]{1,0:T(4,128)(2,1)S(1)}, bf16[4,1024]{1,0:T(4,128)(2,1)S(1)}, u32[]{:S(2)}, u32[]{:S(2)}) %collective-permute-start.12) | collective-permute-done | bytes 8224 | tf_op jit(solution)/shard_map/ppermute | solution.py:245
  28.5 1.5 %collective-permute-start.17 = (bf16[4,1024]{1,0:T(4,128)(2,1)S(1)}, bf16[4,1024]{1,0:T(4,128)(2,1)S(1)}, u32[]{:S(2)}, u32[]{:S(2)}) collective-permute-start(bf16[4,1024]{1,0:T(4,128)(2,1)S(1)} %last_norm.1.refs_0_), channel_id=1, source_target_pairs={{29,0},{20,1},{31,2},{22,3},{25,4},{16,5},{27,6},{18,7},{21,8},{28... | collective-permute-start | bytes 24584 | tf_op jit(solution)/shard_map/ppermute | solution.py:269
  30.4 1.2 %collective-permute-start.15 = (bf16[4,1024]{1,0:T(4,128)(2,1)S(1)}, bf16[4,1024]{1,0:T(4,128)(2,1)S(1)}, u32[]{:S(2)}, u32[]{:S(2)}) collective-permute-start(bf16[4,1024]{1,0:T(4,128)(2,1)S(1)} %last_norm.1.refs_0_), channel_id=1, source_target_pairs={{13,0},{8,1},{15,2},{10,3},{9,4},{12,5},{11,6},{14,7},{5,8},{0,9},... | collective-permute-start | bytes 24584 | tf_op jit(solution)/shard_map/ppermute | solution.py:269
  31.7 3.1 %collective-permute-start.14 = (bf16[4,1024]{1,0:T(4,128)(2,1)S(1)}, bf16[4,1024]{1,0:T(4,128)(2,1)S(1)}, u32[]{:S(2)}, u32[]{:S(2)}) collective-permute-start(bf16[4,1024]{1,0:T(4,128)(2,1)S(1)} %last_norm.1.refs_0_), channel_id=1, source_target_pairs={{5,0},{4,1},{7,2},{6,3},{1,4},{0,5},{3,6},{2,7},{13,8},{12,9},{15,... | collective-permute-start | bytes 24584 | tf_op jit(solution)/shard_map/ppermute | solution.py:269
  34.9 1.3 %collective-permute-done.14.refs_1_ = bf16[4,1024]{1,0:T(4,128)(2,1)S(1)} collective-permute-done((bf16[4,1024]{1,0:T(4,128)(2,1)S(1)}, bf16[4,1024]{1,0:T(4,128)(2,1)S(1)}, u32[]{:S(2)}, u32[]{:S(2)}) %collective-permute-start.14) | collective-permute-done | bytes 8224 | tf_op jit(solution)/shard_map/ppermute | solution.py:269
  36.9 0.8 %collective-permute-done.18.more = bf16[4,1024]{1,0:T(4,128)(2,1)S(1)} collective-permute-done((bf16[4,1024]{1,0:T(4,128)(2,1)S(1)}, bf16[4,1024]{1,0:T(4,128)(2,1)S(1)}, u32[]{:S(2)}, u32[]{:S(2)}) %collective-permute-start.18) | collective-permute-done | bytes 8224 | tf_op jit(solution)/shard_map/ppermute | solution.py:245
  (73 shorter events, 5.6 us)
Async XLA Ops:
  0.0 6.5 %copy-start.14 = (bf16[1024]{0:T(1024)(128)(2,1)S(1)}, bf16[1024]{0:T(1024)(128)(2,1)}, u32[]{:S(2)}) copy-start(bf16[1024]{0:T(1024)(128)(2,1)} %refs_5_.1) | copy-start | bytes 6148
  0.0 6.5 %copy-start.13 = (bf16[1024]{0:T(1024)(128)(2,1)S(1)}, bf16[1024]{0:T(1024)(128)(2,1)}, u32[]{:S(2)}) copy-start(bf16[1024]{0:T(1024)(128)(2,1)} %refs_4_.1) | copy-start | bytes 6148
  0.0 6.5 %copy-start.12 = (bf16[1024]{0:T(1024)(128)(2,1)S(1)}, bf16[1024]{0:T(1024)(128)(2,1)}, u32[]{:S(2)}) copy-start(bf16[1024]{0:T(1024)(128)(2,1)} %refs_3_.1) | copy-start | bytes 6148
  0.1 7.9 %collective-permute-start.1 = (bf16[4,1024]{1,0:T(4,128)(2,1)}, bf16[4,1024]{1,0:T(4,128)(2,1)S(1)}, u32[]{:S(2)}, u32[]{:S(2)}) collective-permute-start(bf16[4,1024]{1,0:T(4,128)(2,1)} %tokens.1), channel_id=1, source_target_pairs={{25,0},{16,1},{27,2},{18,3},{29,4},{20,5},{31,6},{22,7},{17,8},{24... | collective-permute-start | bytes 24584 | tf_op jit(solution)/shard_map/ppermute | solution.py:269
  3.7 6.0 %collective-permute-start = (bf16[4,1024]{1,0:T(4,128)(2,1)}, bf16[4,1024]{1,0:T(4,128)(2,1)S(1)}, u32[]{:S(2)}, u32[]{:S(2)}) collective-permute-start(bf16[4,1024]{1,0:T(4,128)(2,1)} %tokens.1), channel_id=1, source_target_pairs={{29,0},{20,1},{31,2},{22,3},{25,4},{16,5},{27,6},{18,7},{21,8},{28... | collective-permute-start | bytes 24584 | tf_op jit(solution)/shard_map/ppermute | solution.py:269
  5.4 4.3 %collective-permute-start.3 = (bf16[4,1024]{1,0:T(4,128)(2,1)}, bf16[4,1024]{1,0:T(4,128)(2,1)S(1)}, u32[]{:S(2)}, u32[]{:S(2)}) collective-permute-start(bf16[4,1024]{1,0:T(4,128)(2,1)} %tokens.1), channel_id=1, source_target_pairs={{5,0},{4,1},{7,2},{6,3},{1,4},{0,5},{3,6},{2,7},{13,8},{12,9},{15,... | collective-permute-start | bytes 24584 | tf_op jit(solution)/shard_map/ppermute | solution.py:269
  6.5 4.2 %collective-permute-start.2 = (bf16[4,1024]{1,0:T(4,128)(2,1)}, bf16[4,1024]{1,0:T(4,128)(2,1)S(1)}, u32[]{:S(2)}, u32[]{:S(2)}) collective-permute-start(bf16[4,1024]{1,0:T(4,128)(2,1)} %tokens.1), channel_id=1, source_target_pairs={{13,0},{8,1},{15,2},{10,3},{9,4},{12,5},{11,6},{14,7},{5,8},{0,9},... | collective-permute-start | bytes 24584 | tf_op jit(solution)/shard_map/ppermute | solution.py:269
  10.9 1.2 %collective-permute-start.4 = (bf16[4,1024]{1,0:T(4,128)(2,1)S(1)}, bf16[4,1024]{1,0:T(4,128)(2,1)S(1)}, u32[]{:S(2)}, u32[]{:S(2)}) collective-permute-start(bf16[4,1024]{1,0:T(4,128)(2,1)S(1)} %sort_out.1.after.mine), channel_id=1, source_target_pairs={{0,1},{1,0},{2,3},{3,2},{4,5},{5,4},{6,7},{7,6},{8,9},{9,8},{10,11... | collective-permute-start | bytes 24584 | tf_op jit(solution)/shard_map/ppermute | solution.py:245
  13.3 3.1 %collective-permute-start.7 = (bf16[4,1024]{1,0:T(4,128)(2,1)S(1)}, bf16[4,1024]{1,0:T(4,128)(2,1)S(1)}, u32[]{:S(2)}, u32[]{:S(2)}) collective-permute-start(bf16[4,1024]{1,0:T(4,128)(2,1)S(1)} %get-tuple-element.46.p0), channel_id=1, source_target_pairs={{0,3},{1,2},{2,1},{3,0},{4,7},{5,6},{6,5},{7,4},{8,11},{9,10},{10,... | collective-permute-start | bytes 24584 | tf_op jit(solution)/shard_map/ppermute | solution.py:245
  14.6 3.7 %collective-permute-start.6 = (bf16[4,1024]{1,0:T(4,128)(2,1)S(1)}, bf16[4,1024]{1,0:T(4,128)(2,1)S(1)}, u32[]{:S(2)}, u32[]{:S(2)}) collective-permute-start(bf16[4,1024]{1,0:T(4,128)(2,1)S(1)} %get-tuple-element.46.p0), channel_id=1, source_target_pairs={{0,2},{1,3},{2,0},{3,1},{4,6},{5,7},{6,4},{7,5},{8,10},{9,11},{10,... | collective-permute-start | bytes 24584 | tf_op jit(solution)/shard_map/ppermute | solution.py:245
  15.2 3.1 %collective-permute-start.5 = (bf16[4,1024]{1,0:T(4,128)(2,1)S(1)}, bf16[4,1024]{1,0:T(4,128)(2,1)S(1)}, u32[]{:S(2)}, u32[]{:S(2)}) collective-permute-start(bf16[4,1024]{1,0:T(4,128)(2,1)S(1)} %get-tuple-element.46.p0), channel_id=1, source_target_pairs={{0,1},{1,0},{2,3},{3,2},{4,5},{5,4},{6,7},{7,6},{8,9},{9,8},{10,11... | collective-permute-start | bytes 24584 | tf_op jit(solution)/shard_map/ppermute | solution.py:245
  15.2 8.0 %copy-start.1 = (bf16[1024,1024]{1,0:T(8,128)(2,1)S(1)}, bf16[1024,1024]{1,0:T(8,128)(2,1)}, u32[]{:S(2)}) copy-start(bf16[1024,1024]{1,0:T(8,128)(2,1)} %w_up.1) | copy-start | bytes 6291460
  15.2 8.0 %copy-start.2 = (bf16[1024,1024]{1,0:T(8,128)(2,1)S(1)}, bf16[1024,1024]{1,0:T(8,128)(2,1)}, u32[]{:S(2)}) copy-start(bf16[1024,1024]{1,0:T(8,128)(2,1)} %w_down.1) | copy-start | bytes 6291460
  19.5 3.1 %collective-permute-start.10 = (bf16[4,1024]{1,0:T(4,128)(2,1)S(1)}, bf16[4,1024]{1,0:T(4,128)(2,1)S(1)}, u32[]{:S(2)}, u32[]{:S(2)}) collective-permute-start(bf16[4,1024]{1,0:T(4,128)(2,1)S(1)} %get-tuple-element.51.p0), channel_id=1, source_target_pairs={{0,3},{1,2},{2,1},{3,0},{4,7},{5,6},{6,5},{7,4},{8,11},{9,10},{10,... | collective-permute-start | bytes 24584 | tf_op jit(solution)/shard_map/ppermute | solution.py:245
  19.5 3.7 %collective-permute-start.9 = (bf16[4,1024]{1,0:T(4,128)(2,1)S(1)}, bf16[4,1024]{1,0:T(4,128)(2,1)S(1)}, u32[]{:S(2)}, u32[]{:S(2)}) collective-permute-start(bf16[4,1024]{1,0:T(4,128)(2,1)S(1)} %get-tuple-element.51.p0), channel_id=1, source_target_pairs={{0,2},{1,3},{2,0},{3,1},{4,6},{5,7},{6,4},{7,5},{8,10},{9,11},{10,... | collective-permute-start | bytes 24584 | tf_op jit(solution)/shard_map/ppermute | solution.py:245
  20.4 2.9 %collective-permute-start.8 = (bf16[4,1024]{1,0:T(4,128)(2,1)S(1)}, bf16[4,1024]{1,0:T(4,128)(2,1)S(1)}, u32[]{:S(2)}, u32[]{:S(2)}) collective-permute-start(bf16[4,1024]{1,0:T(4,128)(2,1)S(1)} %get-tuple-element.51.p0), channel_id=1, source_target_pairs={{0,1},{1,0},{2,3},{3,2},{4,5},{5,4},{6,7},{7,6},{8,9},{9,8},{10,11... | collective-permute-start | bytes 24584 | tf_op jit(solution)/shard_map/ppermute | solution.py:245
  24.1 3.1 %collective-permute-start.13 = (bf16[4,1024]{1,0:T(4,128)(2,1)S(1)}, bf16[4,1024]{1,0:T(4,128)(2,1)S(1)}, u32[]{:S(2)}, u32[]{:S(2)}) collective-permute-start(bf16[4,1024]{1,0:T(4,128)(2,1)S(1)} %get-tuple-element.56.p0), channel_id=1, source_target_pairs={{0,3},{1,2},{2,1},{3,0},{4,7},{5,6},{6,5},{7,4},{8,11},{9,10},{10,... | collective-permute-start | bytes 24584 | tf_op jit(solution)/shard_map/ppermute | solution.py:245
  24.6 3.7 %collective-permute-start.12 = (bf16[4,1024]{1,0:T(4,128)(2,1)S(1)}, bf16[4,1024]{1,0:T(4,128)(2,1)S(1)}, u32[]{:S(2)}, u32[]{:S(2)}) collective-permute-start(bf16[4,1024]{1,0:T(4,128)(2,1)S(1)} %get-tuple-element.56.p0), channel_id=1, source_target_pairs={{0,2},{1,3},{2,0},{3,1},{4,6},{5,7},{6,4},{7,5},{8,10},{9,11},{10,... | collective-permute-start | bytes 24584 | tf_op jit(solution)/shard_map/ppermute | solution.py:245
  25.2 3.1 %collective-permute-start.11 = (bf16[4,1024]{1,0:T(4,128)(2,1)S(1)}, bf16[4,1024]{1,0:T(4,128)(2,1)S(1)}, u32[]{:S(2)}, u32[]{:S(2)}) collective-permute-start(bf16[4,1024]{1,0:T(4,128)(2,1)S(1)} %get-tuple-element.56.p0), channel_id=1, source_target_pairs={{0,1},{1,0},{2,3},{3,2},{4,5},{5,4},{6,7},{7,6},{8,9},{9,8},{10,11... | collective-permute-start | bytes 24584 | tf_op jit(solution)/shard_map/ppermute | solution.py:245
  28.5 6.3 %collective-permute-start.17 = (bf16[4,1024]{1,0:T(4,128)(2,1)S(1)}, bf16[4,1024]{1,0:T(4,128)(2,1)S(1)}, u32[]{:S(2)}, u32[]{:S(2)}) collective-permute-start(bf16[4,1024]{1,0:T(4,128)(2,1)S(1)} %last_norm.1.refs_0_), channel_id=1, source_target_pairs={{29,0},{20,1},{31,2},{22,3},{25,4},{16,5},{27,6},{18,7},{21,8},{28... | collective-permute-start | bytes 24584 | tf_op jit(solution)/shard_map/ppermute | solution.py:269
  30.0 4.9 %collective-permute-start.16 = (bf16[4,1024]{1,0:T(4,128)(2,1)S(1)}, bf16[4,1024]{1,0:T(4,128)(2,1)S(1)}, u32[]{:S(2)}, u32[]{:S(2)}) collective-permute-start(bf16[4,1024]{1,0:T(4,128)(2,1)S(1)} %last_norm.1.refs_0_), channel_id=1, source_target_pairs={{25,0},{16,1},{27,2},{18,3},{29,4},{20,5},{31,6},{22,7},{17,8},{24... | collective-permute-start | bytes 24584 | tf_op jit(solution)/shard_map/ppermute | solution.py:269
  30.4 4.5 %collective-permute-start.15 = (bf16[4,1024]{1,0:T(4,128)(2,1)S(1)}, bf16[4,1024]{1,0:T(4,128)(2,1)S(1)}, u32[]{:S(2)}, u32[]{:S(2)}) collective-permute-start(bf16[4,1024]{1,0:T(4,128)(2,1)S(1)} %last_norm.1.refs_0_), channel_id=1, source_target_pairs={{13,0},{8,1},{15,2},{10,3},{9,4},{12,5},{11,6},{14,7},{5,8},{0,9},... | collective-permute-start | bytes 24584 | tf_op jit(solution)/shard_map/ppermute | solution.py:269
  31.7 4.5 %collective-permute-start.14 = (bf16[4,1024]{1,0:T(4,128)(2,1)S(1)}, bf16[4,1024]{1,0:T(4,128)(2,1)S(1)}, u32[]{:S(2)}, u32[]{:S(2)}) collective-permute-start(bf16[4,1024]{1,0:T(4,128)(2,1)S(1)} %last_norm.1.refs_0_), channel_id=1, source_target_pairs={{5,0},{4,1},{7,2},{6,3},{1,4},{0,5},{3,6},{2,7},{13,8},{12,9},{15,... | collective-permute-start | bytes 24584 | tf_op jit(solution)/shard_map/ppermute | solution.py:269
  36.3 1.4 %collective-permute-start.18 = (bf16[4,1024]{1,0:T(4,128)(2,1)S(1)}, bf16[4,1024]{1,0:T(4,128)(2,1)S(1)}, u32[]{:S(2)}, u32[]{:S(2)}) collective-permute-start(bf16[4,1024]{1,0:T(4,128)(2,1)S(1)} %sort_back.1.mine), channel_id=1, source_target_pairs={{0,1},{1,0},{2,3},{3,2},{4,5},{5,4},{6,7},{7,6},{8,9},{9,8},{10,11... | collective-permute-start | bytes 24584 | tf_op jit(solution)/shard_map/ppermute | solution.py:245
  (19 other events, 115.1 us)

commit v4 on v3

--- a/solution.py
+++ b/solution.py
@@ -12,6 +12,9 @@
 EPS = 1e-05
 MASKED = -1e30
 SPARE_FLOPS = 10**10
+OUT_STEPS = ((7, 5, 1), (6, 4, 1), (1, 1, 1), (2, 3, 1))
+BACK_STEPS = ((1, 1, 1), (2, 3, 1), (6, 4, 1), (5, 7, 1))
+TP_STEPS = (1, 2, 3)
 NORM_1, NORM_2, NORM_3, B_UP, B_CQ, B_QKV, TABLE_ROWS = 0, 3, 6, 9, 10, 11, 16
 f32 = jnp.float32
 bf16 = jnp.bfloat16
@@ -32,12 +35,6 @@
     return jnp.dot(a.astype(bf16), b, preferred_element_type=f32)
 
 
-def dot_t(a, b):
-    return lax.dot_general(
-        a.astype(bf16), b, (((1,), (1,)), ((), ())), preferred_element_type=f32
-    )
-
-
 def pad_rows(value, rows):
     return jnp.concatenate(
         [value, jnp.zeros((rows - value.shape[0], value.shape[1]), value.dtype)], axis=0
@@ -49,9 +46,9 @@
 
 
 def attend(query, cache, limits, heads, fresh_key=None, fresh_value=None):
-    where = [(ref, s) for ref in cache for s in range(ref.shape[0])]
+    where = [(k.at[s], v.at[s]) for k, v in cache for s in range(k.shape[0])]
     slots = len(where)
-    _, _, span, width = cache[0].shape
+    _, span, width = cache[0][1].shape
     pair = 2 * heads
     scale = HEAD_DIM ** (-0.5)
     row = lax.broadcasted_iota(jnp.int32, (pair, width), 0)
@@ -63,7 +60,7 @@
     rows = []
     for slot in range(0, slots, 2):
         q = jnp.where(own, head_rows(query, slot, heads, first) * scale, 0.0)
-        raw = [dot_t(q, ref[at, 0]) for ref, at in where[slot : slot + 2]]
+        raw = [dot(q, keys[...]) for keys, _ in where[slot : slot + 2]]
         length = limits[slot * heads : (slot + 2) * heads]
         length = jnp.concatenate([length] * (span // LANES), axis=1)
         scores = jnp.where(position < length, jnp.where(first_col, raw[0], raw[1]), MASKED)
@@ -78,7 +75,7 @@
         if fresh_key is not None:
             expn = jnp.exp(fresh - top)
             total = total + expn
-        out = [dot(expo, ref[at, 1]) for ref, at in where[slot : slot + 2]]
+        out = [dot(expo, values[...]) for _, values in where[slot : slot + 2]]
         ctx = jnp.where(first, out[0], out[1])
         if fresh_key is not None:
             ctx = ctx + round_rows(expn) * v_new
@@ -88,36 +85,46 @@
     return jnp.concatenate(rows + [jnp.zeros((8 - slots, width), f32)], axis=0)
 
 
-def split_cache(cache, out_ref, start):
-    slots = out_ref.shape[0]
+def split_cache(cache, key_ref, value_ref, start):
+    slots, _, width = value_ref.shape
     count = cache.shape[1]
-    tiles = out_ref.shape[3] // LANES
+    tiles = width // LANES
     group = 2 * tiles
     step = 256
     part = step // group
     r = lax.broadcasted_iota(jnp.int32, (step, step), 0)
     c = lax.broadcasted_iota(jnp.int32, (step, step), 1)
     order = (c == (r % part) * group + r // part).astype(bf16)
+    pieces = LANES // part
     for slot in range(slots):
-        for at in range(count // step):
-            rows = dot(order, cache[start + slot, at * step : (at + 1) * step]).astype(bf16)
+        for at in range(0, count // step, pieces):
+            rows = [
+                dot(order, cache[start + slot, (at + i) * step : (at + i + 1) * step])
+                for i in range(pieces)
+            ]
+            here = slice(at * part, (at + pieces) * part)
             for tile in range(tiles):
-                for kind in range(2):
-                    g = (tile * 2 + kind) * part
-                    out_ref[
-                        slot, kind, at * part : (at + 1) * part, tile * LANES : (tile + 1) * LANES
-                    ] = rows[g : g + part]
-
-
-def wanted(deal, rows, me, core, back):
-    blocks = len(GATHER[0])
-    shape = (8, blocks * rows)
+                lanes = slice(tile * LANES, (tile + 1) * LANES)
+                g = 2 * tile * part
+                key = jnp.concatenate([x[g : g + part] for x in rows], axis=0)
+                value = jnp.concatenate([x[g + part : g + 2 * part] for x in rows], axis=0)
+                key_ref[slot, lanes, here] = key.T.astype(bf16)
+                value_ref[slot, here, lanes] = value.astype(bf16)
+
+
+def wanted(deal, rows, me, core, steps, back):
+    masks, seen = [(0, 0, 0)] + list(steps), set()
+    origin, used = [], []
+    for a, b, _ in masks:
+        origin.append(me ^ jnp.where(core == 0, a, b))
+        fresh = (a not in seen, b not in seen | {a})
+        seen |= {a, b}
+        used.append(jnp.where(core == 0, fresh[0], fresh[1]))
+    shape = (8, len(masks) * rows)
     row = lax.broadcasted_iota(jnp.int32, shape, 0)
     col = lax.broadcasted_iota(jnp.int32, shape, 1)
-    origin = [me ^ jnp.where(core == 0, a, max(b, 0)) for a, b in zip(*GATHER)]
-    used = [(core == 0) | (b >= 0) for b in GATHER[1]]
     take, have = me * rows + row, jnp.full(shape, -1, jnp.int32)
-    for i in range(blocks * rows):
+    for i in range(shape[1]):
         ident = origin[i // rows] * rows + i % rows
         ident = jnp.where(used[i // rows], deal[ident] if back else ident, -1)
         have = jnp.where(col == i, ident, have)
@@ -150,20 +157,20 @@
 
 
 def plan_kernel(deal, self_len, enc_len, stub, tokens, cache, *refs, heads):
-    *vecs, own_ref, out_ref, back_ref, self_ref, enc_ref, kv_ref, table_ref = refs
+    *vecs, own_ref, out_ref, back_ref, self_ref, enc_ref, key_ref, value_ref, table_ref = refs
     table_kernel(*vecs, table_ref)
     spread_lengths(self_len, self_ref, heads)
     spread_lengths(enc_len, enc_ref, heads)
     me, core = lax.axis_index("req"), lax.axis_index("tp") % 2
     rows = tokens.shape[0]
     own_ref[...] = tokens[...]
-    out_ref[...] = wanted(deal, rows, me, core, False)
-    back_ref[...] = wanted(deal, rows, me, core, True)
-    split_cache(cache, kv_ref, 0)
-
-
-def split_kernel(after, cache, kv_ref, *, start):
-    split_cache(cache, kv_ref, start)
+    out_ref[...] = wanted(deal, rows, me, core, OUT_STEPS, False)
+    back_ref[...] = wanted(deal, rows, me, core, BACK_STEPS, True)
+    split_cache(cache, key_ref, value_ref, 0)
+
+
+def split_kernel(after, cache, key_ref, value_ref, *, start):
+    split_cache(cache, key_ref, value_ref, start)
 
 
 def sort_kernel(hit, *refs):
@@ -176,6 +183,7 @@
     limits, mine, more, w_qkv, vecs, w_out, *refs, heads
 ):
     *cache, x_ref, part_ref = refs
+    cache = list(zip(cache[::2], cache[1::2]))
     slots = x_ref.shape[0]
     x = mine[...].astype(f32) + more[...].astype(f32)
     x_ref[...] = x.astype(bf16)
@@ -194,13 +202,15 @@
     return norm_rows(total, vecs[at + 1 : at + 2], vecs[at + 2 : at + 3]).astype(bf16)
 
 
-def second_kernel(limits, p0, p1, p2, p3, x, vecs, w_cq, cache, w_cout, h_ref, part_ref, *, heads):
+def second_kernel(
+    limits, p0, p1, p2, p3, x, vecs, w_cq, keys, values, w_cout, h_ref, part_ref, *, heads
+):
     slots = p0.shape[0]
     h1 = settle((p0, p1, p2, p3), x, vecs, NORM_1)
     h_ref[...] = h1
     bias = vecs[B_CQ : B_CQ + 1, : w_cq.shape[1]]
     cq = round_rows(dot(pad_rows(h1.astype(f32), 8), w_cq[...]) + bias)
-    ctx = attend(cq, [cache], limits, heads)
+    ctx = attend(cq, [(keys, values)], limits, heads)
     part_ref[...] = dot(ctx, w_cout[...])[:slots].astype(bf16)
 
 
@@ -249,26 +259,20 @@
     return jnp.dot(onehot.astype(whole.dtype), whole, preferred_element_type=f32).astype(whole.dtype)
 
 
-GATHER = ((0, 1, 3, 6, 7), (-1, -1, 2, 4, 5))
-
-
 def in_order(swaps):
     return list(lax.optimization_barrier(swaps))
 
 
-def gather_blocks(value, mesh_shape, far_first):
+def gather_blocks(value, mesh_shape, steps):
     reqs, tps = mesh_shape["req"], mesh_shape["tp"]
-    masks = list(zip(*GATHER))[1:]
     got = []
-    for a, b in masks if far_first else masks[::-1]:
-        b = a if b < 0 else b
+    for a, b, cross in steps:
         pairs = []
         for r in range(reqs):
             for t in range(tps):
-                pairs.append(((r ^ (b if t % 2 else a)) * tps + (t ^ 1), r * tps + t))
+                pairs.append(((r ^ (b if t % 2 else a)) * tps + (t ^ cross), r * tps + t))
         got.append(lax.ppermute(value, ("req", "tp"), pairs))
-    got = in_order(got)
-    return got if far_first else got[::-1]
+    return in_order(got)
 
 
 def sort_rows(hit, own, got, mesh_shape, name):
@@ -291,11 +295,15 @@
     return picked, jnp.zeros_like(picked)
 
 
+def split_shapes(cache, slots):
+    _, span, _, width = cache.shape
+    return [((slots, width, span), bf16), ((slots, span, width), bf16)]
+
+
 def split_part(after, cache, start, slots, name):
-    _, span, _, width = cache.shape
     return call(
         functools.partial(split_kernel, start=start),
-        [((slots, 2, span, width), bf16)],
+        split_shapes(cache, slots),
         [after, tile_rows(cache)],
         name=name,
     )
@@ -310,7 +318,7 @@
 def sum_parts(value, mesh_shape):
     tps = mesh_shape["tp"]
     if tps == 4:
-        return [value] + in_order([swap(value, "tp", tps, mask) for mask in (1, 2, 3)])
+        return [value] + in_order([swap(value, "tp", tps, mask) for mask in TP_STEPS])
     whole = lax.psum(value.astype(f32), "tp")
     zero = jnp.zeros_like(whole)
     return [whole, zero, zero, zero]
@@ -353,20 +361,20 @@
     table = ((TABLE_ROWS, max(model, b_up.shape[0])), f32)
     hops = mesh_shape["req"] == 8 and mesh_shape["tp"] == 4
     if hops:
-        got = gather_blocks(tokens, mesh_shape, False)
-        hits = ((8, len(GATHER[0]) * rows), bf16)
+        got = gather_blocks(tokens, mesh_shape, OUT_STEPS)
+        hits = [((8, (1 + len(steps)) * rows), bf16) for steps in (OUT_STEPS, BACK_STEPS)]
         half = rows // 2
         (stub,) = call(stub_kernel, [((8, LANES), f32)], [], name="stub", cost=SPARE_FLOPS)
         limits = ((rows * heads, LANES), jnp.int32)
-        own, hit_out, hit_back, self_limits, enc_limits, kv, vecs = call(
+        own, hit_out, hit_back, self_limits, enc_limits, keys, values, vecs = call(
             functools.partial(plan_kernel, heads=heads),
-            [state, hits, hits, limits, limits, ((half, 2, self_cache.shape[1], width), bf16), table],
+            [state] + hits + [limits, limits] + split_shapes(self_cache, half) + [table],
             [deal, self_len, enc_len, stub, tokens, tile_rows(self_cache)] + vecs,
             smem=3,
             name="plan",
         )
         mine, more = sort_rows(hit_out, own, got, mesh_shape, "sort_out")
-        self_kv = [kv] + split_part(mine, self_cache, half, rows - half, "split_self")
+        self_kv = [keys, values] + split_part(mine, self_cache, half, rows - half, "split_self")
     else:
         mine, more = deal_whole(tokens, deal, False)
         (vecs,) = call(table_kernel, [table], vecs, name="table")
@@ -381,13 +389,13 @@
         [self_limits, mine, more, w_qkv.transpose(1, 0, 2), vecs, w_out] + self_kv,
         name="self_attention",
     )
-    (cross_kv,) = split_part(x, cross_cache, 0, rows, "split_cross")
+    cross_kv = split_part(x, cross_cache, 0, rows, "split_cross")
     h1, part = call(
         functools.partial(second_kernel, heads=heads),
         [state, sums],
         [enc_limits]
         + sum_parts(part, mesh_shape)
-        + [x, vecs, w_cq, cross_kv, w_cout],
+        + [x, vecs, w_cq] + cross_kv + [w_cout],
         name="cross_attention",
     )
     h2, part = call(
@@ -403,7 +411,7 @@
         name="last_norm",
     )
     if hops:
-        got = gather_blocks(y, mesh_shape, True)
+        got = gather_blocks(y, mesh_shape, BACK_STEPS)
         mine, more = sort_rows(hit_back, y, got, mesh_shape, "sort_back")
     else:
         mine, more = deal_whole(y, deal, True)

time: 38.5 us -> 37.6 us (0.977)
  starting transfers between devices: 18.9 us -> 18 us
    ppermute x8, starting transfers between devices: 12.7 us -> 11.1 us  [gather_blocks(): got.append(lax.ppermute(value, ('req', 'tp'), pairs))]
    ppermute x11, starting transfers between devices: 6.24 us -> 6.89 us  [swap(): return lax.ppermute(value, axis, [(i, i ^ mask) for i in range(size)])]
  transfers between devices with their start and end apart: 19 -> 19, of which waited for: 12 -> 12; matrix products, arithmetic and copies ran while one was open for 0% -> 0% of each run, Pallas kernels for 7% -> 8%
where the time goes in v4:
time: 37.6 us; the launch traced here: 37.5 us
  starting transfers between devices  18 us (48%)
  waiting for transfers between devices  11.9 us (32%)
  Pallas kernels  7.19 us (19%)
    ppermute x8, starting transfers between devices, gather_blocks(): got.append(lax.ppermute(value, ('req', 'tp'), pairs))  11.1 us
    ppermute x11, waiting for transfers between devices, swap(): return lax.ppermute(value, axis, [(i, i ^ mask) for i in range(size)])  7.53 us
    pallas_call x11, Pallas kernels, call(): pl.pallas_call(kernel, out_shape=outs, in_specs=specs, out_specs=[vmem] *...  7.19 us
    ppermute x11, starting transfers between devices, swap(): return lax.ppermute(value, axis, [(i, i ^ mask) for i in range(size)])  6.89 us
    ppermute x8, waiting for transfers between devices, gather_blocks(): got.append(lax.ppermute(value, ('req', 'tp'), pairs))  4.37 us
  transfers between devices with their start and end apart: 19, of which 12 were waited for; matrix products, arithmetic and copies ran while one was open for 0% of the time, Pallas kernels for 8%

profile of v4, /device:TPU:0, one launch (start us, length us, event | category | flops | bytes accessed | tf_op | source)
XLA Modules:
  0.0 37.5 jit_solution(14932451041942716888)
XLA Ops:
  0.1 3.5 %collective-permute-start.1 = (bf16[4,1024]{1,0:T(4,128)(2,1)}, bf16[4,1024]{1,0:T(4,128)(2,1)S(1)}, u32[]{:S(2)}, u32[]{:S(2)}) collective-permute-start(bf16[4,1024]{1,0:T(4,128)(2,1)} %tokens.1), channel_id=1, source_target_pairs={{25,0},{16,1},{27,2},{18,3},{29,4},{20,5},{31,6},{22,7},{17,8},{24... | collective-permute-start | bytes 24584 | tf_op jit(solution)/shard_map/ppermute | solution.py:274
  3.7 1.7 %collective-permute-start = (bf16[4,1024]{1,0:T(4,128)(2,1)}, bf16[4,1024]{1,0:T(4,128)(2,1)S(1)}, u32[]{:S(2)}, u32[]{:S(2)}) collective-permute-start(bf16[4,1024]{1,0:T(4,128)(2,1)} %tokens.1), channel_id=1, source_target_pairs={{29,0},{20,1},{31,2},{22,3},{25,4},{16,5},{27,6},{18,7},{21,8},{28... | collective-permute-start | bytes 24584 | tf_op jit(solution)/shard_map/ppermute | solution.py:274
  5.5 1.0 %collective-permute-start.2 = (bf16[4,1024]{1,0:T(4,128)(2,1)}, bf16[4,1024]{1,0:T(4,128)(2,1)S(1)}, u32[]{:S(2)}, u32[]{:S(2)}) collective-permute-start(bf16[4,1024]{1,0:T(4,128)(2,1)} %tokens.1), channel_id=1, source_target_pairs={{5,0},{4,1},{7,2},{6,3},{1,4},{0,5},{3,6},{2,7},{13,8},{12,9},{15,... | collective-permute-start | bytes 24584 | tf_op jit(solution)/shard_map/ppermute | solution.py:274
  6.7 1.4 %plan.1 = (bf16[4,1024]{1,0:T(4,128)(2,1)S(1)}, bf16[8,20]{1,0:T(8,128)(2,1)S(1)}, bf16[8,20]{1,0:T(8,128)(2,1)S(1)}, s32[16,128]{1,0:T(8,128)S(1)}, s32[16,128]...) custom-call(s32[32]{0:T(128)S(1)} %copy-done.20, ...), custom_call_target="tpu_custom_call" | custom-call | tf_op jit(solution)/shard_map/plan/pallas_call | solution.py:242
  8.1 1.6 %collective-permute-done.refs_1_ = bf16[4,1024]{1,0:T(4,128)(2,1)S(1)} collective-permute-done((bf16[4,1024]{1,0:T(4,128)(2,1)}, bf16[4,1024]{1,0:T(4,128)(2,1)S(1)}, u32[]{:S(2)}, u32[]{:S(2)}) %collective-permute-start) | collective-permute-done | bytes 8224 | tf_op jit(solution)/shard_map/ppermute | solution.py:274
  9.8 0.9 %collective-permute-start.4 = (bf16[4,1024]{1,0:T(4,128)(2,1)S(1)}, bf16[4,1024]{1,0:T(4,128)(2,1)S(1)}, u32[]{:S(2)}, u32[]{:S(2)}) collective-permute-start(bf16[4,1024]{1,0:T(4,128)(2,1)S(1)} %sort_out.1.after.mine), channel_id=1, source_target_pairs={{0,1},{1,0},{2,3},{3,2},{4,5},{5,4},{6,7},{7,6},{8,9},{9,8},{10,11... | collective-permute-start | bytes 24584 | tf_op jit(solution)/shard_map/ppermute | solution.py:255
  10.7 0.8 %split_self.1 = (bf16[2,256,512]{2,1,0:T(8,128)(2,1)S(1)}, bf16[2,512,256]{2,1,0:T(8,128)(2,1)S(1)}) custom-call(bf16[4,1024]{1,0:T(4,128)(2,1)S(1)} %sort_out.1.after.mine, bf16[4,2048,128]{2,1,0:T(8,128)(2,1)S(1)} %bitcast.12), custom_call_target="tpu_custom_call" | custom-call | tf_op jit(solution)/shard_map/split_self/pallas_call | solution.py:242
  11.6 1.2 %self_attention.1 = (bf16[4,1024]{1,0:T(4,128)(2,1)S(1)}, bf16[4,1024]{1,0:T(4,128)(2,1)S(1)}) custom-call(s32[16,128]{1,0:T(8,128)S(1)} %get-tuple-element.42.limits, bf16[4,1024]{1,0:T(4,128)(2,1)S(1)} %sort_out.1.after.mine, bf16[4,1024]{1,0:T(4,128)(2,1)S(1)} %collective-permute-done.4.more, bf16[3,1024,256]{2,1,0:T(8,128)(2,1)S(1)} %bitcast.13, ...), custom_call_target="tpu_custom_call" | custom-call | tf_op jit(solution)/shard_map/self_attention/pallas_call | solution.py:242
  12.8 1.5 %collective-permute-start.7 = (bf16[4,1024]{1,0:T(4,128)(2,1)S(1)}, bf16[4,1024]{1,0:T(4,128)(2,1)S(1)}, u32[]{:S(2)}, u32[]{:S(2)}) collective-permute-start(bf16[4,1024]{1,0:T(4,128)(2,1)S(1)} %get-tuple-element.54.p0), channel_id=1, source_target_pairs={{0,3},{1,2},{2,1},{3,0},{4,7},{5,6},{6,5},{7,4},{8,11},{9,10},{10,... | collective-permute-start | bytes 24584 | tf_op jit(solution)/shard_map/ppermute | solution.py:255
  14.8 0.8 %split_cross.1 = (bf16[4,256,256]{2,1,0:T(8,128)(2,1)S(1)}, bf16[4,256,256]{2,1,0:T(8,128)(2,1)S(1)}) custom-call(bf16[4,1024]{1,0:T(4,128)(2,1)S(1)} %get-tuple-element.58.after.x, bf16[4,1024,128]{2,1,0:T(8,128)(2,1)S(1)} %bitcast.14), custom_call_target="tpu_custom_call" | custom-call | tf_op jit(solution)/shard_map/split_cross/pallas_call | solution.py:242
  15.9 2.0 %collective-permute-done.6.p2 = bf16[4,1024]{1,0:T(4,128)(2,1)S(1)} collective-permute-done((bf16[4,1024]{1,0:T(4,128)(2,1)S(1)}, bf16[4,1024]{1,0:T(4,128)(2,1)S(1)}, u32[]{:S(2)}, u32[]{:S(2)}) %collective-permute-start.6) | collective-permute-done | bytes 8224 | tf_op jit(solution)/shard_map/ppermute | solution.py:255
  17.9 1.2 %cross_attention.1 = (bf16[4,1024]{1,0:T(4,128)(2,1)S(1)}, bf16[4,1024]{1,0:T(4,128)(2,1)S(1)}) custom-call(s32[16,128]{1,0:T(8,128)S(1)} %get-tuple-element.41.limits, bf16[4,1024]{1,0:T(4,128)(2,1)S(1)} %get-tuple-element.54.p0, bf16[4,1024]{1,0:T(4,128)(2,1)S(1)} %collective-permute-done.5.p1, bf16[4,1024]{1,0:T(4,128)(2,1)S(1)} %collective-permute-done.6.p2, ...), custom_call_target="tpu_custom_call" | custom-call | tf_op jit(solution)/shard_map/cross_attention/pallas_call | solution.py:242
  19.8 1.2 %collective-permute-start.8 = (bf16[4,1024]{1,0:T(4,128)(2,1)S(1)}, bf16[4,1024]{1,0:T(4,128)(2,1)S(1)}, u32[]{:S(2)}, u32[]{:S(2)}) collective-permute-start(bf16[4,1024]{1,0:T(4,128)(2,1)S(1)} %get-tuple-element.61.p0), channel_id=1, source_target_pairs={{0,1},{1,0},{2,3},{3,2},{4,5},{5,4},{6,7},{7,6},{8,9},{9,8},{10,11... | collective-permute-start | bytes 24584 | tf_op jit(solution)/shard_map/ppermute | solution.py:255
  21.0 1.2 %collective-permute-done.10.p3 = bf16[4,1024]{1,0:T(4,128)(2,1)S(1)} collective-permute-done((bf16[4,1024]{1,0:T(4,128)(2,1)S(1)}, bf16[4,1024]{1,0:T(4,128)(2,1)S(1)}, u32[]{:S(2)}, u32[]{:S(2)}) %collective-permute-start.10) | collective-permute-done | bytes 8224 | tf_op jit(solution)/shard_map/ppermute | solution.py:255
  22.8 0.8 %feed_forward.1 = (bf16[4,1024]{1,0:T(4,128)(2,1)S(1)}, bf16[4,1024]{1,0:T(4,128)(2,1)S(1)}) custom-call(bf16[4,1024]{1,0:T(4,128)(2,1)S(1)} %get-tuple-element.61.p0, bf16[4,1024]{1,0:T(4,128)(2,1)S(1)} %collective-permute-done.8.p1, bf16[4,1024]{1,0:T(4,128)(2,1)S(1)} %collective-permute-done.9.p2, bf16[4,1024]{1,0:T(4,128)(2,1)S(1)} %collective-permute-done.10.p3, ...), custom_call_target="tpu_custom_call" | custom-call | tf_op jit(solution)/shard_map/feed_forward/pallas_call | solution.py:242
  24.8 0.7 %collective-permute-start.11 = (bf16[4,1024]{1,0:T(4,128)(2,1)S(1)}, bf16[4,1024]{1,0:T(4,128)(2,1)S(1)}, u32[]{:S(2)}, u32[]{:S(2)}) collective-permute-start(bf16[4,1024]{1,0:T(4,128)(2,1)S(1)} %get-tuple-element.66.p0), channel_id=1, source_target_pairs={{0,1},{1,0},{2,3},{3,2},{4,5},{5,4},{6,7},{7,6},{8,9},{9,8},{10,11... | collective-permute-start | bytes 24584 | tf_op jit(solution)/shard_map/ppermute | solution.py:255
  25.5 1.2 %collective-permute-done.13.p3 = bf16[4,1024]{1,0:T(4,128)(2,1)S(1)} collective-permute-done((bf16[4,1024]{1,0:T(4,128)(2,1)S(1)}, bf16[4,1024]{1,0:T(4,128)(2,1)S(1)}, u32[]{:S(2)}, u32[]{:S(2)}) %collective-permute-start.13) | collective-permute-done | bytes 8224 | tf_op jit(solution)/shard_map/ppermute | solution.py:255
  26.8 1.1 %collective-permute-done.12.p2 = bf16[4,1024]{1,0:T(4,128)(2,1)S(1)} collective-permute-done((bf16[4,1024]{1,0:T(4,128)(2,1)S(1)}, bf16[4,1024]{1,0:T(4,128)(2,1)S(1)}, u32[]{:S(2)}, u32[]{:S(2)}) %collective-permute-start.12) | collective-permute-done | bytes 8224 | tf_op jit(solution)/shard_map/ppermute | solution.py:255
  28.1 1.8 %collective-permute-start.17 = (bf16[4,1024]{1,0:T(4,128)(2,1)S(1)}, bf16[4,1024]{1,0:T(4,128)(2,1)S(1)}, u32[]{:S(2)}, u32[]{:S(2)}) collective-permute-start(bf16[4,1024]{1,0:T(4,128)(2,1)S(1)} %last_norm.1.refs_0_), channel_id=1, source_target_pairs={{21,0},{28,1},{23,2},{30,3},{17,4},{24,5},{19,6},{26,7},{29,8},{20... | collective-permute-start | bytes 24584 | tf_op jit(solution)/shard_map/ppermute | solution.py:274
  29.9 1.8 %collective-permute-start.16 = (bf16[4,1024]{1,0:T(4,128)(2,1)S(1)}, bf16[4,1024]{1,0:T(4,128)(2,1)S(1)}, u32[]{:S(2)}, u32[]{:S(2)}) collective-permute-start(bf16[4,1024]{1,0:T(4,128)(2,1)S(1)} %last_norm.1.refs_0_), channel_id=1, source_target_pairs={{25,0},{16,1},{27,2},{18,3},{29,4},{20,5},{31,6},{22,7},{17,8},{24... | collective-permute-start | bytes 24584 | tf_op jit(solution)/shard_map/ppermute | solution.py:274
  31.6 0.8 %collective-permute-start.15 = (bf16[4,1024]{1,0:T(4,128)(2,1)S(1)}, bf16[4,1024]{1,0:T(4,128)(2,1)S(1)}, u32[]{:S(2)}, u32[]{:S(2)}) collective-permute-start(bf16[4,1024]{1,0:T(4,128)(2,1)S(1)} %last_norm.1.refs_0_), channel_id=1, source_target_pairs={{9,0},{12,1},{11,2},{14,3},{13,4},{8,5},{15,6},{10,7},{1,8},{4,9},... | collective-permute-start | bytes 24584 | tf_op jit(solution)/shard_map/ppermute | solution.py:274
  33.0 1.8 %collective-permute-done.16.refs_3_ = bf16[4,1024]{1,0:T(4,128)(2,1)S(1)} collective-permute-done((bf16[4,1024]{1,0:T(4,128)(2,1)S(1)}, bf16[4,1024]{1,0:T(4,128)(2,1)S(1)}, u32[]{:S(2)}, u32[]{:S(2)}) %collective-permute-start.16) | collective-permute-done | bytes 8224 | tf_op jit(solution)/shard_map/ppermute | solution.py:274
  34.8 0.8 %collective-permute-done.14.refs_1_ = bf16[4,1024]{1,0:T(4,128)(2,1)S(1)} collective-permute-done((bf16[4,1024]{1,0:T(4,128)(2,1)S(1)}, bf16[4,1024]{1,0:T(4,128)(2,1)S(1)}, u32[]{:S(2)}, u32[]{:S(2)}) %collective-permute-start.14) | collective-permute-done | bytes 8224 | tf_op jit(solution)/shard_map/ppermute | solution.py:274
  35.9 0.9 %collective-permute-done.18.more = bf16[4,1024]{1,0:T(4,128)(2,1)S(1)} collective-permute-done((bf16[4,1024]{1,0:T(4,128)(2,1)S(1)}, bf16[4,1024]{1,0:T(4,128)(2,1)S(1)}, u32[]{:S(2)}, u32[]{:S(2)}) %collective-permute-start.18) | collective-permute-done | bytes 8224 | tf_op jit(solution)/shard_map/ppermute | solution.py:255
  (73 shorter events, 5.4 us)
Async XLA Ops:
  0.0 6.5 %copy-start.14 = (bf16[1024]{0:T(1024)(128)(2,1)S(1)}, bf16[1024]{0:T(1024)(128)(2,1)}, u32[]{:S(2)}) copy-start(bf16[1024]{0:T(1024)(128)(2,1)} %refs_5_.1) | copy-start | bytes 6148
  0.0 6.5 %copy-start.13 = (bf16[1024]{0:T(1024)(128)(2,1)S(1)}, bf16[1024]{0:T(1024)(128)(2,1)}, u32[]{:S(2)}) copy-start(bf16[1024]{0:T(1024)(128)(2,1)} %refs_4_.1) | copy-start | bytes 6148
  0.0 6.5 %copy-start.12 = (bf16[1024]{0:T(1024)(128)(2,1)S(1)}, bf16[1024]{0:T(1024)(128)(2,1)}, u32[]{:S(2)}) copy-start(bf16[1024]{0:T(1024)(128)(2,1)} %refs_3_.1) | copy-start | bytes 6148
  0.1 7.9 %collective-permute-start.1 = (bf16[4,1024]{1,0:T(4,128)(2,1)}, bf16[4,1024]{1,0:T(4,128)(2,1)S(1)}, u32[]{:S(2)}, u32[]{:S(2)}) collective-permute-start(bf16[4,1024]{1,0:T(4,128)(2,1)} %tokens.1), channel_id=1, source_target_pairs={{25,0},{16,1},{27,2},{18,3},{29,4},{20,5},{31,6},{22,7},{17,8},{24... | collective-permute-start | bytes 24584 | tf_op jit(solution)/shard_map/ppermute | solution.py:274
  3.7 6.0 %collective-permute-start = (bf16[4,1024]{1,0:T(4,128)(2,1)}, bf16[4,1024]{1,0:T(4,128)(2,1)S(1)}, u32[]{:S(2)}, u32[]{:S(2)}) collective-permute-start(bf16[4,1024]{1,0:T(4,128)(2,1)} %tokens.1), channel_id=1, source_target_pairs={{29,0},{20,1},{31,2},{22,3},{25,4},{16,5},{27,6},{18,7},{21,8},{28... | collective-permute-start | bytes 24584 | tf_op jit(solution)/shard_map/ppermute | solution.py:274
  5.4 4.3 %collective-permute-start.3 = (bf16[4,1024]{1,0:T(4,128)(2,1)}, bf16[4,1024]{1,0:T(4,128)(2,1)S(1)}, u32[]{:S(2)}, u32[]{:S(2)}) collective-permute-start(bf16[4,1024]{1,0:T(4,128)(2,1)} %tokens.1), channel_id=1, source_target_pairs={{9,0},{12,1},{11,2},{14,3},{13,4},{8,5},{15,6},{10,7},{1,8},{4,9},... | collective-permute-start | bytes 24584 | tf_op jit(solution)/shard_map/ppermute | solution.py:274
  5.5 4.2 %collective-permute-start.2 = (bf16[4,1024]{1,0:T(4,128)(2,1)}, bf16[4,1024]{1,0:T(4,128)(2,1)S(1)}, u32[]{:S(2)}, u32[]{:S(2)}) collective-permute-start(bf16[4,1024]{1,0:T(4,128)(2,1)} %tokens.1), channel_id=1, source_target_pairs={{5,0},{4,1},{7,2},{6,3},{1,4},{0,5},{3,6},{2,7},{13,8},{12,9},{15,... | collective-permute-start | bytes 24584 | tf_op jit(solution)/shard_map/ppermute | solution.py:274
  9.8 1.7 %collective-permute-start.4 = (bf16[4,1024]{1,0:T(4,128)(2,1)S(1)}, bf16[4,1024]{1,0:T(4,128)(2,1)S(1)}, u32[]{:S(2)}, u32[]{:S(2)}) collective-permute-start(bf16[4,1024]{1,0:T(4,128)(2,1)S(1)} %sort_out.1.after.mine), channel_id=1, source_target_pairs={{0,1},{1,0},{2,3},{3,2},{4,5},{5,4},{6,7},{7,6},{8,9},{9,8},{10,11... | collective-permute-start | bytes 24584 | tf_op jit(solution)/shard_map/ppermute | solution.py:255
  11.6 11.2 %copy-start.2 = (bf16[1024,1024]{1,0:T(8,128)(2,1)S(1)}, bf16[1024,1024]{1,0:T(8,128)(2,1)}, u32[]{:S(2)}) copy-start(bf16[1024,1024]{1,0:T(8,128)(2,1)} %w_down.1) | copy-start | bytes 6291460
  12.8 10.1 %copy-start.1 = (bf16[1024,1024]{1,0:T(8,128)(2,1)S(1)}, bf16[1024,1024]{1,0:T(8,128)(2,1)}, u32[]{:S(2)}) copy-start(bf16[1024,1024]{1,0:T(8,128)(2,1)} %w_up.1) | copy-start | bytes 6291460
  12.8 3.1 %collective-permute-start.7 = (bf16[4,1024]{1,0:T(4,128)(2,1)S(1)}, bf16[4,1024]{1,0:T(4,128)(2,1)S(1)}, u32[]{:S(2)}, u32[]{:S(2)}) collective-permute-start(bf16[4,1024]{1,0:T(4,128)(2,1)S(1)} %get-tuple-element.54.p0), channel_id=1, source_target_pairs={{0,3},{1,2},{2,1},{3,0},{4,7},{5,6},{6,5},{7,4},{8,11},{9,10},{10,... | collective-permute-start | bytes 24584 | tf_op jit(solution)/shard_map/ppermute | solution.py:255
  14.2 3.7 %collective-permute-start.6 = (bf16[4,1024]{1,0:T(4,128)(2,1)S(1)}, bf16[4,1024]{1,0:T(4,128)(2,1)S(1)}, u32[]{:S(2)}, u32[]{:S(2)}) collective-permute-start(bf16[4,1024]{1,0:T(4,128)(2,1)S(1)} %get-tuple-element.54.p0), channel_id=1, source_target_pairs={{0,2},{1,3},{2,0},{3,1},{4,6},{5,7},{6,4},{7,5},{8,10},{9,11},{10,... | collective-permute-start | bytes 24584 | tf_op jit(solution)/shard_map/ppermute | solution.py:255
  14.8 3.1 %collective-permute-start.5 = (bf16[4,1024]{1,0:T(4,128)(2,1)S(1)}, bf16[4,1024]{1,0:T(4,128)(2,1)S(1)}, u32[]{:S(2)}, u32[]{:S(2)}) collective-permute-start(bf16[4,1024]{1,0:T(4,128)(2,1)S(1)} %get-tuple-element.54.p0), channel_id=1, source_target_pairs={{0,1},{1,0},{2,3},{3,2},{4,5},{5,4},{6,7},{7,6},{8,9},{9,8},{10,11... | collective-permute-start | bytes 24584 | tf_op jit(solution)/shard_map/ppermute | solution.py:255
  19.1 3.1 %collective-permute-start.10 = (bf16[4,1024]{1,0:T(4,128)(2,1)S(1)}, bf16[4,1024]{1,0:T(4,128)(2,1)S(1)}, u32[]{:S(2)}, u32[]{:S(2)}) collective-permute-start(bf16[4,1024]{1,0:T(4,128)(2,1)S(1)} %get-tuple-element.61.p0), channel_id=1, source_target_pairs={{0,3},{1,2},{2,1},{3,0},{4,7},{5,6},{6,5},{7,4},{8,11},{9,10},{10,... | collective-permute-start | bytes 24584 | tf_op jit(solution)/shard_map/ppermute | solution.py:255
  19.1 3.7 %collective-permute-start.9 = (bf16[4,1024]{1,0:T(4,128)(2,1)S(1)}, bf16[4,1024]{1,0:T(4,128)(2,1)S(1)}, u32[]{:S(2)}, u32[]{:S(2)}) collective-permute-start(bf16[4,1024]{1,0:T(4,128)(2,1)S(1)} %get-tuple-element.61.p0), channel_id=1, source_target_pairs={{0,2},{1,3},{2,0},{3,1},{4,6},{5,7},{6,4},{7,5},{8,10},{9,11},{10,... | collective-permute-start | bytes 24584 | tf_op jit(solution)/shard_map/ppermute | solution.py:255
  19.8 3.0 %collective-permute-start.8 = (bf16[4,1024]{1,0:T(4,128)(2,1)S(1)}, bf16[4,1024]{1,0:T(4,128)(2,1)S(1)}, u32[]{:S(2)}, u32[]{:S(2)}) collective-permute-start(bf16[4,1024]{1,0:T(4,128)(2,1)S(1)} %get-tuple-element.61.p0), channel_id=1, source_target_pairs={{0,1},{1,0},{2,3},{3,2},{4,5},{5,4},{6,7},{7,6},{8,9},{9,8},{10,11... | collective-permute-start | bytes 24584 | tf_op jit(solution)/shard_map/ppermute | solution.py:255
  23.7 3.1 %collective-permute-start.13 = (bf16[4,1024]{1,0:T(4,128)(2,1)S(1)}, bf16[4,1024]{1,0:T(4,128)(2,1)S(1)}, u32[]{:S(2)}, u32[]{:S(2)}) collective-permute-start(bf16[4,1024]{1,0:T(4,128)(2,1)S(1)} %get-tuple-element.66.p0), channel_id=1, source_target_pairs={{0,3},{1,2},{2,1},{3,0},{4,7},{5,6},{6,5},{7,4},{8,11},{9,10},{10,... | collective-permute-start | bytes 24584 | tf_op jit(solution)/shard_map/ppermute | solution.py:255
  24.2 3.7 %collective-permute-start.12 = (bf16[4,1024]{1,0:T(4,128)(2,1)S(1)}, bf16[4,1024]{1,0:T(4,128)(2,1)S(1)}, u32[]{:S(2)}, u32[]{:S(2)}) collective-permute-start(bf16[4,1024]{1,0:T(4,128)(2,1)S(1)} %get-tuple-element.66.p0), channel_id=1, source_target_pairs={{0,2},{1,3},{2,0},{3,1},{4,6},{5,7},{6,4},{7,5},{8,10},{9,11},{10,... | collective-permute-start | bytes 24584 | tf_op jit(solution)/shard_map/ppermute | solution.py:255
  24.8 3.1 %collective-permute-start.11 = (bf16[4,1024]{1,0:T(4,128)(2,1)S(1)}, bf16[4,1024]{1,0:T(4,128)(2,1)S(1)}, u32[]{:S(2)}, u32[]{:S(2)}) collective-permute-start(bf16[4,1024]{1,0:T(4,128)(2,1)S(1)} %get-tuple-element.66.p0), channel_id=1, source_target_pairs={{0,1},{1,0},{2,3},{3,2},{4,5},{5,4},{6,7},{7,6},{8,9},{9,8},{10,11... | collective-permute-start | bytes 24584 | tf_op jit(solution)/shard_map/ppermute | solution.py:255
  28.1 4.9 %collective-permute-start.17 = (bf16[4,1024]{1,0:T(4,128)(2,1)S(1)}, bf16[4,1024]{1,0:T(4,128)(2,1)S(1)}, u32[]{:S(2)}, u32[]{:S(2)}) collective-permute-start(bf16[4,1024]{1,0:T(4,128)(2,1)S(1)} %last_norm.1.refs_0_), channel_id=1, source_target_pairs={{21,0},{28,1},{23,2},{30,3},{17,4},{24,5},{19,6},{26,7},{29,8},{20... | collective-permute-start | bytes 24584 | tf_op jit(solution)/shard_map/ppermute | solution.py:274
  29.9 4.9 %collective-permute-start.16 = (bf16[4,1024]{1,0:T(4,128)(2,1)S(1)}, bf16[4,1024]{1,0:T(4,128)(2,1)S(1)}, u32[]{:S(2)}, u32[]{:S(2)}) collective-permute-start(bf16[4,1024]{1,0:T(4,128)(2,1)S(1)} %last_norm.1.refs_0_), channel_id=1, source_target_pairs={{25,0},{16,1},{27,2},{18,3},{29,4},{20,5},{31,6},{22,7},{17,8},{24... | collective-permute-start | bytes 24584 | tf_op jit(solution)/shard_map/ppermute | solution.py:274
  31.6 3.2 %collective-permute-start.15 = (bf16[4,1024]{1,0:T(4,128)(2,1)S(1)}, bf16[4,1024]{1,0:T(4,128)(2,1)S(1)}, u32[]{:S(2)}, u32[]{:S(2)}) collective-permute-start(bf16[4,1024]{1,0:T(4,128)(2,1)S(1)} %last_norm.1.refs_0_), channel_id=1, source_target_pairs={{9,0},{12,1},{11,2},{14,3},{13,4},{8,5},{15,6},{10,7},{1,8},{4,9},... | collective-permute-start | bytes 24584 | tf_op jit(solution)/shard_map/ppermute | solution.py:274
  32.5 3.1 %collective-permute-start.14 = (bf16[4,1024]{1,0:T(4,128)(2,1)S(1)}, bf16[4,1024]{1,0:T(4,128)(2,1)S(1)}, u32[]{:S(2)}, u32[]{:S(2)}) collective-permute-start(bf16[4,1024]{1,0:T(4,128)(2,1)S(1)} %last_norm.1.refs_0_), channel_id=1, source_target_pairs={{5,0},{4,1},{7,2},{6,3},{1,4},{0,5},{3,6},{2,7},{13,8},{12,9},{15,... | collective-permute-start | bytes 24584 | tf_op jit(solution)/shard_map/ppermute | solution.py:274
  35.7 1.2 %collective-permute-start.18 = (bf16[4,1024]{1,0:T(4,128)(2,1)S(1)}, bf16[4,1024]{1,0:T(4,128)(2,1)S(1)}, u32[]{:S(2)}, u32[]{:S(2)}) collective-permute-start(bf16[4,1024]{1,0:T(4,128)(2,1)S(1)} %sort_back.1.mine), channel_id=1, source_target_pairs={{0,1},{1,0},{2,3},{3,2},{4,5},{5,4},{6,7},{7,6},{8,9},{9,8},{10,11... | collective-permute-start | bytes 24584 | tf_op jit(solution)/shard_map/ppermute | solution.py:255
  (19 other events, 117.0 us)

commit v5 on v4

--- a/solution.py
+++ b/solution.py
@@ -85,7 +85,7 @@
     return jnp.concatenate(rows + [jnp.zeros((8 - slots, width), f32)], axis=0)
 
 
-def split_cache(cache, key_ref, value_ref, start):
+def split_cache(cache, key_ref, value_ref, start, lens=None):
     slots, _, width = value_ref.shape
     count = cache.shape[1]
     tiles = width // LANES
@@ -96,8 +96,9 @@
     c = lax.broadcasted_iota(jnp.int32, (step, step), 1)
     order = (c == (r % part) * group + r // part).astype(bf16)
     pieces = LANES // part
-    for slot in range(slots):
-        for at in range(0, count // step, pieces):
+
+    def move(slot, steps):
+        for at in steps:
             rows = [
                 dot(order, cache[start + slot, (at + i) * step : (at + i + 1) * step])
                 for i in range(pieces)
@@ -110,6 +111,24 @@
                 value = jnp.concatenate([x[g + part : g + 2 * part] for x in rows], axis=0)
                 key_ref[slot, lanes, here] = key.T.astype(bf16)
                 value_ref[slot, here, lanes] = value.astype(bf16)
+
+    steps = list(range(0, count // step, pieces))
+    if lens is None:
+        for slot in range(slots):
+            move(slot, steps)
+        return
+    low = len(steps) // 2
+    cut = steps[low] * part
+    span = value_ref.shape[1]
+    for slot in range(slots):
+        move(slot, steps[:low])
+        key_ref[slot, :, cut:] = jnp.zeros((width, span - cut), bf16)
+        value_ref[slot, cut:] = jnp.zeros((span - cut, width), bf16)
+    for slot in range(slots):
+
+        @pl.when(lens[slot] > cut)
+        def _():
+            move(slot, steps[low:])
 
 
 def wanted(deal, rows, me, core, steps, back):
@@ -166,7 +185,7 @@
     own_ref[...] = tokens[...]
     out_ref[...] = wanted(deal, rows, me, core, OUT_STEPS, False)
     back_ref[...] = wanted(deal, rows, me, core, BACK_STEPS, True)
-    split_cache(cache, key_ref, value_ref, 0)
+    split_cache(cache, key_ref, value_ref, 0, self_len)
 
 
 def split_kernel(after, cache, key_ref, value_ref, *, start):
@@ -363,7 +382,7 @@
     if hops:
         got = gather_blocks(tokens, mesh_shape, OUT_STEPS)
         hits = [((8, (1 + len(steps)) * rows), bf16) for steps in (OUT_STEPS, BACK_STEPS)]
-        half = rows // 2
+        half = rows - 1
         (stub,) = call(stub_kernel, [((8, LANES), f32)], [], name="stub", cost=SPARE_FLOPS)
         limits = ((rows * heads, LANES), jnp.int32)
         own, hit_out, hit_back, self_limits, enc_limits, keys, values, vecs = call(

time: 37.6 us -> 37.6 us (level)
  transfers between devices with their start and end apart: 19 -> 19, of which waited for: 12 -> 12; matrix products, arithmetic and copies ran while one was open for 0% -> 0% of each run, Pallas kernels for 8% -> 7%
where the time goes in v5:
time: 37.6 us; the launch traced here: 37.5 us
  starting transfers between devices  18 us (48%)
  waiting for transfers between devices  12.2 us (32%)
  Pallas kernels  6.85 us (18%)
    ppermute x8, starting transfers between devices, gather_blocks(): got.append(lax.ppermute(value, ('req', 'tp'), pairs))  11.1 us
    ppermute x11, waiting for transfers between devices, swap(): return lax.ppermute(value, axis, [(i, i ^ mask) for i in range(size)])  7.8 us
    ppermute x11, starting transfers between devices, swap(): return lax.ppermute(value, axis, [(i, i ^ mask) for i in range(size)])  6.89 us
    pallas_call x11, Pallas kernels, call(): pl.pallas_call(kernel, out_shape=outs, in_specs=specs, out_specs=[vmem] *...  6.85 us
    ppermute x8, waiting for transfers between devices, gather_blocks(): got.append(lax.ppermute(value, ('req', 'tp'), pairs))  4.43 us
  transfers between devices with their start and end apart: 19, of which 12 were waited for; matrix products, arithmetic and copies ran while one was open for 0% of the time, Pallas kernels for 7%

profile of v5, /device:TPU:0, one launch (start us, length us, event | category | flops | bytes accessed | tf_op | source)
XLA Modules:
  0.0 37.5 jit_solution(1589227874593094770)
XLA Ops:
  0.1 3.5 %collective-permute-start.1 = (bf16[4,1024]{1,0:T(4,128)(2,1)}, bf16[4,1024]{1,0:T(4,128)(2,1)S(1)}, u32[]{:S(2)}, u32[]{:S(2)}) collective-permute-start(bf16[4,1024]{1,0:T(4,128)(2,1)} %tokens.1), channel_id=1, source_target_pairs={{25,0},{16,1},{27,2},{18,3},{29,4},{20,5},{31,6},{22,7},{17,8},{24... | collective-permute-start | bytes 24584 | tf_op jit(solution)/shard_map/ppermute | solution.py:293
  3.7 1.7 %collective-permute-start = (bf16[4,1024]{1,0:T(4,128)(2,1)}, bf16[4,1024]{1,0:T(4,128)(2,1)S(1)}, u32[]{:S(2)}, u32[]{:S(2)}) collective-permute-start(bf16[4,1024]{1,0:T(4,128)(2,1)} %tokens.1), channel_id=1, source_target_pairs={{29,0},{20,1},{31,2},{22,3},{25,4},{16,5},{27,6},{18,7},{21,8},{28... | collective-permute-start | bytes 24584 | tf_op jit(solution)/shard_map/ppermute | solution.py:293
  5.5 1.0 %collective-permute-start.2 = (bf16[4,1024]{1,0:T(4,128)(2,1)}, bf16[4,1024]{1,0:T(4,128)(2,1)S(1)}, u32[]{:S(2)}, u32[]{:S(2)}) collective-permute-start(bf16[4,1024]{1,0:T(4,128)(2,1)} %tokens.1), channel_id=1, source_target_pairs={{5,0},{4,1},{7,2},{6,3},{1,4},{0,5},{3,6},{2,7},{13,8},{12,9},{15,... | collective-permute-start | bytes 24584 | tf_op jit(solution)/shard_map/ppermute | solution.py:293
  6.7 1.3 %plan.1 = (bf16[4,1024]{1,0:T(4,128)(2,1)S(1)}, bf16[8,20]{1,0:T(8,128)(2,1)S(1)}, bf16[8,20]{1,0:T(8,128)(2,1)S(1)}, s32[16,128]{1,0:T(8,128)S(1)}, s32[16,128]...) custom-call(s32[32]{0:T(128)S(1)} %copy-done.20, ...), custom_call_target="tpu_custom_call" | custom-call | tf_op jit(solution)/shard_map/plan/pallas_call | solution.py:261
  8.0 1.7 %collective-permute-done.refs_1_ = bf16[4,1024]{1,0:T(4,128)(2,1)S(1)} collective-permute-done((bf16[4,1024]{1,0:T(4,128)(2,1)}, bf16[4,1024]{1,0:T(4,128)(2,1)S(1)}, u32[]{:S(2)}, u32[]{:S(2)}) %collective-permute-start) | collective-permute-done | bytes 8224 | tf_op jit(solution)/shard_map/ppermute | solution.py:293
  9.8 0.9 %collective-permute-start.4 = (bf16[4,1024]{1,0:T(4,128)(2,1)S(1)}, bf16[4,1024]{1,0:T(4,128)(2,1)S(1)}, u32[]{:S(2)}, u32[]{:S(2)}) collective-permute-start(bf16[4,1024]{1,0:T(4,128)(2,1)S(1)} %sort_out.1.after.mine), channel_id=1, source_target_pairs={{0,1},{1,0},{2,3},{3,2},{4,5},{5,4},{6,7},{7,6},{8,9},{9,8},{10,11... | collective-permute-start | bytes 24584 | tf_op jit(solution)/shard_map/ppermute | solution.py:274
  11.6 1.2 %self_attention.1 = (bf16[4,1024]{1,0:T(4,128)(2,1)S(1)}, bf16[4,1024]{1,0:T(4,128)(2,1)S(1)}) custom-call(s32[16,128]{1,0:T(8,128)S(1)} %get-tuple-element.42.limits, bf16[4,1024]{1,0:T(4,128)(2,1)S(1)} %sort_out.1.after.mine, bf16[4,1024]{1,0:T(4,128)(2,1)S(1)} %collective-permute-done.4.more, bf16[3,1024,256]{2,1,0:T(8,128)(2,1)S(1)} %bitcast.13, ...), custom_call_target="tpu_custom_call" | custom-call | tf_op jit(solution)/shard_map/self_attention/pallas_call | solution.py:261
  12.8 1.5 %collective-permute-start.7 = (bf16[4,1024]{1,0:T(4,128)(2,1)S(1)}, bf16[4,1024]{1,0:T(4,128)(2,1)S(1)}, u32[]{:S(2)}, u32[]{:S(2)}) collective-permute-start(bf16[4,1024]{1,0:T(4,128)(2,1)S(1)} %get-tuple-element.54.p0), channel_id=1, source_target_pairs={{0,3},{1,2},{2,1},{3,0},{4,7},{5,6},{6,5},{7,4},{8,11},{9,10},{10,... | collective-permute-start | bytes 24584 | tf_op jit(solution)/shard_map/ppermute | solution.py:274
  14.8 0.8 %split_cross.1 = (bf16[4,256,256]{2,1,0:T(8,128)(2,1)S(1)}, bf16[4,256,256]{2,1,0:T(8,128)(2,1)S(1)}) custom-call(bf16[4,1024]{1,0:T(4,128)(2,1)S(1)} %get-tuple-element.58.after.x, bf16[4,1024,128]{2,1,0:T(8,128)(2,1)S(1)} %bitcast.14), custom_call_target="tpu_custom_call" | custom-call | tf_op jit(solution)/shard_map/split_cross/pallas_call | solution.py:261
  15.9 2.0 %collective-permute-done.6.p2 = bf16[4,1024]{1,0:T(4,128)(2,1)S(1)} collective-permute-done((bf16[4,1024]{1,0:T(4,128)(2,1)S(1)}, bf16[4,1024]{1,0:T(4,128)(2,1)S(1)}, u32[]{:S(2)}, u32[]{:S(2)}) %collective-permute-start.6) | collective-permute-done | bytes 8224 | tf_op jit(solution)/shard_map/ppermute | solution.py:274
  17.9 1.2 %cross_attention.1 = (bf16[4,1024]{1,0:T(4,128)(2,1)S(1)}, bf16[4,1024]{1,0:T(4,128)(2,1)S(1)}) custom-call(s32[16,128]{1,0:T(8,128)S(1)} %get-tuple-element.41.limits, bf16[4,1024]{1,0:T(4,128)(2,1)S(1)} %get-tuple-element.54.p0, bf16[4,1024]{1,0:T(4,128)(2,1)S(1)} %collective-permute-done.5.p1, bf16[4,1024]{1,0:T(4,128)(2,1)S(1)} %collective-permute-done.6.p2, ...), custom_call_target="tpu_custom_call" | custom-call | tf_op jit(solution)/shard_map/cross_attention/pallas_call | solution.py:261
  19.1 0.7 %collective-permute-start.9 = (bf16[4,1024]{1,0:T(4,128)(2,1)S(1)}, bf16[4,1024]{1,0:T(4,128)(2,1)S(1)}, u32[]{:S(2)}, u32[]{:S(2)}) collective-permute-start(bf16[4,1024]{1,0:T(4,128)(2,1)S(1)} %get-tuple-element.61.p0), channel_id=1, source_target_pairs={{0,2},{1,3},{2,0},{3,1},{4,6},{5,7},{6,4},{7,5},{8,10},{9,11},{10,... | collective-permute-start | bytes 24584 | tf_op jit(solution)/shard_map/ppermute | solution.py:274
  19.8 1.2 %collective-permute-start.8 = (bf16[4,1024]{1,0:T(4,128)(2,1)S(1)}, bf16[4,1024]{1,0:T(4,128)(2,1)S(1)}, u32[]{:S(2)}, u32[]{:S(2)}) collective-permute-start(bf16[4,1024]{1,0:T(4,128)(2,1)S(1)} %get-tuple-element.61.p0), channel_id=1, source_target_pairs={{0,1},{1,0},{2,3},{3,2},{4,5},{5,4},{6,7},{7,6},{8,9},{9,8},{10,11... | collective-permute-start | bytes 24584 | tf_op jit(solution)/shard_map/ppermute | solution.py:274
  21.0 1.2 %collective-permute-done.10.p3 = bf16[4,1024]{1,0:T(4,128)(2,1)S(1)} collective-permute-done((bf16[4,1024]{1,0:T(4,128)(2,1)S(1)}, bf16[4,1024]{1,0:T(4,128)(2,1)S(1)}, u32[]{:S(2)}, u32[]{:S(2)}) %collective-permute-start.10) | collective-permute-done | bytes 8224 | tf_op jit(solution)/shard_map/ppermute | solution.py:274
  22.8 0.8 %feed_forward.1 = (bf16[4,1024]{1,0:T(4,128)(2,1)S(1)}, bf16[4,1024]{1,0:T(4,128)(2,1)S(1)}) custom-call(bf16[4,1024]{1,0:T(4,128)(2,1)S(1)} %get-tuple-element.61.p0, bf16[4,1024]{1,0:T(4,128)(2,1)S(1)} %collective-permute-done.8.p1, bf16[4,1024]{1,0:T(4,128)(2,1)S(1)} %collective-permute-done.9.p2, bf16[4,1024]{1,0:T(4,128)(2,1)S(1)} %collective-permute-done.10.p3, ...), custom_call_target="tpu_custom_call" | custom-call | tf_op jit(solution)/shard_map/feed_forward/pallas_call | solution.py:261
  24.8 0.7 %collective-permute-start.11 = (bf16[4,1024]{1,0:T(4,128)(2,1)S(1)}, bf16[4,1024]{1,0:T(4,128)(2,1)S(1)}, u32[]{:S(2)}, u32[]{:S(2)}) collective-permute-start(bf16[4,1024]{1,0:T(4,128)(2,1)S(1)} %get-tuple-element.66.p0), channel_id=1, source_target_pairs={{0,1},{1,0},{2,3},{3,2},{4,5},{5,4},{6,7},{7,6},{8,9},{9,8},{10,11... | collective-permute-start | bytes 24584 | tf_op jit(solution)/shard_map/ppermute | solution.py:274
  25.5 1.2 %collective-permute-done.13.p3 = bf16[4,1024]{1,0:T(4,128)(2,1)S(1)} collective-permute-done((bf16[4,1024]{1,0:T(4,128)(2,1)S(1)}, bf16[4,1024]{1,0:T(4,128)(2,1)S(1)}, u32[]{:S(2)}, u32[]{:S(2)}) %collective-permute-start.13) | collective-permute-done | bytes 8224 | tf_op jit(solution)/shard_map/ppermute | solution.py:274
  26.8 1.1 %collective-permute-done.12.p2 = bf16[4,1024]{1,0:T(4,128)(2,1)S(1)} collective-permute-done((bf16[4,1024]{1,0:T(4,128)(2,1)S(1)}, bf16[4,1024]{1,0:T(4,128)(2,1)S(1)}, u32[]{:S(2)}, u32[]{:S(2)}) %collective-permute-start.12) | collective-permute-done | bytes 8224 | tf_op jit(solution)/shard_map/ppermute | solution.py:274
  28.1 1.8 %collective-permute-start.17 = (bf16[4,1024]{1,0:T(4,128)(2,1)S(1)}, bf16[4,1024]{1,0:T(4,128)(2,1)S(1)}, u32[]{:S(2)}, u32[]{:S(2)}) collective-permute-start(bf16[4,1024]{1,0:T(4,128)(2,1)S(1)} %last_norm.1.refs_0_), channel_id=1, source_target_pairs={{21,0},{28,1},{23,2},{30,3},{17,4},{24,5},{19,6},{26,7},{29,8},{20... | collective-permute-start | bytes 24584 | tf_op jit(solution)/shard_map/ppermute | solution.py:293
  29.9 1.8 %collective-permute-start.16 = (bf16[4,1024]{1,0:T(4,128)(2,1)S(1)}, bf16[4,1024]{1,0:T(4,128)(2,1)S(1)}, u32[]{:S(2)}, u32[]{:S(2)}) collective-permute-start(bf16[4,1024]{1,0:T(4,128)(2,1)S(1)} %last_norm.1.refs_0_), channel_id=1, source_target_pairs={{25,0},{16,1},{27,2},{18,3},{29,4},{20,5},{31,6},{22,7},{17,8},{24... | collective-permute-start | bytes 24584 | tf_op jit(solution)/shard_map/ppermute | solution.py:293
  31.6 0.8 %collective-permute-start.15 = (bf16[4,1024]{1,0:T(4,128)(2,1)S(1)}, bf16[4,1024]{1,0:T(4,128)(2,1)S(1)}, u32[]{:S(2)}, u32[]{:S(2)}) collective-permute-start(bf16[4,1024]{1,0:T(4,128)(2,1)S(1)} %last_norm.1.refs_0_), channel_id=1, source_target_pairs={{9,0},{12,1},{11,2},{14,3},{13,4},{8,5},{15,6},{10,7},{1,8},{4,9},... | collective-permute-start | bytes 24584 | tf_op jit(solution)/shard_map/ppermute | solution.py:293
  33.0 1.8 %collective-permute-done.16.refs_3_ = bf16[4,1024]{1,0:T(4,128)(2,1)S(1)} collective-permute-done((bf16[4,1024]{1,0:T(4,128)(2,1)S(1)}, bf16[4,1024]{1,0:T(4,128)(2,1)S(1)}, u32[]{:S(2)}, u32[]{:S(2)}) %collective-permute-start.16) | collective-permute-done | bytes 8224 | tf_op jit(solution)/shard_map/ppermute | solution.py:293
  34.8 0.8 %collective-permute-done.14.refs_1_ = bf16[4,1024]{1,0:T(4,128)(2,1)S(1)} collective-permute-done((bf16[4,1024]{1,0:T(4,128)(2,1)S(1)}, bf16[4,1024]{1,0:T(4,128)(2,1)S(1)}, u32[]{:S(2)}, u32[]{:S(2)}) %collective-permute-start.14) | collective-permute-done | bytes 8224 | tf_op jit(solution)/shard_map/ppermute | solution.py:293
  35.9 0.9 %collective-permute-done.18.more = bf16[4,1024]{1,0:T(4,128)(2,1)S(1)} collective-permute-done((bf16[4,1024]{1,0:T(4,128)(2,1)S(1)}, bf16[4,1024]{1,0:T(4,128)(2,1)S(1)}, u32[]{:S(2)}, u32[]{:S(2)}) %collective-permute-start.18) | collective-permute-done | bytes 8224 | tf_op jit(solution)/shard_map/ppermute | solution.py:274
  (73 shorter events, 5.5 us)
Async XLA Ops:
  0.0 6.5 %copy-start.14 = (bf16[1024]{0:T(1024)(128)(2,1)S(1)}, bf16[1024]{0:T(1024)(128)(2,1)}, u32[]{:S(2)}) copy-start(bf16[1024]{0:T(1024)(128)(2,1)} %refs_5_.1) | copy-start | bytes 6148
  0.0 6.5 %copy-start.13 = (bf16[1024]{0:T(1024)(128)(2,1)S(1)}, bf16[1024]{0:T(1024)(128)(2,1)}, u32[]{:S(2)}) copy-start(bf16[1024]{0:T(1024)(128)(2,1)} %refs_4_.1) | copy-start | bytes 6148
  0.0 6.5 %copy-start.12 = (bf16[1024]{0:T(1024)(128)(2,1)S(1)}, bf16[1024]{0:T(1024)(128)(2,1)}, u32[]{:S(2)}) copy-start(bf16[1024]{0:T(1024)(128)(2,1)} %refs_3_.1) | copy-start | bytes 6148
  0.1 7.9 %collective-permute-start.1 = (bf16[4,1024]{1,0:T(4,128)(2,1)}, bf16[4,1024]{1,0:T(4,128)(2,1)S(1)}, u32[]{:S(2)}, u32[]{:S(2)}) collective-permute-start(bf16[4,1024]{1,0:T(4,128)(2,1)} %tokens.1), channel_id=1, source_target_pairs={{25,0},{16,1},{27,2},{18,3},{29,4},{20,5},{31,6},{22,7},{17,8},{24... | collective-permute-start | bytes 24584 | tf_op jit(solution)/shard_map/ppermute | solution.py:293
  3.7 6.0 %collective-permute-start = (bf16[4,1024]{1,0:T(4,128)(2,1)}, bf16[4,1024]{1,0:T(4,128)(2,1)S(1)}, u32[]{:S(2)}, u32[]{:S(2)}) collective-permute-start(bf16[4,1024]{1,0:T(4,128)(2,1)} %tokens.1), channel_id=1, source_target_pairs={{29,0},{20,1},{31,2},{22,3},{25,4},{16,5},{27,6},{18,7},{21,8},{28... | collective-permute-start | bytes 24584 | tf_op jit(solution)/shard_map/ppermute | solution.py:293
  5.4 4.3 %collective-permute-start.3 = (bf16[4,1024]{1,0:T(4,128)(2,1)}, bf16[4,1024]{1,0:T(4,128)(2,1)S(1)}, u32[]{:S(2)}, u32[]{:S(2)}) collective-permute-start(bf16[4,1024]{1,0:T(4,128)(2,1)} %tokens.1), channel_id=1, source_target_pairs={{9,0},{12,1},{11,2},{14,3},{13,4},{8,5},{15,6},{10,7},{1,8},{4,9},... | collective-permute-start | bytes 24584 | tf_op jit(solution)/shard_map/ppermute | solution.py:293
  5.5 4.2 %collective-permute-start.2 = (bf16[4,1024]{1,0:T(4,128)(2,1)}, bf16[4,1024]{1,0:T(4,128)(2,1)S(1)}, u32[]{:S(2)}, u32[]{:S(2)}) collective-permute-start(bf16[4,1024]{1,0:T(4,128)(2,1)} %tokens.1), channel_id=1, source_target_pairs={{5,0},{4,1},{7,2},{6,3},{1,4},{0,5},{3,6},{2,7},{13,8},{12,9},{15,... | collective-permute-start | bytes 24584 | tf_op jit(solution)/shard_map/ppermute | solution.py:293
  9.8 1.7 %collective-permute-start.4 = (bf16[4,1024]{1,0:T(4,128)(2,1)S(1)}, bf16[4,1024]{1,0:T(4,128)(2,1)S(1)}, u32[]{:S(2)}, u32[]{:S(2)}) collective-permute-start(bf16[4,1024]{1,0:T(4,128)(2,1)S(1)} %sort_out.1.after.mine), channel_id=1, source_target_pairs={{0,1},{1,0},{2,3},{3,2},{4,5},{5,4},{6,7},{7,6},{8,9},{9,8},{10,11... | collective-permute-start | bytes 24584 | tf_op jit(solution)/shard_map/ppermute | solution.py:274
  11.6 11.2 %copy-start.2 = (bf16[1024,1024]{1,0:T(8,128)(2,1)S(1)}, bf16[1024,1024]{1,0:T(8,128)(2,1)}, u32[]{:S(2)}) copy-start(bf16[1024,1024]{1,0:T(8,128)(2,1)} %w_down.1) | copy-start | bytes 6291460
  12.8 10.1 %copy-start.1 = (bf16[1024,1024]{1,0:T(8,128)(2,1)S(1)}, bf16[1024,1024]{1,0:T(8,128)(2,1)}, u32[]{:S(2)}) copy-start(bf16[1024,1024]{1,0:T(8,128)(2,1)} %w_up.1) | copy-start | bytes 6291460
  12.8 3.1 %collective-permute-start.7 = (bf16[4,1024]{1,0:T(4,128)(2,1)S(1)}, bf16[4,1024]{1,0:T(4,128)(2,1)S(1)}, u32[]{:S(2)}, u32[]{:S(2)}) collective-permute-start(bf16[4,1024]{1,0:T(4,128)(2,1)S(1)} %get-tuple-element.54.p0), channel_id=1, source_target_pairs={{0,3},{1,2},{2,1},{3,0},{4,7},{5,6},{6,5},{7,4},{8,11},{9,10},{10,... | collective-permute-start | bytes 24584 | tf_op jit(solution)/shard_map/ppermute | solution.py:274
  14.2 3.7 %collective-permute-start.6 = (bf16[4,1024]{1,0:T(4,128)(2,1)S(1)}, bf16[4,1024]{1,0:T(4,128)(2,1)S(1)}, u32[]{:S(2)}, u32[]{:S(2)}) collective-permute-start(bf16[4,1024]{1,0:T(4,128)(2,1)S(1)} %get-tuple-element.54.p0), channel_id=1, source_target_pairs={{0,2},{1,3},{2,0},{3,1},{4,6},{5,7},{6,4},{7,5},{8,10},{9,11},{10,... | collective-permute-start | bytes 24584 | tf_op jit(solution)/shard_map/ppermute | solution.py:274
  14.8 3.1 %collective-permute-start.5 = (bf16[4,1024]{1,0:T(4,128)(2,1)S(1)}, bf16[4,1024]{1,0:T(4,128)(2,1)S(1)}, u32[]{:S(2)}, u32[]{:S(2)}) collective-permute-start(bf16[4,1024]{1,0:T(4,128)(2,1)S(1)} %get-tuple-element.54.p0), channel_id=1, source_target_pairs={{0,1},{1,0},{2,3},{3,2},{4,5},{5,4},{6,7},{7,6},{8,9},{9,8},{10,11... | collective-permute-start | bytes 24584 | tf_op jit(solution)/shard_map/ppermute | solution.py:274
  19.1 3.1 %collective-permute-start.10 = (bf16[4,1024]{1,0:T(4,128)(2,1)S(1)}, bf16[4,1024]{1,0:T(4,128)(2,1)S(1)}, u32[]{:S(2)}, u32[]{:S(2)}) collective-permute-start(bf16[4,1024]{1,0:T(4,128)(2,1)S(1)} %get-tuple-element.61.p0), channel_id=1, source_target_pairs={{0,3},{1,2},{2,1},{3,0},{4,7},{5,6},{6,5},{7,4},{8,11},{9,10},{10,... | collective-permute-start | bytes 24584 | tf_op jit(solution)/shard_map/ppermute | solution.py:274
  19.1 3.7 %collective-permute-start.9 = (bf16[4,1024]{1,0:T(4,128)(2,1)S(1)}, bf16[4,1024]{1,0:T(4,128)(2,1)S(1)}, u32[]{:S(2)}, u32[]{:S(2)}) collective-permute-start(bf16[4,1024]{1,0:T(4,128)(2,1)S(1)} %get-tuple-element.61.p0), channel_id=1, source_target_pairs={{0,2},{1,3},{2,0},{3,1},{4,6},{5,7},{6,4},{7,5},{8,10},{9,11},{10,... | collective-permute-start | bytes 24584 | tf_op jit(solution)/shard_map/ppermute | solution.py:274
  19.8 3.0 %collective-permute-start.8 = (bf16[4,1024]{1,0:T(4,128)(2,1)S(1)}, bf16[4,1024]{1,0:T(4,128)(2,1)S(1)}, u32[]{:S(2)}, u32[]{:S(2)}) collective-permute-start(bf16[4,1024]{1,0:T(4,128)(2,1)S(1)} %get-tuple-element.61.p0), channel_id=1, source_target_pairs={{0,1},{1,0},{2,3},{3,2},{4,5},{5,4},{6,7},{7,6},{8,9},{9,8},{10,11... | collective-permute-start | bytes 24584 | tf_op jit(solution)/shard_map/ppermute | solution.py:274
  23.7 3.1 %collective-permute-start.13 = (bf16[4,1024]{1,0:T(4,128)(2,1)S(1)}, bf16[4,1024]{1,0:T(4,128)(2,1)S(1)}, u32[]{:S(2)}, u32[]{:S(2)}) collective-permute-start(bf16[4,1024]{1,0:T(4,128)(2,1)S(1)} %get-tuple-element.66.p0), channel_id=1, source_target_pairs={{0,3},{1,2},{2,1},{3,0},{4,7},{5,6},{6,5},{7,4},{8,11},{9,10},{10,... | collective-permute-start | bytes 24584 | tf_op jit(solution)/shard_map/ppermute | solution.py:274
  24.2 3.7 %collective-permute-start.12 = (bf16[4,1024]{1,0:T(4,128)(2,1)S(1)}, bf16[4,1024]{1,0:T(4,128)(2,1)S(1)}, u32[]{:S(2)}, u32[]{:S(2)}) collective-permute-start(bf16[4,1024]{1,0:T(4,128)(2,1)S(1)} %get-tuple-element.66.p0), channel_id=1, source_target_pairs={{0,2},{1,3},{2,0},{3,1},{4,6},{5,7},{6,4},{7,5},{8,10},{9,11},{10,... | collective-permute-start | bytes 24584 | tf_op jit(solution)/shard_map/ppermute | solution.py:274
  24.8 3.1 %collective-permute-start.11 = (bf16[4,1024]{1,0:T(4,128)(2,1)S(1)}, bf16[4,1024]{1,0:T(4,128)(2,1)S(1)}, u32[]{:S(2)}, u32[]{:S(2)}) collective-permute-start(bf16[4,1024]{1,0:T(4,128)(2,1)S(1)} %get-tuple-element.66.p0), channel_id=1, source_target_pairs={{0,1},{1,0},{2,3},{3,2},{4,5},{5,4},{6,7},{7,6},{8,9},{9,8},{10,11... | collective-permute-start | bytes 24584 | tf_op jit(solution)/shard_map/ppermute | solution.py:274
  28.1 4.9 %collective-permute-start.17 = (bf16[4,1024]{1,0:T(4,128)(2,1)S(1)}, bf16[4,1024]{1,0:T(4,128)(2,1)S(1)}, u32[]{:S(2)}, u32[]{:S(2)}) collective-permute-start(bf16[4,1024]{1,0:T(4,128)(2,1)S(1)} %last_norm.1.refs_0_), channel_id=1, source_target_pairs={{21,0},{28,1},{23,2},{30,3},{17,4},{24,5},{19,6},{26,7},{29,8},{20... | collective-permute-start | bytes 24584 | tf_op jit(solution)/shard_map/ppermute | solution.py:293
  29.9 4.9 %collective-permute-start.16 = (bf16[4,1024]{1,0:T(4,128)(2,1)S(1)}, bf16[4,1024]{1,0:T(4,128)(2,1)S(1)}, u32[]{:S(2)}, u32[]{:S(2)}) collective-permute-start(bf16[4,1024]{1,0:T(4,128)(2,1)S(1)} %last_norm.1.refs_0_), channel_id=1, source_target_pairs={{25,0},{16,1},{27,2},{18,3},{29,4},{20,5},{31,6},{22,7},{17,8},{24... | collective-permute-start | bytes 24584 | tf_op jit(solution)/shard_map/ppermute | solution.py:293
  31.6 3.2 %collective-permute-start.15 = (bf16[4,1024]{1,0:T(4,128)(2,1)S(1)}, bf16[4,1024]{1,0:T(4,128)(2,1)S(1)}, u32[]{:S(2)}, u32[]{:S(2)}) collective-permute-start(bf16[4,1024]{1,0:T(4,128)(2,1)S(1)} %last_norm.1.refs_0_), channel_id=1, source_target_pairs={{9,0},{12,1},{11,2},{14,3},{13,4},{8,5},{15,6},{10,7},{1,8},{4,9},... | collective-permute-start | bytes 24584 | tf_op jit(solution)/shard_map/ppermute | solution.py:293
  32.5 3.1 %collective-permute-start.14 = (bf16[4,1024]{1,0:T(4,128)(2,1)S(1)}, bf16[4,1024]{1,0:T(4,128)(2,1)S(1)}, u32[]{:S(2)}, u32[]{:S(2)}) collective-permute-start(bf16[4,1024]{1,0:T(4,128)(2,1)S(1)} %last_norm.1.refs_0_), channel_id=1, source_target_pairs={{5,0},{4,1},{7,2},{6,3},{1,4},{0,5},{3,6},{2,7},{13,8},{12,9},{15,... | collective-permute-start | bytes 24584 | tf_op jit(solution)/shard_map/ppermute | solution.py:293
  35.7 1.2 %collective-permute-start.18 = (bf16[4,1024]{1,0:T(4,128)(2,1)S(1)}, bf16[4,1024]{1,0:T(4,128)(2,1)S(1)}, u32[]{:S(2)}, u32[]{:S(2)}) collective-permute-start(bf16[4,1024]{1,0:T(4,128)(2,1)S(1)} %sort_back.1.mine), channel_id=1, source_target_pairs={{0,1},{1,0},{2,3},{3,2},{4,5},{5,4},{6,7},{7,6},{8,9},{9,8},{10,11... | collective-permute-start | bytes 24584 | tf_op jit(solution)/shard_map/ppermute | solution.py:274
  (19 other events, 117.0 us)

commit v6 on v4

--- a/solution.py
+++ b/solution.py
@@ -12,7 +12,7 @@
 EPS = 1e-05
 MASKED = -1e30
 SPARE_FLOPS = 10**10
-OUT_STEPS = ((7, 5, 1), (6, 4, 1), (1, 1, 1), (2, 3, 1))
+OUT_STEPS = ((6, 4, 1), (7, 5, 1), (1, 1, 1), (2, 3, 1))
 BACK_STEPS = ((1, 1, 1), (2, 3, 1), (6, 4, 1), (5, 7, 1))
 TP_STEPS = (1, 2, 3)
 NORM_1, NORM_2, NORM_3, B_UP, B_CQ, B_QKV, TABLE_ROWS = 0, 3, 6, 9, 10, 11, 16

time: 37.6 us -> 37.6 us (level)
  transfers between devices with their start and end apart: 19 -> 19, of which waited for: 12 -> 11; matrix products, arithmetic and copies ran while one was open for 0% -> 0% of each run, Pallas kernels for 8% -> 8%
where the time goes in v6:
time: 37.6 us; the launch traced here: 37.5 us
  starting transfers between devices  18 us (48%)
  waiting for transfers between devices  11.9 us (32%)
  Pallas kernels  7.2 us (19%)
    ppermute x8, starting transfers between devices, gather_blocks(): got.append(lax.ppermute(value, ('req', 'tp'), pairs))  11.3 us
    ppermute x11, waiting for transfers between devices, swap(): return lax.ppermute(value, axis, [(i, i ^ mask) for i in range(size)])  7.6 us
    pallas_call x11, Pallas kernels, call(): pl.pallas_call(kernel, out_shape=outs, in_specs=specs, out_specs=[vmem] *...  7.2 us
    ppermute x11, starting transfers between devices, swap(): return lax.ppermute(value, axis, [(i, i ^ mask) for i in range(size)])  6.72 us
    ppermute x8, waiting for transfers between devices, gather_blocks(): got.append(lax.ppermute(value, ('req', 'tp'), pairs))  4.25 us
  transfers between devices with their start and end apart: 19, of which 11 were waited for; matrix products, arithmetic and copies ran while one was open for 0% of the time, Pallas kernels for 8%

profile of v6, /device:TPU:0, one launch (start us, length us, event | category | flops | bytes accessed | tf_op | source)
XLA Modules:
  0.0 37.5 jit_solution(7200956096544272449)
XLA Ops:
  0.1 4.5 %collective-permute-start.1 = (bf16[4,1024]{1,0:T(4,128)(2,1)}, bf16[4,1024]{1,0:T(4,128)(2,1)S(1)}, u32[]{:S(2)}, u32[]{:S(2)}) collective-permute-start(bf16[4,1024]{1,0:T(4,128)(2,1)} %tokens.1), channel_id=1, source_target_pairs={{29,0},{20,1},{31,2},{22,3},{25,4},{16,5},{27,6},{18,7},{21,8},{28... | collective-permute-start | bytes 24584 | tf_op jit(solution)/shard_map/ppermute | solution.py:274
  4.6 0.7 %collective-permute-start = (bf16[4,1024]{1,0:T(4,128)(2,1)}, bf16[4,1024]{1,0:T(4,128)(2,1)S(1)}, u32[]{:S(2)}, u32[]{:S(2)}) collective-permute-start(bf16[4,1024]{1,0:T(4,128)(2,1)} %tokens.1), channel_id=1, source_target_pairs={{25,0},{16,1},{27,2},{18,3},{29,4},{20,5},{31,6},{22,7},{17,8},{24... | collective-permute-start | bytes 24584 | tf_op jit(solution)/shard_map/ppermute | solution.py:274
  5.5 1.0 %collective-permute-start.2 = (bf16[4,1024]{1,0:T(4,128)(2,1)}, bf16[4,1024]{1,0:T(4,128)(2,1)S(1)}, u32[]{:S(2)}, u32[]{:S(2)}) collective-permute-start(bf16[4,1024]{1,0:T(4,128)(2,1)} %tokens.1), channel_id=1, source_target_pairs={{5,0},{4,1},{7,2},{6,3},{1,4},{0,5},{3,6},{2,7},{13,8},{12,9},{15,... | collective-permute-start | bytes 24584 | tf_op jit(solution)/shard_map/ppermute | solution.py:274
  6.7 1.4 %plan.1 = (bf16[4,1024]{1,0:T(4,128)(2,1)S(1)}, bf16[8,20]{1,0:T(8,128)(2,1)S(1)}, bf16[8,20]{1,0:T(8,128)(2,1)S(1)}, s32[16,128]{1,0:T(8,128)S(1)}, s32[16,128]...) custom-call(s32[32]{0:T(128)S(1)} %copy-done.20, ...), custom_call_target="tpu_custom_call" | custom-call | tf_op jit(solution)/shard_map/plan/pallas_call | solution.py:242
  8.1 1.6 %collective-permute-done.refs_1_ = bf16[4,1024]{1,0:T(4,128)(2,1)S(1)} collective-permute-done((bf16[4,1024]{1,0:T(4,128)(2,1)}, bf16[4,1024]{1,0:T(4,128)(2,1)S(1)}, u32[]{:S(2)}, u32[]{:S(2)}) %collective-permute-start) | collective-permute-done | bytes 8224 | tf_op jit(solution)/shard_map/ppermute | solution.py:274
  9.9 0.8 %collective-permute-start.4 = (bf16[4,1024]{1,0:T(4,128)(2,1)S(1)}, bf16[4,1024]{1,0:T(4,128)(2,1)S(1)}, u32[]{:S(2)}, u32[]{:S(2)}) collective-permute-start(bf16[4,1024]{1,0:T(4,128)(2,1)S(1)} %sort_out.1.after.mine), channel_id=1, source_target_pairs={{0,1},{1,0},{2,3},{3,2},{4,5},{5,4},{6,7},{7,6},{8,9},{9,8},{10,11... | collective-permute-start | bytes 24584 | tf_op jit(solution)/shard_map/ppermute | solution.py:255
  10.7 0.8 %split_self.1 = (bf16[2,256,512]{2,1,0:T(8,128)(2,1)S(1)}, bf16[2,512,256]{2,1,0:T(8,128)(2,1)S(1)}) custom-call(bf16[4,1024]{1,0:T(4,128)(2,1)S(1)} %sort_out.1.after.mine, bf16[4,2048,128]{2,1,0:T(8,128)(2,1)S(1)} %bitcast.12), custom_call_target="tpu_custom_call" | custom-call | tf_op jit(solution)/shard_map/split_self/pallas_call | solution.py:242
  11.6 1.2 %self_attention.1 = (bf16[4,1024]{1,0:T(4,128)(2,1)S(1)}, bf16[4,1024]{1,0:T(4,128)(2,1)S(1)}) custom-call(s32[16,128]{1,0:T(8,128)S(1)} %get-tuple-element.42.limits, bf16[4,1024]{1,0:T(4,128)(2,1)S(1)} %sort_out.1.after.mine, bf16[4,1024]{1,0:T(4,128)(2,1)S(1)} %collective-permute-done.4.more, bf16[3,1024,256]{2,1,0:T(8,128)(2,1)S(1)} %bitcast.13, ...), custom_call_target="tpu_custom_call" | custom-call | tf_op jit(solution)/shard_map/self_attention/pallas_call | solution.py:242
  12.7 1.5 %collective-permute-start.7 = (bf16[4,1024]{1,0:T(4,128)(2,1)S(1)}, bf16[4,1024]{1,0:T(4,128)(2,1)S(1)}, u32[]{:S(2)}, u32[]{:S(2)}) collective-permute-start(bf16[4,1024]{1,0:T(4,128)(2,1)S(1)} %get-tuple-element.54.p0), channel_id=1, source_target_pairs={{0,3},{1,2},{2,1},{3,0},{4,7},{5,6},{6,5},{7,4},{8,11},{9,10},{10,... | collective-permute-start | bytes 24584 | tf_op jit(solution)/shard_map/ppermute | solution.py:255
  14.8 0.8 %split_cross.1 = (bf16[4,256,256]{2,1,0:T(8,128)(2,1)S(1)}, bf16[4,256,256]{2,1,0:T(8,128)(2,1)S(1)}) custom-call(bf16[4,1024]{1,0:T(4,128)(2,1)S(1)} %get-tuple-element.58.after.x, bf16[4,1024,128]{2,1,0:T(8,128)(2,1)S(1)} %bitcast.14), custom_call_target="tpu_custom_call" | custom-call | tf_op jit(solution)/shard_map/split_cross/pallas_call | solution.py:242
  15.8 2.0 %collective-permute-done.6.p2 = bf16[4,1024]{1,0:T(4,128)(2,1)S(1)} collective-permute-done((bf16[4,1024]{1,0:T(4,128)(2,1)S(1)}, bf16[4,1024]{1,0:T(4,128)(2,1)S(1)}, u32[]{:S(2)}, u32[]{:S(2)}) %collective-permute-start.6) | collective-permute-done | bytes 8224 | tf_op jit(solution)/shard_map/ppermute | solution.py:255
  17.9 1.2 %cross_attention.1 = (bf16[4,1024]{1,0:T(4,128)(2,1)S(1)}, bf16[4,1024]{1,0:T(4,128)(2,1)S(1)}) custom-call(s32[16,128]{1,0:T(8,128)S(1)} %get-tuple-element.41.limits, bf16[4,1024]{1,0:T(4,128)(2,1)S(1)} %get-tuple-element.54.p0, bf16[4,1024]{1,0:T(4,128)(2,1)S(1)} %collective-permute-done.5.p1, bf16[4,1024]{1,0:T(4,128)(2,1)S(1)} %collective-permute-done.6.p2, ...), custom_call_target="tpu_custom_call" | custom-call | tf_op jit(solution)/shard_map/cross_attention/pallas_call | solution.py:242
  19.7 1.2 %collective-permute-start.8 = (bf16[4,1024]{1,0:T(4,128)(2,1)S(1)}, bf16[4,1024]{1,0:T(4,128)(2,1)S(1)}, u32[]{:S(2)}, u32[]{:S(2)}) collective-permute-start(bf16[4,1024]{1,0:T(4,128)(2,1)S(1)} %get-tuple-element.61.p0), channel_id=1, source_target_pairs={{0,1},{1,0},{2,3},{3,2},{4,5},{5,4},{6,7},{7,6},{8,9},{9,8},{10,11... | collective-permute-start | bytes 24584 | tf_op jit(solution)/shard_map/ppermute | solution.py:255
  21.0 1.2 %collective-permute-done.10.p3 = bf16[4,1024]{1,0:T(4,128)(2,1)S(1)} collective-permute-done((bf16[4,1024]{1,0:T(4,128)(2,1)S(1)}, bf16[4,1024]{1,0:T(4,128)(2,1)S(1)}, u32[]{:S(2)}, u32[]{:S(2)}) %collective-permute-start.10) | collective-permute-done | bytes 8224 | tf_op jit(solution)/shard_map/ppermute | solution.py:255
  22.8 0.8 %feed_forward.1 = (bf16[4,1024]{1,0:T(4,128)(2,1)S(1)}, bf16[4,1024]{1,0:T(4,128)(2,1)S(1)}) custom-call(bf16[4,1024]{1,0:T(4,128)(2,1)S(1)} %get-tuple-element.61.p0, bf16[4,1024]{1,0:T(4,128)(2,1)S(1)} %collective-permute-done.8.p1, bf16[4,1024]{1,0:T(4,128)(2,1)S(1)} %collective-permute-done.9.p2, bf16[4,1024]{1,0:T(4,128)(2,1)S(1)} %collective-permute-done.10.p3, ...), custom_call_target="tpu_custom_call" | custom-call | tf_op jit(solution)/shard_map/feed_forward/pallas_call | solution.py:242
  24.8 0.7 %collective-permute-start.11 = (bf16[4,1024]{1,0:T(4,128)(2,1)S(1)}, bf16[4,1024]{1,0:T(4,128)(2,1)S(1)}, u32[]{:S(2)}, u32[]{:S(2)}) collective-permute-start(bf16[4,1024]{1,0:T(4,128)(2,1)S(1)} %get-tuple-element.66.p0), channel_id=1, source_target_pairs={{0,1},{1,0},{2,3},{3,2},{4,5},{5,4},{6,7},{7,6},{8,9},{9,8},{10,11... | collective-permute-start | bytes 24584 | tf_op jit(solution)/shard_map/ppermute | solution.py:255
  25.5 1.2 %collective-permute-done.13.p3 = bf16[4,1024]{1,0:T(4,128)(2,1)S(1)} collective-permute-done((bf16[4,1024]{1,0:T(4,128)(2,1)S(1)}, bf16[4,1024]{1,0:T(4,128)(2,1)S(1)}, u32[]{:S(2)}, u32[]{:S(2)}) %collective-permute-start.13) | collective-permute-done | bytes 8224 | tf_op jit(solution)/shard_map/ppermute | solution.py:255
  26.7 1.1 %collective-permute-done.12.p2 = bf16[4,1024]{1,0:T(4,128)(2,1)S(1)} collective-permute-done((bf16[4,1024]{1,0:T(4,128)(2,1)S(1)}, bf16[4,1024]{1,0:T(4,128)(2,1)S(1)}, u32[]{:S(2)}, u32[]{:S(2)}) %collective-permute-start.12) | collective-permute-done | bytes 8224 | tf_op jit(solution)/shard_map/ppermute | solution.py:255
  28.1 1.8 %collective-permute-start.17 = (bf16[4,1024]{1,0:T(4,128)(2,1)S(1)}, bf16[4,1024]{1,0:T(4,128)(2,1)S(1)}, u32[]{:S(2)}, u32[]{:S(2)}) collective-permute-start(bf16[4,1024]{1,0:T(4,128)(2,1)S(1)} %last_norm.1.refs_0_), channel_id=1, source_target_pairs={{21,0},{28,1},{23,2},{30,3},{17,4},{24,5},{19,6},{26,7},{29,8},{20... | collective-permute-start | bytes 24584 | tf_op jit(solution)/shard_map/ppermute | solution.py:274
  29.9 0.9 %collective-permute-start.16 = (bf16[4,1024]{1,0:T(4,128)(2,1)S(1)}, bf16[4,1024]{1,0:T(4,128)(2,1)S(1)}, u32[]{:S(2)}, u32[]{:S(2)}) collective-permute-start(bf16[4,1024]{1,0:T(4,128)(2,1)S(1)} %last_norm.1.refs_0_), channel_id=1, source_target_pairs={{25,0},{16,1},{27,2},{18,3},{29,4},{20,5},{31,6},{22,7},{17,8},{24... | collective-permute-start | bytes 24584 | tf_op jit(solution)/shard_map/ppermute | solution.py:274
  30.8 1.7 %collective-permute-start.15 = (bf16[4,1024]{1,0:T(4,128)(2,1)S(1)}, bf16[4,1024]{1,0:T(4,128)(2,1)S(1)}, u32[]{:S(2)}, u32[]{:S(2)}) collective-permute-start(bf16[4,1024]{1,0:T(4,128)(2,1)S(1)} %last_norm.1.refs_0_), channel_id=1, source_target_pairs={{9,0},{12,1},{11,2},{14,3},{13,4},{8,5},{15,6},{10,7},{1,8},{4,9},... | collective-permute-start | bytes 24584 | tf_op jit(solution)/shard_map/ppermute | solution.py:274
  33.0 1.7 %collective-permute-done.16.refs_3_ = bf16[4,1024]{1,0:T(4,128)(2,1)S(1)} collective-permute-done((bf16[4,1024]{1,0:T(4,128)(2,1)S(1)}, bf16[4,1024]{1,0:T(4,128)(2,1)S(1)}, u32[]{:S(2)}, u32[]{:S(2)}) %collective-permute-start.16) | collective-permute-done | bytes 8224 | tf_op jit(solution)/shard_map/ppermute | solution.py:274
  34.7 0.8 %collective-permute-done.14.refs_1_ = bf16[4,1024]{1,0:T(4,128)(2,1)S(1)} collective-permute-done((bf16[4,1024]{1,0:T(4,128)(2,1)S(1)}, bf16[4,1024]{1,0:T(4,128)(2,1)S(1)}, u32[]{:S(2)}, u32[]{:S(2)}) %collective-permute-start.14) | collective-permute-done | bytes 8224 | tf_op jit(solution)/shard_map/ppermute | solution.py:274
  35.9 1.0 %collective-permute-done.18.more = bf16[4,1024]{1,0:T(4,128)(2,1)S(1)} collective-permute-done((bf16[4,1024]{1,0:T(4,128)(2,1)S(1)}, bf16[4,1024]{1,0:T(4,128)(2,1)S(1)}, u32[]{:S(2)}, u32[]{:S(2)}) %collective-permute-start.18) | collective-permute-done | bytes 8224 | tf_op jit(solution)/shard_map/ppermute | solution.py:255
  (73 shorter events, 5.4 us)
Async XLA Ops:
  0.0 6.6 %copy-start.14 = (bf16[1024]{0:T(1024)(128)(2,1)S(1)}, bf16[1024]{0:T(1024)(128)(2,1)}, u32[]{:S(2)}) copy-start(bf16[1024]{0:T(1024)(128)(2,1)} %refs_5_.1) | copy-start | bytes 6148
  0.0 6.6 %copy-start.13 = (bf16[1024]{0:T(1024)(128)(2,1)S(1)}, bf16[1024]{0:T(1024)(128)(2,1)}, u32[]{:S(2)}) copy-start(bf16[1024]{0:T(1024)(128)(2,1)} %refs_4_.1) | copy-start | bytes 6148
  0.0 6.6 %copy-start.12 = (bf16[1024]{0:T(1024)(128)(2,1)S(1)}, bf16[1024]{0:T(1024)(128)(2,1)}, u32[]{:S(2)}) copy-start(bf16[1024]{0:T(1024)(128)(2,1)} %refs_3_.1) | copy-start | bytes 6148
  0.1 8.0 %collective-permute-start.1 = (bf16[4,1024]{1,0:T(4,128)(2,1)}, bf16[4,1024]{1,0:T(4,128)(2,1)S(1)}, u32[]{:S(2)}, u32[]{:S(2)}) collective-permute-start(bf16[4,1024]{1,0:T(4,128)(2,1)} %tokens.1), channel_id=1, source_target_pairs={{29,0},{20,1},{31,2},{22,3},{25,4},{16,5},{27,6},{18,7},{21,8},{28... | collective-permute-start | bytes 24584 | tf_op jit(solution)/shard_map/ppermute | solution.py:274
  4.6 5.1 %collective-permute-start = (bf16[4,1024]{1,0:T(4,128)(2,1)}, bf16[4,1024]{1,0:T(4,128)(2,1)S(1)}, u32[]{:S(2)}, u32[]{:S(2)}) collective-permute-start(bf16[4,1024]{1,0:T(4,128)(2,1)} %tokens.1), channel_id=1, source_target_pairs={{25,0},{16,1},{27,2},{18,3},{29,4},{20,5},{31,6},{22,7},{17,8},{24... | collective-permute-start | bytes 24584 | tf_op jit(solution)/shard_map/ppermute | solution.py:274
  5.4 4.4 %collective-permute-start.3 = (bf16[4,1024]{1,0:T(4,128)(2,1)}, bf16[4,1024]{1,0:T(4,128)(2,1)S(1)}, u32[]{:S(2)}, u32[]{:S(2)}) collective-permute-start(bf16[4,1024]{1,0:T(4,128)(2,1)} %tokens.1), channel_id=1, source_target_pairs={{9,0},{12,1},{11,2},{14,3},{13,4},{8,5},{15,6},{10,7},{1,8},{4,9},... | collective-permute-start | bytes 24584 | tf_op jit(solution)/shard_map/ppermute | solution.py:274
  5.5 4.2 %collective-permute-start.2 = (bf16[4,1024]{1,0:T(4,128)(2,1)}, bf16[4,1024]{1,0:T(4,128)(2,1)S(1)}, u32[]{:S(2)}, u32[]{:S(2)}) collective-permute-start(bf16[4,1024]{1,0:T(4,128)(2,1)} %tokens.1), channel_id=1, source_target_pairs={{5,0},{4,1},{7,2},{6,3},{1,4},{0,5},{3,6},{2,7},{13,8},{12,9},{15,... | collective-permute-start | bytes 24584 | tf_op jit(solution)/shard_map/ppermute | solution.py:274
  9.9 1.6 %collective-permute-start.4 = (bf16[4,1024]{1,0:T(4,128)(2,1)S(1)}, bf16[4,1024]{1,0:T(4,128)(2,1)S(1)}, u32[]{:S(2)}, u32[]{:S(2)}) collective-permute-start(bf16[4,1024]{1,0:T(4,128)(2,1)S(1)} %sort_out.1.after.mine), channel_id=1, source_target_pairs={{0,1},{1,0},{2,3},{3,2},{4,5},{5,4},{6,7},{7,6},{8,9},{9,8},{10,11... | collective-permute-start | bytes 24584 | tf_op jit(solution)/shard_map/ppermute | solution.py:255
  11.5 11.2 %copy-start.2 = (bf16[1024,1024]{1,0:T(8,128)(2,1)S(1)}, bf16[1024,1024]{1,0:T(8,128)(2,1)}, u32[]{:S(2)}) copy-start(bf16[1024,1024]{1,0:T(8,128)(2,1)} %w_down.1) | copy-start | bytes 6291460
  12.7 10.1 %copy-start.1 = (bf16[1024,1024]{1,0:T(8,128)(2,1)S(1)}, bf16[1024,1024]{1,0:T(8,128)(2,1)}, u32[]{:S(2)}) copy-start(bf16[1024,1024]{1,0:T(8,128)(2,1)} %w_up.1) | copy-start | bytes 6291460
  12.7 3.1 %collective-permute-start.7 = (bf16[4,1024]{1,0:T(4,128)(2,1)S(1)}, bf16[4,1024]{1,0:T(4,128)(2,1)S(1)}, u32[]{:S(2)}, u32[]{:S(2)}) collective-permute-start(bf16[4,1024]{1,0:T(4,128)(2,1)S(1)} %get-tuple-element.54.p0), channel_id=1, source_target_pairs={{0,3},{1,2},{2,1},{3,0},{4,7},{5,6},{6,5},{7,4},{8,11},{9,10},{10,... | collective-permute-start | bytes 24584 | tf_op jit(solution)/shard_map/ppermute | solution.py:255
  14.2 3.7 %collective-permute-start.6 = (bf16[4,1024]{1,0:T(4,128)(2,1)S(1)}, bf16[4,1024]{1,0:T(4,128)(2,1)S(1)}, u32[]{:S(2)}, u32[]{:S(2)}) collective-permute-start(bf16[4,1024]{1,0:T(4,128)(2,1)S(1)} %get-tuple-element.54.p0), channel_id=1, source_target_pairs={{0,2},{1,3},{2,0},{3,1},{4,6},{5,7},{6,4},{7,5},{8,10},{9,11},{10,... | collective-permute-start | bytes 24584 | tf_op jit(solution)/shard_map/ppermute | solution.py:255
  14.8 3.1 %collective-permute-start.5 = (bf16[4,1024]{1,0:T(4,128)(2,1)S(1)}, bf16[4,1024]{1,0:T(4,128)(2,1)S(1)}, u32[]{:S(2)}, u32[]{:S(2)}) collective-permute-start(bf16[4,1024]{1,0:T(4,128)(2,1)S(1)} %get-tuple-element.54.p0), channel_id=1, source_target_pairs={{0,1},{1,0},{2,3},{3,2},{4,5},{5,4},{6,7},{7,6},{8,9},{9,8},{10,11... | collective-permute-start | bytes 24584 | tf_op jit(solution)/shard_map/ppermute | solution.py:255
  19.1 3.1 %collective-permute-start.10 = (bf16[4,1024]{1,0:T(4,128)(2,1)S(1)}, bf16[4,1024]{1,0:T(4,128)(2,1)S(1)}, u32[]{:S(2)}, u32[]{:S(2)}) collective-permute-start(bf16[4,1024]{1,0:T(4,128)(2,1)S(1)} %get-tuple-element.61.p0), channel_id=1, source_target_pairs={{0,3},{1,2},{2,1},{3,0},{4,7},{5,6},{6,5},{7,4},{8,11},{9,10},{10,... | collective-permute-start | bytes 24584 | tf_op jit(solution)/shard_map/ppermute | solution.py:255
  19.1 3.7 %collective-permute-start.9 = (bf16[4,1024]{1,0:T(4,128)(2,1)S(1)}, bf16[4,1024]{1,0:T(4,128)(2,1)S(1)}, u32[]{:S(2)}, u32[]{:S(2)}) collective-permute-start(bf16[4,1024]{1,0:T(4,128)(2,1)S(1)} %get-tuple-element.61.p0), channel_id=1, source_target_pairs={{0,2},{1,3},{2,0},{3,1},{4,6},{5,7},{6,4},{7,5},{8,10},{9,11},{10,... | collective-permute-start | bytes 24584 | tf_op jit(solution)/shard_map/ppermute | solution.py:255
  19.7 3.0 %collective-permute-start.8 = (bf16[4,1024]{1,0:T(4,128)(2,1)S(1)}, bf16[4,1024]{1,0:T(4,128)(2,1)S(1)}, u32[]{:S(2)}, u32[]{:S(2)}) collective-permute-start(bf16[4,1024]{1,0:T(4,128)(2,1)S(1)} %get-tuple-element.61.p0), channel_id=1, source_target_pairs={{0,1},{1,0},{2,3},{3,2},{4,5},{5,4},{6,7},{7,6},{8,9},{9,8},{10,11... | collective-permute-start | bytes 24584 | tf_op jit(solution)/shard_map/ppermute | solution.py:255
  23.6 3.1 %collective-permute-start.13 = (bf16[4,1024]{1,0:T(4,128)(2,1)S(1)}, bf16[4,1024]{1,0:T(4,128)(2,1)S(1)}, u32[]{:S(2)}, u32[]{:S(2)}) collective-permute-start(bf16[4,1024]{1,0:T(4,128)(2,1)S(1)} %get-tuple-element.66.p0), channel_id=1, source_target_pairs={{0,3},{1,2},{2,1},{3,0},{4,7},{5,6},{6,5},{7,4},{8,11},{9,10},{10,... | collective-permute-start | bytes 24584 | tf_op jit(solution)/shard_map/ppermute | solution.py:255
  24.2 3.7 %collective-permute-start.12 = (bf16[4,1024]{1,0:T(4,128)(2,1)S(1)}, bf16[4,1024]{1,0:T(4,128)(2,1)S(1)}, u32[]{:S(2)}, u32[]{:S(2)}) collective-permute-start(bf16[4,1024]{1,0:T(4,128)(2,1)S(1)} %get-tuple-element.66.p0), channel_id=1, source_target_pairs={{0,2},{1,3},{2,0},{3,1},{4,6},{5,7},{6,4},{7,5},{8,10},{9,11},{10,... | collective-permute-start | bytes 24584 | tf_op jit(solution)/shard_map/ppermute | solution.py:255
  24.8 3.1 %collective-permute-start.11 = (bf16[4,1024]{1,0:T(4,128)(2,1)S(1)}, bf16[4,1024]{1,0:T(4,128)(2,1)S(1)}, u32[]{:S(2)}, u32[]{:S(2)}) collective-permute-start(bf16[4,1024]{1,0:T(4,128)(2,1)S(1)} %get-tuple-element.66.p0), channel_id=1, source_target_pairs={{0,1},{1,0},{2,3},{3,2},{4,5},{5,4},{6,7},{7,6},{8,9},{9,8},{10,11... | collective-permute-start | bytes 24584 | tf_op jit(solution)/shard_map/ppermute | solution.py:255
  28.1 4.9 %collective-permute-start.17 = (bf16[4,1024]{1,0:T(4,128)(2,1)S(1)}, bf16[4,1024]{1,0:T(4,128)(2,1)S(1)}, u32[]{:S(2)}, u32[]{:S(2)}) collective-permute-start(bf16[4,1024]{1,0:T(4,128)(2,1)S(1)} %last_norm.1.refs_0_), channel_id=1, source_target_pairs={{21,0},{28,1},{23,2},{30,3},{17,4},{24,5},{19,6},{26,7},{29,8},{20... | collective-permute-start | bytes 24584 | tf_op jit(solution)/shard_map/ppermute | solution.py:274
  29.9 4.9 %collective-permute-start.16 = (bf16[4,1024]{1,0:T(4,128)(2,1)S(1)}, bf16[4,1024]{1,0:T(4,128)(2,1)S(1)}, u32[]{:S(2)}, u32[]{:S(2)}) collective-permute-start(bf16[4,1024]{1,0:T(4,128)(2,1)S(1)} %last_norm.1.refs_0_), channel_id=1, source_target_pairs={{25,0},{16,1},{27,2},{18,3},{29,4},{20,5},{31,6},{22,7},{17,8},{24... | collective-permute-start | bytes 24584 | tf_op jit(solution)/shard_map/ppermute | solution.py:274
  30.8 3.9 %collective-permute-start.15 = (bf16[4,1024]{1,0:T(4,128)(2,1)S(1)}, bf16[4,1024]{1,0:T(4,128)(2,1)S(1)}, u32[]{:S(2)}, u32[]{:S(2)}) collective-permute-start(bf16[4,1024]{1,0:T(4,128)(2,1)S(1)} %last_norm.1.refs_0_), channel_id=1, source_target_pairs={{9,0},{12,1},{11,2},{14,3},{13,4},{8,5},{15,6},{10,7},{1,8},{4,9},... | collective-permute-start | bytes 24584 | tf_op jit(solution)/shard_map/ppermute | solution.py:274
  32.5 3.1 %collective-permute-start.14 = (bf16[4,1024]{1,0:T(4,128)(2,1)S(1)}, bf16[4,1024]{1,0:T(4,128)(2,1)S(1)}, u32[]{:S(2)}, u32[]{:S(2)}) collective-permute-start(bf16[4,1024]{1,0:T(4,128)(2,1)S(1)} %last_norm.1.refs_0_), channel_id=1, source_target_pairs={{5,0},{4,1},{7,2},{6,3},{1,4},{0,5},{3,6},{2,7},{13,8},{12,9},{15,... | collective-permute-start | bytes 24584 | tf_op jit(solution)/shard_map/ppermute | solution.py:274
  35.7 1.2 %collective-permute-start.18 = (bf16[4,1024]{1,0:T(4,128)(2,1)S(1)}, bf16[4,1024]{1,0:T(4,128)(2,1)S(1)}, u32[]{:S(2)}, u32[]{:S(2)}) collective-permute-start(bf16[4,1024]{1,0:T(4,128)(2,1)S(1)} %sort_back.1.mine), channel_id=1, source_target_pairs={{0,1},{1,0},{2,3},{3,2},{4,5},{5,4},{6,7},{7,6},{8,9},{9,8},{10,11... | collective-permute-start | bytes 24584 | tf_op jit(solution)/shard_map/ppermute | solution.py:255
  (19 other events, 117.6 us)
